TPU v7x, 32 devices: a whole 2x2x4 slice. The times are simulated.
32 devices in a mesh: expert: 8 (over y, x, core), hidden: 4 (over z).
Axes of the slice: x: 2, y: 2, z: 4, core: 2. Of those that a mesh axis runs over, the one named last changes fastest.
Arguments:
- tokens: bfloat16 [32768, 512], P(('expert', 'hidden')), may hold values from -6 to 6
- cotangent: bfloat16 [32768, 512], P(('expert', 'hidden')), may hold values from -6 to 6
- w_qkv: bfloat16 [512, 1536], replicated, may hold values from -0.25 to 0.25
- bias_qv: float32 [2, 512], replicated, may hold values from -1.5 to 1.5
- w_out: bfloat16 [512, 512], replicated, may hold values from -0.75 to 0.75
- out_bias: float32 [512], replicated, may hold values from -1.5 to 1.5
- norm_gains: float32 [2, 512], replicated, may hold values from 0.25 to 1.75
- norm_shifts: float32 [2, 512], replicated, may hold values from -1.5 to 1.5
- gate_table: float32 [30, 2], replicated, may hold values from -3 to 3
- w_in: bfloat16 [8, 512, 2048], P('expert', None, 'hidden'), may hold values from -0.25 to 0.25
- w_down: bfloat16 [8, 2048, 512], P('expert', 'hidden'), may hold values from -0.125 to 0.125
- lengths: int32 [32, 32], P(('expert', 'hidden')), may hold values from 1 to 64, 1024 in all within a row
- seg_task: int32 [32, 32], P(('expert', 'hidden')), may hold values from 0 to 29
- routes: int32 [30, 2], replicated, may hold values from 0 to 7, all different within a row
Outputs:
- layer_out: bfloat16 [32768, 512], P(('expert', 'hidden'))
- input_grad: bfloat16 [32768, 512], P(('expert', 'hidden'))
- grad_qkv: float32 [512, 1536], replicated
- grad_bias_qv: float32 [2, 512], replicated
- grad_out: float32 [512, 512], replicated
- grad_out_bias: float32 [512], replicated
- grad_gains: float32 [2, 512], replicated
- grad_shifts: float32 [2, 512], replicated
- grad_gate: float32 [30, 2], replicated
- grad_w_in: float32 [8, 512, 2048], P('expert', None, 'hidden')
- grad_w_down: float32 [8, 2048, 512], P('expert', 'hidden')
Inputs may be any that keep to these rules, and one draw needn't show every extreme that they name: Each pack's 32 sentence lengths sum to 1024; every pack has one sentence of exactly 64 tokens. `routes`: each task names 2 different experts; every expert is named by some task.
All inputs are finite; a program needn't handle non-finite values.
Results may differ from a plain program's by a relative error of at most 0.017.
Values may be sent and summed in bfloat16 or wider, within the bound.
No kernel may reach another device: no remote copies, remote signals or barrier semaphores. Data moves between devices by JAX's collectives and lax.ppermute only.
A program may use at most 384 MiB of HBM per device.

v0:
```python
import jax
import jax.numpy as jnp
from jax import lax
from jax.sharding import PartitionSpec as P

HEADS = 8
HD = 64


NORM_EPS = 1e-05
MASK_FILL = -1000000000.0


def norm_rows(values, gain, shift):
    center = jnp.mean(values, axis=-1, keepdims=True)
    centred = values - center
    spread = jnp.mean(centred * centred, axis=-1, keepdims=True)
    return centred * lax.rsqrt(spread + NORM_EPS) * gain + shift


def soft_gelu(values):
    return jax.nn.gelu(values, approximate=True)


def expert_back(inputs, grad_slots, weight_in, weight_down):
    pre_act = jnp.einsum("red,edf->ref", inputs, weight_in, preferred_element_type=jnp.float32)
    active, gelu_back = jax.vjp(soft_gelu, pre_act)
    active_low = active.astype(jnp.bfloat16)
    grad_active = jnp.einsum(
        "red,efd->ref", grad_slots, weight_down, preferred_element_type=jnp.float32
    )
    grad_pre = gelu_back(grad_active)[0].astype(jnp.bfloat16)
    grad_down = jnp.einsum(
        "ref,red->efd", active_low, grad_slots, preferred_element_type=jnp.float32
    )
    grad_in = jnp.einsum("red,ref->edf", inputs, grad_pre, preferred_element_type=jnp.float32)
    return (grad_pre, grad_in, grad_down)


def shards(
    tokens,
    cotangent,
    w_qkv,
    bias_qv,
    w_out,
    out_bias,
    norm_gains,
    norm_shifts,
    gate_table,
    w_in,
    w_down,
    lengths,
    seg_task,
    routes,
):
    packs_here, seg_count = lengths.shape
    tok_count, width_model = tokens.shape
    pack_len = tok_count // packs_here
    local_experts = w_in.shape[0]
    groups = lax.axis_size("expert")
    experts_all = local_experts * groups
    top_count = routes.shape[1]
    task_total = gate_table.shape[0]
    capacity = 3 * top_count * tok_count // (2 * experts_all)
    rows_here = groups * capacity
    score_scale = HD ** (-0.5)
    places = jnp.arange(pack_len, dtype=jnp.int32)
    bounds = jnp.cumsum(lengths, axis=1, dtype=jnp.int32)
    segment = jnp.sum(
        (places[None, :, None] >= bounds[:, None, :]).astype(jnp.int32), axis=2, dtype=jnp.int32
    )
    seg_match = segment[:, :, None] == jnp.arange(seg_count, dtype=jnp.int32)[None, None, :]
    task_tok = jnp.sum(
        jnp.where(seg_match, seg_task[:, None, :], 0), axis=2, dtype=jnp.int32
    ).reshape(-1)
    task_onehot = task_tok[:, None] == jnp.arange(task_total, dtype=jnp.int32)[None, :]
    chosen = jnp.sum(
        jnp.where(task_onehot[:, :, None], routes[None, :, :], 0), axis=1, dtype=jnp.int32
    )
    task_float = task_onehot.astype(jnp.float32)
    logits = jnp.dot(task_float, gate_table, precision=lax.Precision.HIGHEST)
    gate_probs = jax.nn.softmax(logits, axis=-1)
    flat_route = chosen.reshape(-1)
    route_hits = (flat_route[:, None] == jnp.arange(experts_all, dtype=jnp.int32)[None, :]).astype(
        jnp.int32
    )
    before = jnp.cumsum(route_hits, axis=0, dtype=jnp.int32) - route_hits
    position = jnp.sum(before * route_hits, axis=1, dtype=jnp.int32)
    slot_index = jnp.where(
        position < capacity, flat_route * capacity + position, experts_all * capacity
    )
    token_float = tokens.astype(jnp.float32)
    normed_one = norm_rows(token_float, norm_gains[0], norm_shifts[0]).astype(jnp.bfloat16)
    qkv = jnp.dot(normed_one, w_qkv, preferred_element_type=jnp.float32)
    queries = (qkv[:, :width_model] + bias_qv[0]).astype(jnp.bfloat16)
    keyset = qkv[:, width_model : 2 * width_model].astype(jnp.bfloat16)
    values = (qkv[:, 2 * width_model :] + bias_qv[1]).astype(jnp.bfloat16)

    def by_pack(array):
        return array.reshape(packs_here, pack_len, HEADS, HD)

    def scores_of(query_pack, key_pack, seg_pack):
        raw_scores = (
            jnp.einsum("qhc,khc->hqk", query_pack, key_pack, preferred_element_type=jnp.float32)
            * score_scale
        )
        same_seg = seg_pack[:, None] == seg_pack[None, :]
        return jnp.where(same_seg[None], raw_scores, MASK_FILL)

    def forward_pack(packed):
        query_pack, key_pack, value_pack, seg_pack = packed
        scores = scores_of(query_pack, key_pack, seg_pack)
        row_peak = jnp.max(scores, axis=-1, keepdims=True)
        exp_total = jnp.sum(jnp.exp(scores - row_peak), axis=-1, keepdims=True)
        log_total = row_peak + jnp.log(exp_total)
        soft_probs = jnp.exp(scores - log_total).astype(jnp.bfloat16)
        attended = jnp.einsum(
            "hqk,khc->qhc", soft_probs, value_pack, preferred_element_type=jnp.float32
        )
        return (attended.astype(jnp.bfloat16), log_total)

    attended, log_totals = lax.map(
        forward_pack, (by_pack(queries), by_pack(keyset), by_pack(values), segment)
    )
    attended_flat = attended.reshape(tok_count, width_model)
    hidden_state = (
        token_float + jnp.dot(attended_flat, w_out, preferred_element_type=jnp.float32) + out_bias
    )
    normed_two, norm_back_two = jax.vjp(norm_rows, hidden_state, norm_gains[1], norm_shifts[1])
    normed_low = normed_two.astype(jnp.bfloat16)
    spread_rows = jnp.repeat(normed_low, top_count, axis=0)
    outgoing = (
        jnp.zeros((experts_all * capacity + 1, width_model), jnp.bfloat16)
        .at[slot_index]
        .set(spread_rows)
    )
    outgoing = outgoing[:-1].reshape(experts_all, capacity, width_model)
    arrived = lax.all_to_all(outgoing, "expert", split_axis=0, concat_axis=0, tiled=True)

    def to_rows(expert_block):
        return (
            expert_block.reshape(groups, local_experts, capacity, width_model)
            .transpose(0, 2, 1, 3)
            .reshape(rows_here, local_experts, width_model)
        )

    def from_rows(row_block):
        return (
            row_block.reshape(groups, capacity, local_experts, width_model)
            .transpose(0, 2, 1, 3)
            .reshape(experts_all, capacity, width_model)
        )

    expert_in = to_rows(arrived)
    pre_piece = jnp.einsum(
        "red,edf->ref",
        lax.all_gather(expert_in, "hidden", axis=0, tiled=True),
        w_in,
        preferred_element_type=jnp.float32,
    )
    active = soft_gelu(pre_piece).astype(jnp.bfloat16)
    row_piece = active
    expert_out = lax.psum_scatter(
        jnp.einsum("ref,efd->red", row_piece, w_down, preferred_element_type=jnp.float32).astype(
            jnp.bfloat16
        ),
        "hidden",
        scatter_dimension=0,
        tiled=True,
    )
    returned = lax.all_to_all(
        from_rows(expert_out), "expert", split_axis=0, concat_axis=0, tiled=True
    )
    padded_back = jnp.concatenate(
        [returned.reshape(-1, width_model), jnp.zeros((1, width_model), jnp.bfloat16)], axis=0
    )
    picked = padded_back[slot_index].reshape(tok_count, top_count, width_model).astype(jnp.float32)
    layer_out = (hidden_state + jnp.sum(gate_probs[:, :, None] * picked, axis=1)).astype(
        jnp.bfloat16
    )
    grad_final = cotangent.astype(jnp.float32)
    gate_grad = jnp.sum(grad_final[:, None, :] * picked, axis=2)
    slot_grad = (
        (gate_probs[:, :, None] * grad_final[:, None, :])
        .astype(jnp.bfloat16)
        .reshape(-1, width_model)
    )
    grad_outgoing = (
        jnp.zeros((experts_all * capacity + 1, width_model), jnp.bfloat16)
        .at[slot_index]
        .set(slot_grad)
    )
    grad_outgoing = grad_outgoing[:-1].reshape(experts_all, capacity, width_model)
    grad_arrived = lax.all_to_all(grad_outgoing, "expert", split_axis=0, concat_axis=0, tiled=True)
    grad_rows = to_rows(grad_arrived)
    gathered_in, grad_gathered = (
        lax.all_gather(expert_in, "hidden", axis=0, tiled=True),
        lax.all_gather(grad_rows, "hidden", axis=0, tiled=True),
    )
    grad_pre, grad_w_in, grad_w_down = expert_back(gathered_in, grad_gathered, w_in, w_down)
    row_piece = grad_pre
    slot_input_grad = lax.psum_scatter(
        jnp.einsum("ref,edf->red", row_piece, w_in, preferred_element_type=jnp.float32).astype(
            jnp.bfloat16
        ),
        "hidden",
        scatter_dimension=0,
        tiled=True,
    )
    grad_back = lax.all_to_all(
        from_rows(slot_input_grad), "expert", split_axis=0, concat_axis=0, tiled=True
    )
    grad_padded = jnp.concatenate(
        [grad_back.reshape(-1, width_model), jnp.zeros((1, width_model), jnp.bfloat16)], axis=0
    )
    grad_picked = (
        grad_padded[slot_index].reshape(tok_count, top_count, width_model).astype(jnp.float32)
    )
    grad_normed_two = jnp.sum(grad_picked, axis=1)
    grad_hidden_part, grad_gain_two, grad_shift_two = norm_back_two(grad_normed_two)
    grad_hidden = grad_final + grad_hidden_part
    gate_inner = jnp.sum(gate_probs * gate_grad, axis=-1, keepdims=True)
    grad_logits = gate_probs * (gate_grad - gate_inner)
    grad_table = jnp.einsum("tk,tr->kr", task_float, grad_logits, precision=lax.Precision.HIGHEST)
    grad_attn = grad_hidden.astype(jnp.bfloat16)
    grad_out_bias = jnp.sum(grad_hidden, axis=0)
    grad_w_out = jnp.einsum(
        "td,te->de", attended_flat, grad_attn, preferred_element_type=jnp.float32
    )
    grad_attended = jnp.einsum(
        "te,de->td", grad_attn, w_out, preferred_element_type=jnp.float32
    ).astype(jnp.bfloat16)

    def backward_pack(packed):
        query_pack, key_pack, value_pack, seg_pack, log_total, grad_pack = packed
        scores = scores_of(query_pack, key_pack, seg_pack)
        soft_probs = jnp.exp(scores - log_total)
        grad_probs = jnp.einsum(
            "qhc,khc->hqk", grad_pack, value_pack, preferred_element_type=jnp.float32
        )
        grad_values = jnp.einsum(
            "hqk,qhc->khc",
            soft_probs.astype(jnp.bfloat16),
            grad_pack,
            preferred_element_type=jnp.float32,
        )
        inner_sum = jnp.sum(soft_probs * grad_probs, axis=-1, keepdims=True)
        grad_scores = (soft_probs * (grad_probs - inner_sum)).astype(jnp.bfloat16)
        grad_queries = (
            jnp.einsum("hqk,khc->qhc", grad_scores, key_pack, preferred_element_type=jnp.float32)
            * score_scale
        )
        grad_keys = (
            jnp.einsum("hqk,qhc->khc", grad_scores, query_pack, preferred_element_type=jnp.float32)
            * score_scale
        )
        return (
            grad_queries.astype(jnp.bfloat16),
            grad_keys.astype(jnp.bfloat16),
            grad_values.astype(jnp.bfloat16),
        )

    grad_queries, grad_keys, grad_values = lax.map(
        backward_pack,
        (
            by_pack(queries),
            by_pack(keyset),
            by_pack(values),
            segment,
            log_totals,
            by_pack(grad_attended),
        ),
    )
    grad_queries = grad_queries.reshape(tok_count, width_model)
    grad_keys = grad_keys.reshape(tok_count, width_model)
    grad_values = grad_values.reshape(tok_count, width_model)
    grad_joined = jnp.concatenate([grad_queries, grad_keys, grad_values], axis=1)
    grad_qkv = jnp.einsum("td,te->de", normed_one, grad_joined, preferred_element_type=jnp.float32)
    grad_bias_qv = jnp.stack(
        [
            jnp.sum(grad_queries.astype(jnp.float32), axis=0),
            jnp.sum(grad_values.astype(jnp.float32), axis=0),
        ]
    )
    grad_normed_one = jnp.einsum(
        "te,de->td", grad_joined, w_qkv, preferred_element_type=jnp.float32
    )
    primal_one, norm_back_one = jax.vjp(norm_rows, token_float, norm_gains[0], norm_shifts[0])
    grad_token_part, grad_gain_one, grad_shift_one = norm_back_one(grad_normed_one)
    input_grad = (grad_hidden + grad_token_part).astype(jnp.bfloat16)
    grad_gains = jnp.stack([grad_gain_one, grad_gain_two])
    grad_shifts = jnp.stack([grad_shift_one, grad_shift_two])
    summed = lax.psum(
        (grad_qkv, grad_bias_qv, grad_w_out, grad_out_bias, grad_gains, grad_shifts, grad_table),
        ("expert", "hidden"),
    )
    return (
        layer_out,
        input_grad,
        summed[0],
        summed[1],
        summed[2],
        summed[3],
        summed[4],
        summed[5],
        summed[6],
        grad_w_in,
        grad_w_down,
    )


def solution(mesh):
    return jax.shard_map(
        shards,
        mesh=mesh,
        in_specs=(
            P(("expert", "hidden"), None),
            P(("expert", "hidden"), None),
            P(),
            P(),
            P(),
            P(),
            P(),
            P(),
            P(),
            P("expert", None, "hidden"),
            P("expert", "hidden", None),
            P(("expert", "hidden"), None),
            P(("expert", "hidden"), None),
            P(),
        ),
        out_specs=(
            P(("expert", "hidden"), None),
            P(("expert", "hidden"), None),
            P(),
            P(),
            P(),
            P(),
            P(),
            P(),
            P(),
            P("expert", None, "hidden"),
            P("expert", "hidden", None),
        ),
        check_vma=False,
    )
```

profile of v0, /device:TPU:0, one launch (start us, length us, event | category | flops | bytes accessed | tf_op | source)
XLA Modules:
  0.0 1390.3 jit_solution(11438155259370410206)
XLA Ops:
  22.5 3.3 fusion.97
  35.7 14.9 %fusion = (f32[8,1024]{1,0:T(8,128)S(1)}, f32[8,1024,1024]{1,2,0:T(8,128)}) fusion(pred[1024,1024]{0,1:T(8,128)(4,1)S(1)} %broadcast_compare_fusion, bf16[1024,8,64]{0,2,1:T(8,128)(2,1)} %bitcast.178, bf16[1024,8,64]{0,2,1:T(8,128)(2,1)} %bitcast.176), kind=kOutput, calls=%fused_computation.11 | convolution fusion | flops 1098899456 | bytes 36732928 | tf_op jit(solution)/shard_map/while/body/eval_jaxpr/qhc,khc->hqk/dot_general | solution.py:104
  50.6 14.3 %exponential_reduce_fusion = f32[8,1024]{1,0:T(8,128)S(1)} fusion(f32[8,1024,1024]{1,2,0:T(8,128)} %get-tuple-element.131, f32[8,1024]{1,0:T(8,128)S(1)} %get-tuple-element.130, pred[1024,1024]{0,1:T(8,128)(4,1)S(1)} %broadcast_compare_fusion), kind=kLoop, calls=%fused_computation.9 | loop fusion | flops 33546240 | bytes 34668544 | tf_op jit(solution)/shard_map/while/body/eval_jaxpr/reduce_sum | solution.py:114
  65.0 16.2 %convolution_convert_fusion.4 = bf16[8,64,1024]{2,1,0:T(8,128)(2,1)} fusion(bf16[1024,8,64]{0,2,1:T(8,128)(2,1)S(1)} %bitcast.187, f32[8,1024,1024]{1,2,0:T(8,128)} %get-tuple-element.131, f32[8,1024]{1,0:T(8,128)S(1)} %log_add_fusion, pred[1024,1024]{0,1:T(8,128)(4,1)S(1)} %broadcast_compare_fusion), kind=kOutput, calls=%fused_computation.88 | convolution fusion | flops 1107820544 | bytes 36732928 | tf_op jit(solution)/shard_map/while/body/eval_jaxpr/hqk,khc->qhc/dot_general | solution.py:117
  87.8 2.4 broadcast_in_dim.142
  90.2 4.1 reshape.462
  94.4 12.0 scatter_custom_fusion
  108.3 43.0 %all_to_all.20 = bf16[8,384,512]{2,1,0:T(8,128)(2,1)} all-to-all(bf16[8,384,512]{2,1,0:T(8,128)(2,1)S(1)} %bitcast.181), channel_id=1, replica_groups=mesh['expert'=8,'hidden'=4] {'expert'}, dimensions={0} | all-to-all | bytes 6291456 | tf_op jit(solution)/shard_map/all_to_all | solution.py:138
  158.0 5.3 mul.269
  163.3 6.3 mul.270
  169.7 13.0 scatter_custom_fusion.1
  184.6 41.2 %all_to_all.21 = bf16[8,384,512]{2,1,0:T(8,128)(2,1)} all-to-all(bf16[8,384,512]{2,1,0:T(8,128)(2,1)S(1)} %bitcast.180), channel_id=1, replica_groups=mesh['expert'=8,'hidden'=4] {'expert'}, dimensions={0} | all-to-all | bytes 6291456 | tf_op jit(solution)/shard_map/all_to_all | solution.py:194
  225.8 143.3 %all-gather.3.cloned.1.call-done = bf16[12288,1,512]{2,0,1:T(8,128)(2,1)} async-done(((bf16[3072,1,512]{2,0,1:T(8,128)(2,1)}), bf16[12288,1,512]{2,0,1:T(8,128)(2,1)}) %all-gather.3.cloned.1.call-update) | async-done | bytes 12582928 | tf_op jit(solution)/shard_map/all_gather | solution.py:157
  369.1 18.3 %fusion.25 = f32[12288,512]{1,0:T(8,128)} fusion(bf16[12288,1,512]{2,0,1:T(8,128)(2,1)} %all-gather.3.cloned.1.call-done, bf16[1,512,512]{2,1,0:T(8,128)(2,1)S(1)} %copy-done.22), kind=kOutput, calls=%fused_computation.41 | convolution fusion | flops 6442450944 | bytes 38273024 | tf_op jit(solution)/shard_map/red,edf->ref/dot_general | solution.py:155
  387.4 16.6 %fusion.13 = bf16[12288,1,512]{2,0,1:T(8,128)(2,1)} fusion(f32[12288,512]{1,0:T(8,128)} %fusion.25, bf16[1,512,512]{2,1,0:T(8,128)(2,1)S(1)} %copy-done.53), kind=kOutput, calls=%fused_computation.29 | convolution fusion | flops 6505365504 | bytes 38273024 | tf_op jit(solution)/shard_map/ref,efd->red/dot_general | solution.py:164
  404.1 183.0 %all-gather.5.cloned.1.call-done = bf16[12288,1,512]{2,0,1:T(8,128)(2,1)} async-done(((bf16[3072,1,512]{2,0,1:T(8,128)(2,1)}), bf16[12288,1,512]{2,0,1:T(8,128)(2,1)}) %all-gather.5.cloned.1.call-update) | async-done | bytes 12582928 | tf_op jit(solution)/shard_map/all_gather | solution.py:198
  587.1 29.2 %fusion.7 = bf16[12288,1,512]{2,0,1:T(8,128)(2,1)} fusion(f32[12288,512]{1,0:T(8,128)} %fusion.25, bf16[12288,1,512]{2,0,1:T(8,128)(2,1)} %all-gather.5.cloned.1.call-done, bf16[1,512,512]{2,1,0:T(8,128)(2,1)S(1)} %copy-done.53), kind=kOutput, calls=%fused_computation.18 | convolution fusion | flops 6568280064 | bytes 50855936 | tf_op jit(solution)/shard_map/red,efd->ref/dot_general | solution.py:29
  616.2 14.2 %fusion.14 = bf16[12288,1,512]{2,0,1:T(8,128)(2,1)} fusion(bf16[12288,1,512]{2,0,1:T(8,128)(2,1)} %fusion.7, bf16[1,512,512]{2,1,0:T(8,128)(2,1)S(1)} %copy-done.22), kind=kOutput, calls=%fused_computation.30 | convolution fusion | flops 6448742400 | bytes 25690112 | tf_op jit(solution)/shard_map/ref,edf->red/dot_general | solution.py:203
  630.4 169.1 %reduce-scatter.3.cloned.1.call-done = bf16[3072,1,512]{2,0,1:T(8,128)(2,1)} async-done(((bf16[12288,1,512]{2,0,1:T(8,128)(2,1)}), bf16[3072,1,512]{2,0,1:T(8,128)(2,1)}) %reduce-scatter.3.cloned.1.call-update) | async-done | bytes 3145744 | tf_op jit(solution)/shard_map/reduce_scatter | solution.py:163
  799.5 4.5 all-to-all-start.1
  804.0 210.6 %reduce-scatter.5.cloned.1.call-done = bf16[3072,1,512]{2,0,1:T(8,128)(2,1)} async-done(((bf16[12288,1,512]{2,0,1:T(8,128)(2,1)}), bf16[3072,1,512]{2,0,1:T(8,128)(2,1)}) %reduce-scatter.5.cloned.1.call-update) | async-done | bytes 3145744 | tf_op jit(solution)/shard_map/reduce_scatter | solution.py:202
  1014.7 4.5 all-to-all-start.3
  1019.2 18.6 %fusion.48 = f32[1,512,512]{2,1,0:T(8,128)} fusion(bf16[12288,1,512]{2,0,1:T(8,128)(2,1)} %all-gather.5.cloned.1.call-done, f32[12288,512]{1,0:T(8,128)} %fusion.25), kind=kOutput, calls=%fused_computation.89 | convolution fusion | flops 6499074048 | bytes 38797312 | tf_op jit(solution)/shard_map/ref,red->efd/dot_general | solution.py:33
  1037.7 14.1 %fusion.53 = f32[1,512,512]{2,1,0:T(8,128)} fusion(bf16[12288,1,512]{2,0,1:T(8,128)(2,1)} %fusion.7, bf16[12288,1,512]{2,0,1:T(8,128)(2,1)} %all-gather.3.cloned.1.call-done), kind=kOutput, calls=%fused_computation.90 | convolution fusion | flops 6442450944 | bytes 26214400 | tf_op jit(solution)/shard_map/red,ref->edf/dot_general | solution.py:36
  1051.8 3.7 concatenate.9
  1057.0 3.7 concatenate.10
  1060.7 11.5 gather_fusion
  1072.2 11.5 gather_fusion.1
  1083.8 5.6 reshape.441
  1089.4 8.5 reduce_sum.290
  1097.9 2.9 copy.101
  1100.8 2.7 multiply_reduce_fusion.4
  1105.2 5.5 reshape.440
  1110.7 11.2 multiply_reduce_fusion.1
  1121.9 3.2 copy.97
  1125.1 4.9 fusion.99
  1133.5 16.0 %convert_reduce_fusion.1 = (f32[8,64]{1,0:T(8,128)S(1)}, bf16[8,64,1024]{2,1,0:T(8,128)(2,1)}) fusion(bf16[1024,8,64]{0,2,1:T(8,128)(2,1)} %bitcast.184, f32[8,1024,1024]{1,2,0:T(8,128)} %get-tuple-element.131, f32[8,1024]{1,0:T(8,128)S(1)} %copy-done.18, pred[1024,1024]{0,1:T(8,128)(4,1)S(1)} %copy-done.4), kind=kOutput, calls=%fused_computation.71 | convolution fusion | flops 1108868608 | bytes 36734976 | tf_op jit(solution)/shard_map/while/body/eval_jaxpr/hqk,qhc->khc/dot_general | solution.py:241
  1149.5 23.8 %multiply_reduce_fusion = (f32[8,1024]{1,0:T(8,128)S(1)}, f32[8,1024,1024]{1,2,0:T(8,128)}) fusion(f32[8,1024,1024]{1,2,0:T(8,128)} %get-tuple-element.131, f32[8,1024]{1,0:T(8,128)S(1)} %copy-done.18, pred[1024,1024]{0,1:T(8,128)(4,1)S(1)} %copy-done.4, bf16[1024,8,64]{0,2,1:T(8,128)(2,1)} %bitcast.185, bf16[1024,8,64]{0,2,1:T(8,128)(2,1)} %bitcast.186), kind=kOutput, calls=%fused_computation.7 | convolution fusion | flops 1115676672 | bytes 70320128 | tf_op jit(solution)/shard_map/while/body/eval_jaxpr/qhc,khc->hqk/dot_general | solution.py:238
  1173.3 28.7 %multiply_convert_fusion = bf16[8,1024,1024]{1,2,0:T(8,128)(2,1)} fusion(f32[8,1024,1024]{1,2,0:T(8,128)} %get-tuple-element.137, f32[8,1024,1024]{1,2,0:T(8,128)} %get-tuple-element.131, f32[8,1024]{1,0:T(8,128)S(1)} %get-tuple-element.136, f32[8,1024]{1,0:T(8,128)S(1)} %copy-done.18, pred[1024,1024]{0,1:T(8,128)(4,1)S(1)} %copy-done.4), kind=kLoop, calls=%fused_computation.6 | loop fusion | flops 50331648 | bytes 85000192 | tf_op jit(solution)/shard_map/while/body/eval_jaxpr/convert_element_type | solution.py:248
  1201.9 12.3 multiply_convert_fusion.3
  1214.3 9.0 convert_reduce_fusion.2
  1223.4 3.2 fusion.105
  1226.6 3.6 fusion.58
  1232.9 3.2 copy.105
  1238.3 2.5 fusion.37
  1247.0 41.2 %all-reduce.2 = (f32[2,512]{1,0:T(2,128)}, f32[512]{0:T(512)}, f32[2,512]{1,0:T(2,128)}, f32[2,512]{1,0:T(2,128)}, f32[30,2]{0,1:T(2,128)}) all-reduce(f32[2,512]{1,0:T(2,128)S(1)} %get-tuple-element.144, f32[512]{0:T(512)S(1)} %get-tuple-element.119, ...), channel_id=1, replica_groups=mesh['expert'=8,'hidden'=4] {'expert','hidden'}, use_global_device_ids=true, to_apply=%region_29.30 | all-reduce | flops 3644 | bytes 29152 | tf_op jit(solution)/shard_map/psum | solution.py:293
  1288.2 90.3 %all-reduce.6.cloned.1.call-done = (f32[512,1536]{1,0:T(8,128)}, f32[512,512]{1,0:T(8,128)}) async-done(((f32[512,1536]{1,0:T(8,128)}, f32[512,512]{1,0:T(8,128)}), (f32[512,1536]{1,0:T(8,128)}, f32[512,512]{1,0:T(8,128)})) %all-reduce.6.cloned.1.call-update) | async-done | bytes 4194320 | tf_op jit(solution)/shard_map/psum | solution.py:293
  1378.5 3.8 copy.120
  (198 shorter events, 60.8 us)
Async XLA Ops:
  7.2 15.3 %copy-start = (bf16[512,1536]{1,0:T(8,128)(2,1)S(1)}, bf16[512,1536]{1,0:T(8,128)(2,1)}, u32[]{:S(2)}) copy-start(bf16[512,1536]{1,0:T(8,128)(2,1)} %param.16) | copy-start | bytes 4718596
  7.2 361.9 %all-gather.3.cloned.1.call-start = ((), (), s32[]{:S(2)}) async-start(), calls=%async_computation.6 | async-start | bytes 15728640 | tf_op jit(solution)/shard_map/all_gather | solution.py:157
  9.8 141.6 %copy-start.49 = (s32[1024]{0:T(1024)}, s32[1024]{0:T(1024)S(1)}, u32[]{:S(2)}) copy-start(s32[1024]{0:T(1024)S(1)} %select_reduce_fusion.1) | copy-start | bytes 12292
  11.5 53.4 %copy-start.3 = (pred[1024,1024]{0,1:T(8,128)(4,1)}, pred[1024,1024]{0,1:T(8,128)(4,1)S(1)}, u32[]{:S(2)}) copy-start(pred[1024,1024]{0,1:T(8,128)(4,1)S(1)} %broadcast_compare_fusion) | copy-start | bytes 3145732
  13.1 12.7 copy-start.47
  13.1 71.3 %copy-start.33 = (f32[1,512]{1,0:T(1,128)}, f32[1,512]{1,0:T(1,128)S(1)}, u32[]{:S(2)}) copy-start(f32[1,512]{1,0:T(1,128)S(1)} %get-tuple-element.124) | copy-start | bytes 6148
  13.9 11.9 copy-start.51
  21.0 4.9 copy-start.27
  22.5 3.3 copy-start.35
  22.5 3.3 copy-start.43
  50.6 14.3 %copy-start.16 = (bf16[1024,512]{0,1:T(8,128)(2,1)S(1)}, bf16[1024,512]{0,1:T(8,128)(2,1)}, u32[]{:S(2)}) copy-start(bf16[1024,512]{0,1:T(8,128)(2,1)} %copy.87) | copy-start | bytes 3145732
  64.9 16.2 %copy-start.17 = (f32[8,1024]{1,0:T(8,128)}, f32[8,1024]{1,0:T(8,128)S(1)}, u32[]{:S(2)}) copy-start(f32[8,1024]{1,0:T(8,128)S(1)} %log_add_fusion) | copy-start | bytes 98308
  65.0 16.2 %copy-start.5 = (bf16[1024,512]{0,1:T(8,128)(2,1)S(1)}, bf16[1024,512]{0,1:T(8,128)(2,1)}, u32[]{:S(2)}) copy-start(bf16[1024,512]{0,1:T(8,128)(2,1)} %copy.86) | copy-start | bytes 3145732
  65.0 16.2 %copy-start.23 = (bf16[512,512]{1,0:T(8,128)(2,1)S(1)}, bf16[512,512]{1,0:T(8,128)(2,1)}, u32[]{:S(2)}) copy-start(bf16[512,512]{1,0:T(8,128)(2,1)} %param.18) | copy-start | bytes 1572868
  65.0 16.2 %copy-start.54 = (f32[512]{0:T(512)S(1)}, f32[512]{0:T(512)}, u32[]{:S(2)}) copy-start(f32[512]{0:T(512)} %param.19) | copy-start | bytes 6148
  108.3 43.1 %copy-start.55 = (f32[30,2]{0,1:T(2,128)S(1)}, f32[30,2]{0,1:T(2,128)}, u32[]{:S(2)}) copy-start(f32[30,2]{0,1:T(2,128)} %param.22) | copy-start | bytes 724
  151.4 435.7 %all-gather.5.cloned.1.call-start = ((), (), s32[]{:S(2)}) async-start(), calls=%async_computation.8 | async-start | bytes 15728640 | tf_op jit(solution)/shard_map/all_gather | solution.py:198
  156.4 7.0 copy-start.12
  184.6 184.5 %copy-start.22 = (bf16[1,512,512]{2,1,0:T(8,128)(2,1)S(1)}, bf16[1,512,512]{2,1,0:T(8,128)(2,1)}, u32[]{:S(2)}) copy-start(bf16[1,512,512]{2,1,0:T(8,128)(2,1)} %param.23) | copy-start | bytes 1572868
  225.8 161.7 %copy-start.53 = (bf16[1,512,512]{2,1,0:T(8,128)(2,1)S(1)}, bf16[1,512,512]{2,1,0:T(8,128)(2,1)}, u32[]{:S(2)}) copy-start(bf16[1,512,512]{2,1,0:T(8,128)(2,1)} %param.24) | copy-start | bytes 1572868
  225.8 573.8 %reduce-scatter.3.cloned.1.call-start = ((), (), s32[]{:S(2)}) async-start(), calls=%async_computation.7 | async-start | bytes 15728640 | tf_op jit(solution)/shard_map/reduce_scatter | solution.py:163
  404.0 610.6 %reduce-scatter.5.cloned.1.call-start = ((), (), s32[]{:S(2)}) async-start(), calls=%async_computation.9 | async-start | bytes 15728640 | tf_op jit(solution)/shard_map/reduce_scatter | solution.py:202
  799.5 215.1 %all-to-all-start.1 = ((bf16[8,384,512]{2,1,0:T(8,128)(2,1)}), bf16[8,384,512]{2,1,0:T(8,128)(2,1)}, u32[]{:S(2)}, u32[]{:S(2)}) async-start(bf16[8,384,512]{2,1,0:T(8,128)(2,1)} %bitcast.189), calls=%async_computation.2 | async-start | bytes 6291456 | tf_op jit(solution)/shard_map/all_to_all | solution.py:171
  1014.7 42.3 %all-to-all-start.3 = ((bf16[8,384,512]{2,1,0:T(8,128)(2,1)}), bf16[8,384,512]{2,1,0:T(8,128)(2,1)}, u32[]{:S(2)}, u32[]{:S(2)}) async-start(bf16[8,384,512]{2,1,0:T(8,128)(2,1)} %bitcast.188), calls=%async_computation.5 | async-start | bytes 6291456 | tf_op jit(solution)/shard_map/all_to_all | solution.py:210
  1019.1 359.4 %all-reduce.6.cloned.1.call-start = ((), (), s32[]{:S(2)}) async-start(), calls=%async_computation.10 | async-start | bytes 8388608 | tf_op jit(solution)/shard_map/psum | solution.py:293
  1097.9 5.7 copy-start.38
  1100.8 3.5 copy-start.9
  1100.8 3.5 copy-start.32
  1105.2 5.6 copy-start.15
  1125.1 4.9 copy-start.21
  1130.0 3.5 copy-start.7
  1130.0 3.4 copy-start.4
  1130.0 3.4 copy-start.18
  1201.9 12.4 copy-start.11
  1214.3 9.0 copy-start.19
  1214.3 9.0 copy-start.56
  1223.3 3.3 copy-start.6
  1223.3 3.3 copy-start.28
  1223.3 3.3 copy-start.44
  1223.3 3.3 copy-start.48
  1236.1 4.6 copy-start.8
  1236.1 4.6 copy-start.10
  1242.5 4.3 copy-start.30
  1242.5 4.3 copy-start.40
  1242.5 4.3 copy-start.42
  1242.5 4.3 copy-start.46
  1242.5 4.3 copy-start.50
  1378.5 3.8 copy-start.20
  (18 other events, 30.1 us)
Sparse Core Ops, SparseCore 0:
  151.5 217.5 all-gather.2
  370.7 216.3 all-gather.4
  589.4 210.0 reduce-scatter.2
  801.7 212.8 reduce-scatter.4
  1236.2 142.2 all-reduce.5
where the time goes:
time: 1400 us; the launch traced here: 1390 us
  waiting for transfers between devices  798 us (57%)
  matrix products  219 us (16%)
  blocking collectives  125 us (9%)
  local copies, waits for them, and re-layouts  120 us (9%)
  other arithmetic  104 us (7%)
  between operations  15.1 us (1%)
    reduce_scatter x1, waiting for transfers between devices, shards(): lax.psum_scatter(jnp.einsum('ref,edf->red', row_piece, w_in, preferred_el...  211 us
    all_gather x1, waiting for transfers between devices, shards(): lax.all_gather(grad_rows, 'hidden', axis=0, tiled=True)  183 us
    reduce_scatter x1, waiting for transfers between devices, shards(): lax.psum_scatter(jnp.einsum('ref,efd->red', row_piece, w_down, preferred_...  169 us
    all_gather x1, waiting for transfers between devices, shards(): lax.all_gather(expert_in, 'hidden', axis=0, tiled=True)  143 us
    psum x1, waiting for transfers between devices, shards(): lax.psum((grad_qkv, grad_bias_qv, grad_w_out, grad_out_bias, grad_gains,...  90.3 us
    all_to_all x1, blocking collectives, shards(): lax.all_to_all(outgoing, 'expert', split_axis=0, concat_axis=0, tiled=True)  43 us
    psum x1, blocking collectives, shards(): lax.psum((grad_qkv, grad_bias_qv, grad_w_out, grad_out_bias, grad_gains,...  41.2 us
    all_to_all x1, blocking collectives, shards(): lax.all_to_all(grad_outgoing, 'expert', split_axis=0, concat_axis=0, tile...  41.2 us
  transfers between devices with their start and end apart: 7, of which 6 were waited for; matrix products, arithmetic and copies ran while one was open for 11% of the time, Pallas kernels for 0%

commit v1 on v0

--- a/solution.py
+++ b/solution.py
@@ -64,6 +64,11 @@
     capacity = 3 * top_count * tok_count // (2 * experts_all)
     rows_here = groups * capacity
     score_scale = HD ** (-0.5)
+    planes = lax.axis_size("hidden")
+    down_shape = w_down.shape
+    in_shape = w_in.shape
+    w_in = lax.all_gather(w_in, "hidden", axis=2, tiled=True)
+    w_down = lax.all_gather(w_down, "hidden", axis=1, tiled=True)
     places = jnp.arange(pack_len, dtype=jnp.int32)
     bounds = jnp.cumsum(lengths, axis=1, dtype=jnp.int32)
     segment = jnp.sum(
@@ -154,20 +159,15 @@
     expert_in = to_rows(arrived)
     pre_piece = jnp.einsum(
         "red,edf->ref",
-        lax.all_gather(expert_in, "hidden", axis=0, tiled=True),
+        expert_in,
         w_in,
         preferred_element_type=jnp.float32,
     )
     active = soft_gelu(pre_piece).astype(jnp.bfloat16)
     row_piece = active
-    expert_out = lax.psum_scatter(
-        jnp.einsum("ref,efd->red", row_piece, w_down, preferred_element_type=jnp.float32).astype(
-            jnp.bfloat16
-        ),
-        "hidden",
-        scatter_dimension=0,
-        tiled=True,
-    )
+    expert_out = jnp.einsum(
+        "ref,efd->red", row_piece, w_down, preferred_element_type=jnp.float32
+    ).astype(jnp.bfloat16)
     returned = lax.all_to_all(
         from_rows(expert_out), "expert", split_axis=0, concat_axis=0, tiled=True
     )
@@ -193,20 +193,24 @@
     grad_outgoing = grad_outgoing[:-1].reshape(experts_all, capacity, width_model)
     grad_arrived = lax.all_to_all(grad_outgoing, "expert", split_axis=0, concat_axis=0, tiled=True)
     grad_rows = to_rows(grad_arrived)
-    gathered_in, grad_gathered = (
-        lax.all_gather(expert_in, "hidden", axis=0, tiled=True),
-        lax.all_gather(grad_rows, "hidden", axis=0, tiled=True),
-    )
-    grad_pre, grad_w_in, grad_w_down = expert_back(gathered_in, grad_gathered, w_in, w_down)
+    grad_pre, grad_w_in, grad_w_down = expert_back(expert_in, grad_rows, w_in, w_down)
+
+    def over_planes(pieces):
+        moved = lax.all_to_all(
+            pieces.astype(jnp.bfloat16), "hidden", split_axis=0, concat_axis=0, tiled=True
+        )
+        return jnp.sum(moved.astype(jnp.float32), axis=0)
+
+    grad_w_in = over_planes(
+        grad_w_in.reshape(in_shape[:2] + (planes, in_shape[2])).transpose(2, 0, 1, 3)
+    )
+    grad_w_down = over_planes(
+        grad_w_down.reshape((down_shape[0], planes) + down_shape[1:]).transpose(1, 0, 2, 3)
+    )
     row_piece = grad_pre
-    slot_input_grad = lax.psum_scatter(
-        jnp.einsum("ref,edf->red", row_piece, w_in, preferred_element_type=jnp.float32).astype(
-            jnp.bfloat16
-        ),
-        "hidden",
-        scatter_dimension=0,
-        tiled=True,
-    )
+    slot_input_grad = jnp.einsum(
+        "ref,edf->red", row_piece, w_in, preferred_element_type=jnp.float32
+    ).astype(jnp.bfloat16)
     grad_back = lax.all_to_all(
         from_rows(slot_input_grad), "expert", split_axis=0, concat_axis=0, tiled=True
     )

time: 1400 us -> 683 us (0.49)
  waiting for transfers between devices: 798 us -> 105 us
  blocking collectives: 125 us -> 60.9 us
  local copies, waits for them, and re-layouts: 120 us -> 142 us
  starting transfers between devices: 9.15 us -> 30.3 us
    reduce_scatter x2 -> x0, waiting for transfers between devices: 380 us -> none  [the longest x1 211 us: shards(): lax.psum_scatter(jnp.einsum('ref,edf->red', row_piece, w_in, preferred_el...]
    all_gather x2, waiting for transfers between devices: 326 us -> 0.01 us  [the longest x1 0.01 us: shards(): w_in = lax.all_gather(w_in, 'hidden', axis=2, tiled=True)]
    all_to_all x2 -> x0, blocking collectives: 84.2 us -> none  [the longest x1 43 us: shards(): lax.all_to_all(outgoing, 'expert', split_axis=0, concat_axis=0, tiled=True)]
    all_to_all x0 -> x4, starting transfers between devices: none -> 20.5 us  [the longest x2 10.6 us: over_planes(): lax.all_to_all(pieces.astype(jnp.bfloat16), 'hidden', split_axis=0, conca...]
    psum x1, blocking collectives: 41.2 us -> 60.9 us  [shards(): lax.psum((grad_qkv, grad_bias_qv, grad_w_out, grad_out_bias, grad_gains,...]
  transfers between devices with their start and end apart: 7 -> 9, of which waited for: 6 -> 3; matrix products, arithmetic and copies ran while one was open for 11% -> 67% of each run, Pallas kernels for 0% -> 0%
where the time goes in v1:
time: 683 us; the launch traced here: 674 us
  matrix products  209 us (31%)
  local copies, waits for them, and re-layouts  142 us (21%)
  other arithmetic  112 us (16%)
  waiting for transfers between devices  105 us (15%)
  blocking collectives  60.9 us (9%)
  starting transfers between devices  30.3 us (4%)
  between operations  14.9 us (2%)
    psum x1, waiting for transfers between devices, shards(): lax.psum((grad_qkv, grad_bias_qv, grad_w_out, grad_out_bias, grad_gains,...  89.5 us
    psum x1, blocking collectives, shards(): lax.psum((grad_qkv, grad_bias_qv, grad_w_out, grad_out_bias, grad_gains,...  60.9 us
    convert_element_type x1, other arithmetic, backward_pack(): grad_scores = (soft_probs * (grad_probs - inner_sum)).astype(jnp.bfloat16)  28.4 us
    dot_general x1, matrix products, expert_back(): jnp.einsum('red,efd->ref', grad_slots, weight_down, preferred_element_typ...  27.1 us
    dot_general x1, matrix products, backward_pack(): jnp.einsum('qhc,khc->hqk', grad_pack, value_pack, preferred_element_type=...  23.9 us
    dot_general x1, matrix products, shards(): jnp.einsum('red,edf->ref', expert_in, w_in, preferred_element_type=jnp.fl...  21 us
    unnamed x127, local copies, waits for them, and re-layouts  20.2 us
    dot_general x1, matrix products, forward_pack(): jnp.einsum('hqk,khc->qhc', soft_probs, value_pack, preferred_element_type...  16.1 us
  transfers between devices with their start and end apart: 9, of which 3 were waited for; matrix products, arithmetic and copies ran while one was open for 67% of the time, Pallas kernels for 0%

profile of v1, /device:TPU:0, one launch (start us, length us, event | category | flops | bytes accessed | tf_op | source)
XLA Modules:
  0.0 673.6 jit_solution(12515564280658761508)
XLA Ops:
  19.9 3.3 fusion.75
  33.1 15.1 %fusion = (f32[8,1024]{1,0:T(8,128)S(1)}, f32[8,1024,1024]{1,2,0:T(8,128)}) fusion(pred[1024,1024]{0,1:T(8,128)(4,1)S(1)} %broadcast_compare_fusion, bf16[1024,8,64]{0,2,1:T(8,128)(2,1)} %bitcast.179, bf16[1024,8,64]{0,2,1:T(8,128)(2,1)} %bitcast.181), kind=kOutput, calls=%fused_computation.11 | convolution fusion | flops 1098899456 | bytes 36732928 | tf_op jit(solution)/shard_map/while/body/eval_jaxpr/qhc,khc->hqk/dot_general | solution.py:109
  48.1 14.3 %exponential_reduce_fusion = f32[8,1024]{1,0:T(8,128)S(1)} fusion(f32[8,1024,1024]{1,2,0:T(8,128)} %get-tuple-element.131, f32[8,1024]{1,0:T(8,128)S(1)} %get-tuple-element.130, pred[1024,1024]{0,1:T(8,128)(4,1)S(1)} %broadcast_compare_fusion), kind=kLoop, calls=%fused_computation.9 | loop fusion | flops 33546240 | bytes 34668544 | tf_op jit(solution)/shard_map/while/body/eval_jaxpr/reduce_sum | solution.py:119
  62.5 16.1 %convolution_convert_fusion.2 = bf16[8,64,1024]{2,1,0:T(8,128)(2,1)} fusion(bf16[1024,8,64]{0,2,1:T(8,128)(2,1)S(1)} %bitcast.187, f32[8,1024,1024]{1,2,0:T(8,128)} %get-tuple-element.131, f32[8,1024]{1,0:T(8,128)S(1)} %log_add_fusion, pred[1024,1024]{0,1:T(8,128)(4,1)S(1)} %broadcast_compare_fusion), kind=kOutput, calls=%fused_computation.88 | convolution fusion | flops 1107820544 | bytes 36732928 | tf_op jit(solution)/shard_map/while/body/eval_jaxpr/hqk,khc->qhc/dot_general | solution.py:122
  90.3 4.1 reshape.480
  94.5 12.0 %scatter_custom_fusion = bf16[3073,512]{1,0:T(8,128)(2,1)} fusion(s32[2048]{0:T(1024)S(1)} %bitcast.205, bf16[2048,512]{1,0:T(8,128)(2,1)} %reshape.480, bf16[]{:T(256)} %constant.86.clone.1), kind=kCustom, calls=%fused_computation.84 | custom fusion | bytes 3147264 | tf_op jit(solution)/shard_map/scatter | solution.py:140
  106.6 3.8 slice.62
  110.3 5.1 copy.103
  115.4 5.3 all-to-all-start
  127.7 5.0 mul.269
  132.7 6.1 mul.270
  138.8 13.0 %scatter_custom_fusion.1 = bf16[3073,512]{1,0:T(8,128)(2,1)} fusion(s32[2048]{0:T(1024)S(1)} %bitcast.206, f32[2048,512]{1,0:T(8,128)} %mul.270, f32[2048]{0:T(1024)S(1)} %mul.267, bf16[]{:T(256)} %constant.86.clone.1), kind=kCustom, calls=%fused_computation.56 | custom fusion | flops 2097152 | bytes 7349250 | tf_op jit(solution)/shard_map/scatter | solution.py:191
  151.8 3.8 slice.63
  158.7 4.6 all-to-all-start.2
  163.3 4.1 copy.126
  167.5 5.4 copy.104
  172.9 5.9 reshape.492
  178.7 21.0 %fusion.11 = (bf16[3072,1,2048]{0,2,1:T(8,128)(2,1)}, f32[3072,2048]{0,1:T(8,128)}) fusion(bf16[3072,512]{0,1:T(8,128)(2,1)} %bitcast.191, bf16[1,512,2048]{2,1,0:T(8,128)(2,1)} %all-gather.3.cloned.1.call-done), kind=kOutput, calls=%fused_computation.25 | convolution fusion | flops 6499074048 | bytes 42991616 | tf_op jit(solution)/shard_map/red,edf->ref/dot_general | solution.py:160
  199.8 13.6 %fusion.17 = bf16[3072,512]{1,0:T(8,128)(2,1)} fusion(bf16[3072,1,2048]{0,2,1:T(8,128)(2,1)} %get-tuple-element.136, bf16[1,2048,512]{2,1,0:T(8,128)(2,1)} %all-gather.5.cloned.1.call-done), kind=kOutput, calls=%fused_computation.31 | convolution fusion | flops 6444023808 | bytes 17825792 | tf_op jit(solution)/shard_map/ref,efd->red/dot_general | solution.py:168
  213.3 4.8 all-to-all-start.1
  218.2 27.1 %fusion.7 = bf16[3072,1,2048]{0,2,1:T(8,128)(2,1)} fusion(f32[3072,2048]{0,1:T(8,128)} %get-tuple-element.137, bf16[3072,512]{1,0:T(8,128)(2,1)} %bitcast.31, bf16[1,2048,512]{2,1,0:T(8,128)(2,1)} %all-gather.5.cloned.1.call-done), kind=kOutput, calls=%fused_computation.18 | convolution fusion | flops 6568280064 | bytes 42991616 | tf_op jit(solution)/shard_map/red,efd->ref/dot_general | solution.py:29
  245.3 11.0 %fusion.20 = bf16[3072,512]{1,0:T(8,128)(2,1)} fusion(bf16[3072,1,2048]{0,2,1:T(8,128)(2,1)} %fusion.7, bf16[1,512,2048]{2,1,0:T(8,128)(2,1)S(1)} %copy-done.57), kind=kOutput, calls=%fused_computation.32 | convolution fusion | flops 6444023808 | bytes 17825792 | tf_op jit(solution)/shard_map/ref,edf->red/dot_general | solution.py:211
  256.3 4.6 all-to-all-start.3
  260.9 11.6 %convert_bitcast_fusion.1 = bf16[4,1,512,512]{3,2,1,0:T(8,128)(2,1)} fusion(bf16[3072,512,1]{0,1,2:T(8,128)(2,1)} %reshape.492, bf16[4,512,3072]{2,1,0:T(8,128)(2,1)} %bitcast.226), kind=kOutput, calls=%fused_computation.69 | convolution fusion | flops 6443499520 | bytes 17825792 | tf_op jit(solution)/shard_map/red,ref->edf/dot_general | solution.py:36
  272.6 11.5 %convert_bitcast_fusion = bf16[4,1,512,512]{3,2,1,0:T(8,128)(2,1)} fusion(bf16[4,512,3072]{2,1,0:T(8,128)(2,1)} %bitcast.225, bf16[3072,512,1]{1,0,2:T(8,128)(2,1)} %bitcast.63), kind=kOutput, calls=%fused_computation.68 | convolution fusion | flops 6443499520 | bytes 17825792 | tf_op jit(solution)/shard_map/ref,red->efd/dot_general | solution.py:33
  284.1 3.7 concatenate.9
  287.8 11.0 %all-to-all-done.3 = bf16[8,384,512]{2,1,0:T(8,128)(2,1)} async-done(((bf16[8,384,512]{2,1,0:T(8,128)(2,1)}), bf16[8,384,512]{2,1,0:T(8,128)(2,1)}, u32[]{:S(2)}, u32[]{:S(2)}) %all-to-all-start.3) | async-done | bytes 3145760 | tf_op jit(solution)/shard_map/all_to_all | solution.py:214
  298.8 5.5 all-to-all-start.5
  304.3 3.7 concatenate.10
  308.0 11.5 %gather_fusion = bf16[2048,512]{1,0:T(8,128)(2,1)} fusion(bf16[3073,512]{1,0:T(8,128)(2,1)} %concatenate.9, s32[2048]{0:T(1024)S(1)} %broadcast_clamp_fusion), kind=kCustom, calls=%fused_computation | custom fusion | bytes 4202496 | tf_op jit(solution)/shard_map/gather | solution.py:177
  319.5 11.5 %gather_fusion.1 = bf16[2048,512]{1,0:T(8,128)(2,1)} fusion(bf16[3073,512]{1,0:T(8,128)(2,1)} %concatenate.10, s32[2048]{0:T(1024)S(1)} %broadcast_clamp_fusion), kind=kCustom, calls=%fused_computation.1 | custom fusion | bytes 4202496 | tf_op jit(solution)/shard_map/gather | solution.py:221
  331.0 5.5 reshape.459
  336.5 8.5 %reduce_sum.312 = f32[1024,512]{1,0:T(8,128)} reduce(f32[1024,2,512]{2,1,0:T(2,128)} %reshape.459, f32[]{:T(128)} %constant.79.clone.1), dimensions={1}, to_apply=%region_18.19 | reduce | flops 524288 | bytes 6291460 | tf_op jit(solution)/shard_map/reduce_sum | solution.py:223
  352.3 5.5 reshape.458
  357.9 11.6 %multiply_reduce_fusion.1 = (f32[1024,2]{1,0:T(8,128)S(1)}, f32[1024,512]{1,0:T(8,128)}) fusion(f32[1024,2,512]{2,1,0:T(2,128)} %reshape.458, f32[1024,512]{1,0:T(8,128)} %copy.108, f32[1024,2]{1,0:T(8,128)S(1)} %copy-done.15), kind=kLoop, calls=%fused_computation.35 | loop fusion | flops 3667968 | bytes 8404992 | tf_op jit(solution)/shard_map/reduce_sum | solution.py:182
  372.5 4.8 fusion.77
  379.6 23.9 %multiply_reduce_fusion = (f32[8,1024]{1,0:T(8,128)S(1)}, f32[8,1024,1024]{1,2,0:T(8,128)}) fusion(f32[8,1024,1024]{1,2,0:T(8,128)} %get-tuple-element.131, f32[8,1024]{1,0:T(8,128)S(1)} %copy-done.20, pred[1024,1024]{0,1:T(8,128)(4,1)S(1)} %copy-done.4, bf16[1024,8,64]{0,2,1:T(8,128)(2,1)S(1)} %bitcast.185, bf16[1024,8,64]{0,2,1:T(8,128)(2,1)S(1)} %bitcast.188), kind=kOutput, calls=%fused_computation.7 | convolution fusion | flops 1115676672 | bytes 70320128 | tf_op jit(solution)/shard_map/while/body/eval_jaxpr/qhc,khc->hqk/dot_general | solution.py:242
  403.5 28.4 %multiply_convert_fusion = bf16[8,1024,1024]{1,2,0:T(8,128)(2,1)} fusion(f32[8,1024,1024]{1,2,0:T(8,128)} %get-tuple-element.139, f32[8,1024,1024]{1,2,0:T(8,128)} %get-tuple-element.131, f32[8,1024]{1,0:T(8,128)S(1)} %get-tuple-element.138, f32[8,1024]{1,0:T(8,128)S(1)} %copy-done.20, pred[1024,1024]{0,1:T(8,128)(4,1)S(1)} %copy-done.4), kind=kLoop, calls=%fused_computation.6 | loop fusion | flops 50331648 | bytes 85000192 | tf_op jit(solution)/shard_map/while/body/eval_jaxpr/convert_element_type | solution.py:252
  431.9 15.9 %convert_reduce_fusion.3 = (f32[8,64]{1,0:T(8,128)S(1)}, bf16[8,64,1024]{2,1,0:T(8,128)(2,1)}) fusion(bf16[1024,8,64]{0,2,1:T(8,128)(2,1)} %bitcast.186, f32[8,1024,1024]{1,2,0:T(8,128)} %get-tuple-element.131, f32[8,1024]{1,0:T(8,128)S(1)} %copy-done.20, pred[1024,1024]{0,1:T(8,128)(4,1)S(1)} %copy-done.4), kind=kOutput, calls=%fused_computation.71 | convolution fusion | flops 1108868608 | bytes 36734976 | tf_op jit(solution)/shard_map/while/body/eval_jaxpr/hqk,qhc->khc/dot_general | solution.py:245
  450.5 10.2 %convert_reduce_fusion.4 = (f32[8,64]{1,0:T(8,128)S(1)}, bf16[8,64,1024]{2,1,0:T(8,128)(2,1)}) fusion(bf16[1024,8,64]{0,2,1:T(8,128)(2,1)} %bitcast.182, bf16[8,1024,1024]{1,2,0:T(8,128)(2,1)} %multiply_convert_fusion), kind=kOutput, calls=%fused_computation.72 | convolution fusion | flops 1075838464 | bytes 18876416 | tf_op jit(solution)/shard_map/while/body/eval_jaxpr/hqk,khc->qhc/dot_general | solution.py:254
  460.8 11.9 %multiply_convert_fusion.3 = bf16[8,64,1024]{2,1,0:T(8,128)(2,1)} fusion(bf16[1024,8,64]{0,2,1:T(8,128)(2,1)S(1)} %bitcast.180, bf16[8,1024,1024]{1,2,0:T(8,128)(2,1)} %multiply_convert_fusion), kind=kOutput, calls=%fused_computation.74 | convolution fusion | flops 1074790400 | bytes 18874368 | tf_op jit(solution)/shard_map/while/body/eval_jaxpr/hqk,qhc->khc/dot_general | solution.py:258
  472.7 5.0 fusion.83
  480.7 5.1 all-to-all-start.4
  486.1 3.8 fusion.52
  489.9 4.8 fusion.50
  505.6 60.9 %all-reduce.2 = (f32[2,512]{1,0:T(2,128)}, f32[512]{0:T(512)}, f32[2,512]{1,0:T(2,128)}, f32[2,512]{1,0:T(2,128)}, f32[30,2]{0,1:T(2,128)}) all-reduce(f32[2,512]{1,0:T(2,128)S(1)} %get-tuple-element.146, f32[512]{0:T(512)S(1)} %get-tuple-element.119, ...), channel_id=1, replica_groups=mesh['expert'=8,'hidden'=4] {'expert','hidden'}, use_global_device_ids=true, to_apply=%region_27.28 | all-reduce | flops 3644 | bytes 29152 | tf_op jit(solution)/shard_map/psum | solution.py:297
  572.5 89.5 %all-reduce.6.cloned.1.call-done = (f32[512,1536]{1,0:T(8,128)}, f32[512,512]{1,0:T(8,128)}) async-done(((f32[512,1536]{1,0:T(8,128)}, f32[512,512]{1,0:T(8,128)}), (f32[512,1536]{1,0:T(8,128)}, f32[512,512]{1,0:T(8,128)})) %all-reduce.6.cloned.1.call-update) | async-done | bytes 4194320 | tf_op jit(solution)/shard_map/psum | solution.py:297
  662.0 3.8 copy.131
  (208 shorter events, 80.3 us)
Async XLA Ops:
  7.2 12.7 %copy-start = (bf16[512,1536]{1,0:T(8,128)(2,1)S(1)}, bf16[512,1536]{1,0:T(8,128)(2,1)}, u32[]{:S(2)}) copy-start(bf16[512,1536]{1,0:T(8,128)(2,1)} %param.16) | copy-start | bytes 4718596
  7.2 5.0 copy-start.52
  7.2 5.0 copy-start.53
  7.2 5.0 copy-start.54
  7.2 171.5 %all-gather.3.cloned.1.call-start = ((), (), s32[]{:S(2)}) async-start(), calls=%async_computation.6 | async-start | bytes 2621440 | tf_op jit(solution)/shard_map/all_gather | solution.py:70
  10.4 111.0 %copy-start.50 = (s32[1024]{0:T(1024)}, s32[1024]{0:T(1024)S(1)}, u32[]{:S(2)}) copy-start(s32[1024]{0:T(1024)S(1)} %select_reduce_fusion.1) | copy-start | bytes 12292
  12.2 50.3 %copy-start.3 = (pred[1024,1024]{0,1:T(8,128)(4,1)}, pred[1024,1024]{0,1:T(8,128)(4,1)S(1)}, u32[]{:S(2)}) copy-start(pred[1024,1024]{0,1:T(8,128)(4,1)S(1)} %broadcast_compare_fusion) | copy-start | bytes 3145732
  12.2 10.9 %copy-start.48 = (f32[1,512]{1,0:T(1,128)}, f32[1,512]{1,0:T(1,128)S(1)}, u32[]{:S(2)}) copy-start(f32[1,512]{1,0:T(1,128)S(1)} %get-tuple-element.125) | copy-start | bytes 6148
  12.2 71.2 %copy-start.34 = (f32[1,512]{1,0:T(1,128)}, f32[1,512]{1,0:T(1,128)S(1)}, u32[]{:S(2)}) copy-start(f32[1,512]{1,0:T(1,128)S(1)} %get-tuple-element.124) | copy-start | bytes 6148
  12.2 10.9 %copy-start.55 = (f32[1,512]{1,0:T(1,128)}, f32[1,512]{1,0:T(1,128)S(1)}, u32[]{:S(2)}) copy-start(f32[1,512]{1,0:T(1,128)S(1)} %get-tuple-element.127) | copy-start | bytes 6148
  18.2 4.9 copy-start.28
  48.1 14.3 %copy-start.17 = (bf16[1024,512]{0,1:T(8,128)(2,1)S(1)}, bf16[1024,512]{0,1:T(8,128)(2,1)}, u32[]{:S(2)}) copy-start(bf16[1024,512]{0,1:T(8,128)(2,1)} %copy.93) | copy-start | bytes 3145732
  62.4 16.2 %copy-start.19 = (f32[8,1024]{1,0:T(8,128)}, f32[8,1024]{1,0:T(8,128)S(1)}, u32[]{:S(2)}) copy-start(f32[8,1024]{1,0:T(8,128)S(1)} %log_add_fusion) | copy-start | bytes 98308
  62.5 16.2 %copy-start.5 = (bf16[1024,512]{0,1:T(8,128)(2,1)S(1)}, bf16[1024,512]{0,1:T(8,128)(2,1)}, u32[]{:S(2)}) copy-start(bf16[1024,512]{0,1:T(8,128)(2,1)} %copy.92) | copy-start | bytes 3145732
  62.5 16.2 %copy-start.24 = (bf16[512,512]{1,0:T(8,128)(2,1)S(1)}, bf16[512,512]{1,0:T(8,128)(2,1)}, u32[]{:S(2)}) copy-start(bf16[512,512]{1,0:T(8,128)(2,1)} %param.18) | copy-start | bytes 1572868
  62.5 16.2 %copy-start.58 = (f32[512]{0:T(512)S(1)}, f32[512]{0:T(512)}, u32[]{:S(2)}) copy-start(f32[512]{0:T(512)} %param.19) | copy-start | bytes 6148
  82.4 5.5 copy-start.38
  115.4 6.1 copy-start.59
  115.4 43.3 %all-to-all-start = ((bf16[8,384,512]{1,2,0:T(8,128)(2,1)}), bf16[8,384,512]{1,2,0:T(8,128)(2,1)}, u32[]{:S(2)}, u32[]{:S(2)}) async-start(bf16[8,384,512]{1,2,0:T(8,128)(2,1)} %copy.103), calls=%async_computation | async-start | bytes 6291456 | tf_op jit(solution)/shard_map/all_to_all | solution.py:143
  120.7 79.0 %all-gather.5.cloned.1.call-start = ((), (), s32[]{:S(2)}) async-start(), calls=%async_computation.7 | async-start | bytes 2621440 | tf_op jit(solution)/shard_map/all_gather | solution.py:71
  126.0 6.6 copy-start.12
  158.7 54.6 %all-to-all-start.2 = ((bf16[8,384,512]{2,1,0:T(8,128)(2,1)}), bf16[8,384,512]{2,1,0:T(8,128)(2,1)}, u32[]{:S(2)}, u32[]{:S(2)}) async-start(bf16[8,384,512]{2,1,0:T(8,128)(2,1)} %bitcast.183), calls=%async_computation.2 | async-start | bytes 6291456 | tf_op jit(solution)/shard_map/all_to_all | solution.py:194
  213.3 43.0 %all-to-all-start.1 = ((bf16[8,384,512]{2,1,0:T(8,128)(2,1)}), bf16[8,384,512]{2,1,0:T(8,128)(2,1)}, u32[]{:S(2)}, u32[]{:S(2)}) async-start(bf16[8,384,512]{2,1,0:T(8,128)(2,1)} %bitcast.190), calls=%async_computation.1 | async-start | bytes 6291456 | tf_op jit(solution)/shard_map/all_to_all | solution.py:171
  218.2 27.1 %copy-start.57 = (bf16[1,512,2048]{2,1,0:T(8,128)(2,1)S(1)}, bf16[1,512,2048]{2,1,0:T(8,128)(2,1)}, u32[]{:S(2)}) copy-start(bf16[1,512,2048]{2,1,0:T(8,128)(2,1)} %all-gather.3.cloned.1.call-done) | copy-start | bytes 6291460
  256.3 42.5 %all-to-all-start.3 = ((bf16[8,384,512]{2,1,0:T(8,128)(2,1)}), bf16[8,384,512]{2,1,0:T(8,128)(2,1)}, u32[]{:S(2)}, u32[]{:S(2)}) async-start(bf16[8,384,512]{2,1,0:T(8,128)(2,1)} %bitcast.189), calls=%async_computation.3 | async-start | bytes 6291456 | tf_op jit(solution)/shard_map/all_to_all | solution.py:214
  298.8 181.9 %all-to-all-start.5 = ((bf16[4,1,512,512]{3,2,1,0:T(8,128)(2,1)}), bf16[4,1,512,512]{3,2,1,0:T(8,128)(2,1)}, u32[]{:S(2)}, u32[]{:S(2)}) async-start(bf16[4,1,512,512]{3,2,1,0:T(8,128)(2,1)} %convert_bitcast_fusion), calls=%async_computation.5 | async-start | bytes 4194304 | tf_op jit(solution)/shard_map/all_to_all | solution.py:199
  348.0 3.5 copy-start.10
  352.3 5.6 copy-start.15
  372.5 6.3 copy-start.25
  379.5 24.0 %copy-start.16 = (bf16[1024,512]{0,1:T(8,128)(2,1)}, bf16[1024,512]{0,1:T(8,128)(2,1)S(1)}, u32[]{:S(2)}) copy-start(bf16[1024,512]{0,1:T(8,128)(2,1)S(1)} %convolution_convert_fusion) | copy-start | bytes 3145732
  450.5 10.3 %copy-start.11 = (bf16[1024,512]{0,1:T(8,128)(2,1)S(1)}, bf16[1024,512]{0,1:T(8,128)(2,1)}, u32[]{:S(2)}) copy-start(bf16[1024,512]{0,1:T(8,128)(2,1)} %copy.94) | copy-start | bytes 3145732
  480.7 88.8 %all-to-all-start.4 = ((bf16[4,1,512,512]{3,2,1,0:T(8,128)(2,1)}), bf16[4,1,512,512]{3,2,1,0:T(8,128)(2,1)}, u32[]{:S(2)}, u32[]{:S(2)}) async-start(bf16[4,1,512,512]{3,2,1,0:T(8,128)(2,1)} %convert_bitcast_fusion.1), calls=%async_computation.4 | async-start | bytes 4194304 | tf_op jit(solution)/shard_map/all_to_all | solution.py:199
  485.8 4.1 copy-start.6
  485.8 4.1 copy-start.29
  485.8 4.1 copy-start.45
  485.8 4.1 copy-start.49
  485.8 4.1 copy-start.56
  485.8 176.2 %all-reduce.6.cloned.1.call-start = ((), (), s32[]{:S(2)}) async-start(), calls=%async_computation.8 | async-start | bytes 8388608 | tf_op jit(solution)/shard_map/psum | solution.py:297
  486.1 3.8 copy-start.21
  486.1 3.8 copy-start.22
  494.8 4.6 copy-start.8
  494.8 4.6 copy-start.9
  501.2 4.3 copy-start.31
  501.2 4.3 copy-start.41
  501.2 4.3 copy-start.43
  501.2 4.3 copy-start.47
  501.2 4.3 copy-start.51
  662.0 3.8 copy-start.23
  (21 other events, 43.5 us)
Sparse Core Ops, SparseCore 0:
  9.6 48.6 all-gather.2
  123.1 48.2 all-gather.4
  494.9 167.0 all-reduce.5

commit v2 on v0

v2 whole, which is shorter than its diff:
```python
import functools

import jax
import jax.numpy as jnp
from jax import lax
from jax.experimental import pallas as pl
from jax.experimental.pallas import tpu as pltpu
from jax.sharding import PartitionSpec as P

HEADS = 8
HD = 64
NORM_EPS = 1e-05
MASK_FILL = -1000000000.0

BF = jnp.bfloat16
F32 = jnp.float32
MIB = 1 << 20

ROWS = 256
QROWS = 128
REACH = 64
KROWS = QROWS + 2 * REACH
PAIR = 2 * HD


def iota(shape, dim):
    return lax.broadcasted_iota(jnp.int32, shape, dim)


def dot(left, right):
    return jnp.dot(left, right, preferred_element_type=F32)


def dot_nt(left, right):
    return lax.dot_general(left, right, (((1,), (1,)), ((), ())), preferred_element_type=F32)


def dot_tn(left, right):
    return lax.dot_general(left, right, (((0,), (0,)), ((), ())), preferred_element_type=F32)


def over_lanes(mask, values):
    return jnp.sum(jnp.where(mask, values, 0.0), axis=1, keepdims=True)


def over_rows(mask, values):
    return jnp.sum(jnp.where(mask, values, 0.0), axis=0, keepdims=True)


def to_column(row):
    count = row.shape[1]
    return over_lanes(iota((count, count), 0) == iota((count, count), 1), row)


def centred_of(values):
    centred = values - jnp.mean(values, axis=-1, keepdims=True)
    spread = jnp.mean(centred * centred, axis=-1, keepdims=True)
    return centred * lax.rsqrt(spread + NORM_EPS), lax.rsqrt(spread + NORM_EPS)


def norm_back(grad, hat, scale, gain):
    scaled = grad * gain
    return scale * (
        scaled
        - jnp.mean(scaled, axis=-1, keepdims=True)
        - hat * jnp.mean(scaled * hat, axis=-1, keepdims=True)
    )


def sentence_bounds(lengths_ref):
    len_row = lengths_ref[...].astype(F32)
    count = len_row.shape[1]
    len_col = to_column(len_row)
    below = iota((count, count), 1) < iota((count, count), 0)
    above = iota((count, count), 0) < iota((count, count), 1)
    start_col = over_lanes(below, len_row)
    start_row = over_rows(above, len_col)
    return (len_row, len_col, start_row, start_col)


def routing(lengths_ref, task_ref, routes_ref, table_ref, me, capacity):
    len_row, len_col, start_row, start_col = sentence_bounds(lengths_ref)
    count = len_row.shape[1]
    tasks = routes_ref.shape[0]
    hit = iota((tasks, count), 0) == task_ref[...]
    expert_rows = [over_rows(hit, routes_ref[:, r : r + 1].astype(F32)) for r in range(2)]
    logit_rows = [over_rows(hit, table_ref[:, r : r + 1]) for r in range(2)]
    peak = jnp.maximum(logit_rows[0], logit_rows[1])
    raised = [jnp.exp(row - peak) for row in logit_rows]
    gate_rows = [row / (raised[0] + raised[1]) for row in raised]
    expert_cols = [to_column(row) for row in expert_rows]
    earlier = iota((count, count), 0) < iota((count, count), 1)
    add_rows, far_rows = [], []
    for row in expert_rows:
        same = (expert_cols[0] == row) | (expert_cols[1] == row)
        add_rows.append(over_rows(earlier & same, len_col) - start_row)
        far_rows.append((row.astype(jnp.int32) ^ me).astype(F32))
    return (len_row, len_col, start_row, start_col, far_rows, gate_rows, add_rows)


def dispatch_body(
    weighted, capacity, me_ref, len_ref, task_ref, routes_ref, table_ref, data_ref, *out_refs
):
    me = me_ref[0]
    tables = routing(len_ref, task_ref, routes_ref, table_ref, me, capacity)
    len_row, len_col, start_row, start_col, far_rows, gate_rows, add_rows = tables
    tok_count = data_ref.shape[0]
    count = len_row.shape[1]
    place = iota((count, tok_count), 1).astype(F32)
    inside = (place >= start_col) & (place < start_col + len_col)
    token_place = iota((1, tok_count), 1).astype(F32)

    def per_token(row):
        return over_rows(inside, to_column(row))

    far = [per_token(row) for row in far_rows]
    position = [token_place + per_token(row) for row in add_rows]
    gates = [per_token(row) for row in gate_rows]
    data = data_ref[...]
    slots = iota((capacity, tok_count), 0)
    for k, out_ref in enumerate(out_refs):
        first = far[0] == k
        slot = jnp.where(first, position[0], jnp.where(far[1] == k, position[1], -1.0))
        hit = slots == slot.astype(jnp.int32)
        picked = dot(hit.astype(F32).astype(BF), data)
        if weighted:
            picked = picked * over_lanes(hit, jnp.where(first, gates[0], gates[1]))
        out_ref[...] = picked.astype(BF)


def dispatch(weighted, capacity, groups, me, lengths, seg_task, routes, gate_table, data):
    tok_count, width = data.shape
    whole = pl.BlockSpec(memory_space=pltpu.VMEM)
    return pl.pallas_call(
        functools.partial(dispatch_body, weighted, capacity),
        out_shape=[jax.ShapeDtypeStruct((capacity, width), BF)] * groups,
        in_specs=[pl.BlockSpec(memory_space=pltpu.SMEM)] + [whole] * 5,
        out_specs=[whole] * groups,
        compiler_params=pltpu.CompilerParams(vmem_limit_bytes=40 * MIB),
        cost_estimate=pl.CostEstimate(
            flops=2 * groups * capacity * tok_count * width,
            bytes_accessed=2 * width * (tok_count + groups * capacity),
            transcendentals=0,
        ),
        name="dispatch_grads" if weighted else "dispatch_rows",
    )(me, lengths, seg_task, routes, gate_table, data)


def window_start(block, tok_count):
    start = jnp.clip(block * QROWS - REACH, 0, tok_count - KROWS)
    return pl.multiple_of(start, REACH)


def split_heads(block):
    low = iota(block.shape, 1) < HD
    zero = jnp.zeros_like(block)
    return jnp.concatenate([jnp.where(low, block, zero), jnp.where(low, zero, block)], axis=0)


def join_heads(stacked):
    half = stacked.shape[0] // 2
    low = iota((half, stacked.shape[1]), 1) < HD
    return jnp.where(low, stacked[:half], stacked[half:])


def attend_body(
    len_ref,
    tok_ref,
    wqkv_ref,
    bias_ref,
    wout_ref,
    obias_ref,
    gains_ref,
    shifts_ref,
    qkv_ref,
    att_ref,
    hid_ref,
    one_ref,
    two_ref,
):
    tok_count, width = tok_ref.shape
    len_row, len_col, start_row, start_col = sentence_bounds(len_ref)
    end_row, end_col = start_row + len_row, start_col + len_col
    count = len_row.shape[1]

    def project(step, carry):
        rows = pl.ds(pl.multiple_of(step * ROWS, ROWS), ROWS)
        hat, _ = centred_of(tok_ref[rows, :].astype(F32))
        one = (hat * gains_ref[0:1, :] + shifts_ref[0:1, :]).astype(BF)
        one_ref[rows, :] = one
        qkv = dot(one, wqkv_ref[...])
        queries = (qkv[:, :width] + bias_ref[0:1, :]).astype(BF)
        qkv_ref[rows, :width] = queries * jnp.asarray(HD**-0.5, BF)
        qkv_ref[rows, width : 2 * width] = qkv[:, width : 2 * width].astype(BF)
        qkv_ref[rows, 2 * width :] = (qkv[:, 2 * width :] + bias_ref[1:2, :]).astype(BF)
        return carry

    lax.fori_loop(0, tok_count // ROWS, project, 0)

    def attend(block, carry):
        rows = pl.ds(pl.multiple_of(block * QROWS, QROWS), QROWS)
        start = window_start(block, tok_count)
        keys = pl.ds(start, KROWS)
        key_place = (iota((count, KROWS), 1) + start).astype(F32)
        key_seg = jnp.sum((key_place >= end_col).astype(F32), axis=0, keepdims=True)
        query_place = (iota((QROWS, count), 0) + block * QROWS).astype(F32)
        query_seg = jnp.sum((query_place >= end_row).astype(F32), axis=1, keepdims=True)
        same = key_seg == query_seg
        same = jnp.concatenate([same, same], axis=0)
        for pair in range(width // PAIR):
            lanes = slice(pair * PAIR, (pair + 1) * PAIR)
            stacked = split_heads(qkv_ref[rows, lanes])
            key_rows = qkv_ref[keys, slice(width + lanes.start, width + lanes.stop)]
            value_rows = qkv_ref[keys, slice(2 * width + lanes.start, 2 * width + lanes.stop)]
            scores = jnp.where(same, dot_nt(stacked, key_rows), MASK_FILL)
            raised = jnp.exp(scores - jnp.max(scores, axis=1, keepdims=True))
            total = jnp.sum(raised, axis=1, keepdims=True)
            probs = (raised * (1.0 / total)).astype(BF)
            att_ref[rows, lanes] = join_heads(dot(probs, value_rows)).astype(BF)
        return carry

    lax.fori_loop(0, tok_count // QROWS, attend, 0)

    def finish(step, carry):
        rows = pl.ds(pl.multiple_of(step * ROWS, ROWS), ROWS)
        hidden = tok_ref[rows, :].astype(F32) + dot(att_ref[rows, :], wout_ref[...]) + obias_ref[...]
        hid_ref[rows, :] = hidden
        hat, _ = centred_of(hidden)
        two_ref[rows, :] = (hat * gains_ref[1:2, :] + shifts_ref[1:2, :]).astype(BF)
        return carry

    lax.fori_loop(0, tok_count // ROWS, finish, 0)


def attend_forward(lengths, tokens, w_qkv, bias_qv, w_out, out_bias, gains, shifts):
    tok_count, width = tokens.shape
    whole = pl.BlockSpec(memory_space=pltpu.VMEM)
    return pl.pallas_call(
        attend_body,
        out_shape=[
            jax.ShapeDtypeStruct((tok_count, 3 * width), BF),
            jax.ShapeDtypeStruct((tok_count, width), BF),
            jax.ShapeDtypeStruct((tok_count, width), F32),
            jax.ShapeDtypeStruct((tok_count, width), BF),
            jax.ShapeDtypeStruct((tok_count, width), BF),
        ],
        in_specs=[whole] * 8,
        out_specs=[whole] * 5,
        compiler_params=pltpu.CompilerParams(vmem_limit_bytes=40 * MIB),
        cost_estimate=pl.CostEstimate(
            flops=8 * tok_count * width * width + 16 * tok_count * KROWS * width,
            bytes_accessed=20 * tok_count * width,
            transcendentals=tok_count * KROWS * HEADS,
        ),
        name="attend_forward",
    )(lengths, tokens, w_qkv, bias_qv, w_out, out_bias.reshape(1, width), gains, shifts)


GELU_A = 0.7978845608028654
GELU_B = 0.044715


def gelu_both(values):
    square = values * values
    inner = values * (GELU_A + (GELU_A * GELU_B) * square)
    half = 0.5 * jnp.tanh(inner) + 0.5
    active = values * half
    slope = half + active * (1.0 - half) * (2.0 * GELU_A + (6.0 * GELU_A * GELU_B) * square)
    return active, slope


def load_all(pairs, sem):
    copies = [pltpu.make_async_copy(source, target, sem.at[i]) for i, (source, target) in enumerate(pairs)]
    for copy in copies:
        copy.start()
    for copy in copies:
        copy.wait()


def expert_body(blocks, planes, *refs):
    refs = list(refs)
    take = lambda count: [refs.pop(0) for _ in range(count)]
    x_in, g_in = take(blocks), take(blocks)
    w_in, w_down = take(planes), take(planes)
    out_refs, dx_refs = take(blocks), take(blocks)
    act_ref, pre_ref, xt_ref, gt_ref = take(4)
    xs, gs, sem = take(3)
    cap = x_in[0].shape[0]
    hid = w_in[0].shape[1]
    spots = [pl.ds(i * cap, cap) for i in range(blocks)]
    load_all(
        [(ref, xs.at[spot]) for ref, spot in zip(x_in, spots)]
        + [(ref, gs.at[spot]) for ref, spot in zip(g_in, spots)],
        sem,
    )
    x, g = xs[...], gs[...]
    out = dx = None
    for c in range(planes):
        lanes = slice(c * hid, (c + 1) * hid)
        active, slope = gelu_both(dot(x, w_in[c][...]))
        active = active.astype(BF)
        grad_pre = (dot_nt(g, w_down[c][...]) * slope).astype(BF)
        act_ref[:, lanes] = active
        pre_ref[:, lanes] = grad_pre
        new_out = dot(active, w_down[c][...])
        new_dx = dot_nt(grad_pre, w_in[c][...])
        out = new_out if out is None else out + new_out
        dx = new_dx if dx is None else dx + new_dx
    for i, spot in enumerate(spots):
        dx_refs[i][...] = dx[i * cap : (i + 1) * cap].astype(BF)
        out_refs[i][...] = out[i * cap : (i + 1) * cap].astype(BF)
    xt_ref[...] = x.T
    gt_ref[...] = g.T


def expert_rows(x_blocks, g_blocks, w_in, w_down):
    blocks, planes = len(x_blocks), len(w_in)
    cap, width = x_blocks[0].shape
    hid = w_in[0].shape[1]
    rows = blocks * cap
    whole = pl.BlockSpec(memory_space=pltpu.VMEM)
    anywhere = pl.BlockSpec(memory_space=pl.ANY)
    slot = jax.ShapeDtypeStruct((cap, width), BF)
    units = jax.ShapeDtypeStruct((rows, planes * hid), BF)
    turned = jax.ShapeDtypeStruct((width, rows), BF)
    result = pl.pallas_call(
        functools.partial(expert_body, blocks, planes),
        out_shape=[slot] * (2 * blocks) + [units] * 2 + [turned] * 2,
        in_specs=[anywhere] * (2 * blocks) + [whole] * (2 * planes),
        out_specs=[whole] * (2 * blocks + 4),
        scratch_shapes=[
            pltpu.VMEM((rows, width), BF),
            pltpu.VMEM((rows, width), BF),
            pltpu.SemaphoreType.DMA((2 * blocks,)),
        ],
        compiler_params=pltpu.CompilerParams(vmem_limit_bytes=56 * MIB),
        cost_estimate=pl.CostEstimate(
            flops=8 * rows * width * planes * hid,
            bytes_accessed=4 * rows * planes * hid + 12 * rows * width,
            transcendentals=rows * planes * hid,
        ),
        name="expert_rows",
    )(*x_blocks, *g_blocks, *w_in, *w_down)
    return (
        result[:blocks],
        result[blocks : 2 * blocks],
        result[2 * blocks],
        result[2 * blocks + 1],
        result[2 * blocks + 2],
        result[2 * blocks + 3],
    )


def weight_body(calls, *refs):
    act, pre, xt, gt = (refs[i * calls : (i + 1) * calls] for i in range(4))
    out_ref = refs[4 * calls]
    width = xt[0].shape[0]
    grad_in = grad_down = None
    for i in range(calls):
        new_in = dot(xt[i][...], pre[i][...])
        new_down = dot(gt[i][...], act[i][...])
        grad_in = new_in if grad_in is None else grad_in + new_in
        grad_down = new_down if grad_down is None else grad_down + new_down
    out_ref[0, :width, :] = grad_in.astype(out_ref.dtype)
    out_ref[0, width:, :] = grad_down.astype(out_ref.dtype)


def weight_grads(first, count, planes, dtype, act, pre, xt, gt):
    calls = len(act)
    width, rows = xt[0].shape
    hid = act[0].shape[1] // planes
    units = pl.BlockSpec((rows, hid), lambda i: (0, (i + first) % planes))
    turned = pl.BlockSpec((width, rows), lambda i: (0, 0))
    return pl.pallas_call(
        functools.partial(weight_body, calls),
        grid=(count,),
        out_shape=jax.ShapeDtypeStruct((count, 2 * width, hid), dtype),
        in_specs=[units] * (2 * calls) + [turned] * (2 * calls),
        out_specs=pl.BlockSpec((1, 2 * width, hid), lambda i: (i, 0, 0)),
        compiler_params=pltpu.CompilerParams(vmem_limit_bytes=56 * MIB),
        cost_estimate=pl.CostEstimate(
            flops=4 * count * calls * rows * width * hid,
            bytes_accessed=4 * calls * rows * (count * hid + width),
            transcendentals=0,
        ),
        name="weight_grads",
    )(*act, *pre, *xt, *gt)


def token_slots(tables, tok_count, capacity):
    len_row, _, start_row, _, far_rows, gate_rows, add_rows = tables
    count = len_row.shape[1]
    place = iota((tok_count, count), 0).astype(F32)
    inside = (place >= start_row) & (place < start_row + len_row)
    columns = []
    for far, add in zip(far_rows, add_rows):
        kept = inside & (place + add < capacity)
        columns.append((over_lanes(kept, place + (add + far * capacity + 1.0)) - 1.0).astype(jnp.int32))
    gates = [over_lanes(inside, row) for row in gate_rows]
    return columns, gates, inside


def first_back_body(
    groups,
    capacity,
    me_ref,
    len_ref,
    task_ref,
    routes_ref,
    table_ref,
    cot_ref,
    hid_ref,
    att_ref,
    wout_ref,
    gains_ref,
    *refs,
):
    back_refs = refs[:groups]
    grad_ref, gatt_ref, gout_ref, small_ref, back, slot_ref, sem = refs[groups:]
    load = [(ref, back.at[pl.ds(i * capacity, capacity)]) for i, ref in enumerate(back_refs)]
    tok_count, width = cot_ref.shape
    tables = routing(len_ref, task_ref, routes_ref, table_ref, me_ref[0], capacity)
    columns, _, _ = token_slots(tables, tok_count, capacity)
    slot_ref[:, 0:1] = columns[0]
    slot_ref[:, 1:2] = columns[1]
    load_all(load, sem)
    small_ref[...] = jnp.zeros_like(small_ref)

    def step(index, carry):
        rows = pl.ds(pl.multiple_of(index * ROWS, ROWS), ROWS)
        slots = iota((ROWS, groups * capacity), 1)
        hit = (slots == slot_ref[rows, 0:1]) | (slots == slot_ref[rows, 1:2])
        grad_two = dot(hit.astype(F32).astype(BF), back[...])
        hat, scale = centred_of(hid_ref[rows, :])
        grad = cot_ref[rows, :].astype(F32) + norm_back(grad_two, hat, scale, gains_ref[1:2, :])
        grad_ref[rows, :] = grad
        small_ref[0:1, :] += jnp.sum(grad_two * hat, axis=0, keepdims=True)
        small_ref[1:2, :] += jnp.sum(grad_two, axis=0, keepdims=True)
        small_ref[2:3, :] += jnp.sum(grad, axis=0, keepdims=True)
        low = grad.astype(BF)
        gatt_ref[rows, :] = dot_nt(low, wout_ref[...]).astype(BF)
        return carry

    lax.fori_loop(0, tok_count // ROWS, step, 0)
    gout_ref[...] = dot_tn(att_ref[...], grad_ref[...].astype(BF)).astype(gout_ref.dtype)


def first_back(me, lengths, seg_task, routes, gate_table, cotangent, hidden, attended, w_out, gains, back, capacity):
    tok_count, width = cotangent.shape
    groups = len(back)
    whole = pl.BlockSpec(memory_space=pltpu.VMEM)
    return pl.pallas_call(
        functools.partial(first_back_body, groups, capacity),
        out_shape=[
            jax.ShapeDtypeStruct((tok_count, width), F32),
            jax.ShapeDtypeStruct((tok_count, width), BF),
            jax.ShapeDtypeStruct((width, width), F32),
            jax.ShapeDtypeStruct((8, width), F32),
        ],
        in_specs=[pl.BlockSpec(memory_space=pltpu.SMEM)]
        + [whole] * 9
        + [pl.BlockSpec(memory_space=pl.ANY)] * groups,
        out_specs=[whole] * 4,
        scratch_shapes=[
            pltpu.VMEM((groups * capacity, width), BF),
            pltpu.VMEM((tok_count, 2), jnp.int32),
            pltpu.SemaphoreType.DMA((groups,)),
        ],
        compiler_params=pltpu.CompilerParams(vmem_limit_bytes=56 * MIB),
        cost_estimate=pl.CostEstimate(
            flops=2 * tok_count * width * (groups * capacity + 2 * width),
            bytes_accessed=16 * tok_count * width,
            transcendentals=0,
        ),
        name="first_back",
    )(me, lengths, seg_task, routes, gate_table, cotangent, hidden, attended, w_out, gains, *back)


def attend_back_body(
    len_ref, qkv_ref, gatt_ref, one_ref, gqkv_ref, dqkv_ref, small_ref, key_acc, value_acc
):
    tok_count, width = gatt_ref.shape
    len_row, len_col, start_row, start_col = sentence_bounds(len_ref)
    end_row, end_col = start_row + len_row, start_col + len_col
    count = len_row.shape[1]
    key_acc[...] = jnp.zeros_like(key_acc)
    value_acc[...] = jnp.zeros_like(value_acc)

    def step(block, carry):
        rows = pl.ds(pl.multiple_of(block * QROWS, QROWS), QROWS)
        start = window_start(block, tok_count)
        keys = pl.ds(start, KROWS)
        query_place = (iota((count, QROWS), 1) + block * QROWS).astype(F32)
        query_seg = jnp.sum((query_place >= end_col).astype(F32), axis=0, keepdims=True)
        key_place = (iota((KROWS, count), 0) + start).astype(F32)
        key_seg = jnp.sum((key_place >= end_row).astype(F32), axis=1, keepdims=True)
        same = key_seg == query_seg
        same = jnp.concatenate([same, same], axis=1)
        for pair in range(width // PAIR):
            lanes = slice(pair * PAIR, (pair + 1) * PAIR)
            stacked = split_heads(qkv_ref[rows, lanes])
            grads = split_heads(gatt_ref[rows, lanes])
            key_rows = qkv_ref[keys, slice(width + lanes.start, width + lanes.stop)]
            value_rows = qkv_ref[keys, slice(2 * width + lanes.start, 2 * width + lanes.stop)]
            scores = jnp.where(same, dot_nt(key_rows, stacked), MASK_FILL)
            raised = jnp.exp(scores - jnp.max(scores, axis=0, keepdims=True))
            probs = raised * (1.0 / jnp.sum(raised, axis=0, keepdims=True))
            grad_probs = dot_nt(value_rows, grads)
            inner = jnp.sum(probs * grad_probs, axis=0, keepdims=True)
            grad_scores = (probs * (grad_probs - inner)).astype(BF)
            value_acc[keys, lanes] += dot(probs.astype(BF), grads)
            key_acc[keys, lanes] += dot(grad_scores, stacked)
            grad_queries = join_heads(dot_tn(grad_scores, key_rows)) * HD**-0.5
            dqkv_ref[rows, lanes] = grad_queries.astype(BF)
        return carry

    lax.fori_loop(0, tok_count // QROWS, step, 0)
    dqkv_ref[:, width : 2 * width] = key_acc[...].astype(BF)
    dqkv_ref[:, 2 * width :] = value_acc[...].astype(BF)
    small_ref[...] = jnp.zeros_like(small_ref)
    small_ref[0:1, :] = jnp.sum(dqkv_ref[:, :width].astype(F32), axis=0, keepdims=True)
    small_ref[1:2, :] = jnp.sum(dqkv_ref[:, 2 * width :].astype(F32), axis=0, keepdims=True)
    gqkv_ref[...] = dot_tn(one_ref[...], dqkv_ref[...]).astype(gqkv_ref.dtype)


def attend_back(lengths, qkv, grad_attended, normed_one):
    tok_count, width = grad_attended.shape
    whole = pl.BlockSpec(memory_space=pltpu.VMEM)
    return pl.pallas_call(
        attend_back_body,
        out_shape=[
            jax.ShapeDtypeStruct((width, 3 * width), F32),
            jax.ShapeDtypeStruct((tok_count, 3 * width), BF),
            jax.ShapeDtypeStruct((8, width), F32),
        ],
        in_specs=[whole] * 4,
        out_specs=[whole] * 3,
        scratch_shapes=[
            pltpu.VMEM((tok_count, width), F32),
            pltpu.VMEM((tok_count, width), F32),
        ],
        compiler_params=pltpu.CompilerParams(vmem_limit_bytes=56 * MIB),
        cost_estimate=pl.CostEstimate(
            flops=40 * tok_count * KROWS * width + 6 * tok_count * width * width,
            bytes_accessed=24 * tok_count * width,
            transcendentals=tok_count * KROWS * HEADS,
        ),
        name="attend_back",
    )(lengths, qkv, grad_attended, normed_one)


def last_back_body(dqkv_ref, wqkv_ref, tok_ref, grad_ref, gains_ref, out_ref, small_ref):
    tok_count, width = tok_ref.shape
    small_ref[...] = jnp.zeros_like(small_ref)

    def step(index, carry):
        rows = pl.ds(pl.multiple_of(index * ROWS, ROWS), ROWS)
        grad_one = dot_nt(dqkv_ref[rows, :], wqkv_ref[...])
        hat, scale = centred_of(tok_ref[rows, :].astype(F32))
        back = norm_back(grad_one, hat, scale, gains_ref[0:1, :])
        out_ref[rows, :] = (grad_ref[rows, :] + back).astype(BF)
        small_ref[0:1, :] += jnp.sum(grad_one * hat, axis=0, keepdims=True)
        small_ref[1:2, :] += jnp.sum(grad_one, axis=0, keepdims=True)
        return carry

    lax.fori_loop(0, tok_count // ROWS, step, 0)


def last_back(dqkv, w_qkv, tokens, grad_hidden, gains):
    tok_count, width = tokens.shape
    whole = pl.BlockSpec(memory_space=pltpu.VMEM)
    return pl.pallas_call(
        last_back_body,
        out_shape=[
            jax.ShapeDtypeStruct((tok_count, width), BF),
            jax.ShapeDtypeStruct((8, width), F32),
        ],
        in_specs=[whole] * 5,
        out_specs=[whole] * 2,
        compiler_params=pltpu.CompilerParams(vmem_limit_bytes=40 * MIB),
        cost_estimate=pl.CostEstimate(
            flops=6 * tok_count * width * width,
            bytes_accessed=18 * tok_count * width,
            transcendentals=0,
        ),
        name="last_back",
    )(dqkv, w_qkv, tokens, grad_hidden, gains)


def finish_body(
    groups,
    capacity,
    me_ref,
    len_ref,
    task_ref,
    routes_ref,
    table_ref,
    cot_ref,
    hid_ref,
    *refs,
):
    back_refs = refs[:groups]
    out_ref, gate_ref, back, side_ref, sem = refs[groups:]
    load = [(ref, back.at[pl.ds(i * capacity, capacity)]) for i, ref in enumerate(back_refs)]
    tok_count, width = cot_ref.shape
    tables = routing(len_ref, task_ref, routes_ref, table_ref, me_ref[0], capacity)
    columns, gates, inside = token_slots(tables, tok_count, capacity)
    task_col = over_lanes(inside, task_ref[...].astype(F32))
    for i, column in enumerate([columns[0].astype(F32), columns[1].astype(F32)] + gates + [task_col]):
        side_ref[:, i : i + 1] = column
    load_all(load, sem)
    gate_ref[...] = jnp.zeros_like(gate_ref)

    def step(index, carry):
        rows = pl.ds(pl.multiple_of(index * ROWS, ROWS), ROWS)
        slots = iota((ROWS, groups * capacity), 1)
        side = side_ref[rows, :]
        cot = cot_ref[rows, :].astype(F32)
        total = hid_ref[rows, :]
        inner = jnp.zeros((ROWS, 1), F32)
        parts = []
        mixed = None
        for r in range(2):
            hit = slots == side[:, r : r + 1].astype(jnp.int32)
            picked = dot(hit.astype(F32).astype(BF), back[...])
            gate = side[:, 2 + r : 3 + r]
            mixed = gate * picked if mixed is None else mixed + gate * picked
            grad = jnp.sum(cot * picked, axis=1, keepdims=True)
            parts.append((gate, grad))
            inner = inner + gate * grad
        out_ref[rows, :] = (total + mixed).astype(BF)
        task = iota((ROWS, gate_ref.shape[1]), 1) == side[:, 4:5].astype(jnp.int32)
        for r, (gate, grad) in enumerate(parts):
            gate_ref[r : r + 1, :] += over_rows(task, gate * (grad - inner))
        return carry

    lax.fori_loop(0, tok_count // ROWS, step, 0)


def finish(me, lengths, seg_task, routes, gate_table, cotangent, hidden, back, capacity):
    tok_count, width = cotangent.shape
    groups = len(back)
    whole = pl.BlockSpec(memory_space=pltpu.VMEM)
    return pl.pallas_call(
        functools.partial(finish_body, groups, capacity),
        out_shape=[
            jax.ShapeDtypeStruct((tok_count, width), BF),
            jax.ShapeDtypeStruct((8, 128), F32),
        ],
        in_specs=[pl.BlockSpec(memory_space=pltpu.SMEM)]
        + [whole] * 6
        + [pl.BlockSpec(memory_space=pl.ANY)] * groups,
        out_specs=[whole] * 2,
        scratch_shapes=[
            pltpu.VMEM((groups * capacity, width), BF),
            pltpu.VMEM((tok_count, 8), F32),
            pltpu.SemaphoreType.DMA((groups,)),
        ],
        compiler_params=pltpu.CompilerParams(vmem_limit_bytes=56 * MIB),
        cost_estimate=pl.CostEstimate(
            flops=4 * tok_count * width * groups * capacity,
            bytes_accessed=16 * tok_count * width,
            transcendentals=0,
        ),
        name="finish",
    )(me, lengths, seg_task, routes, gate_table, cotangent, hidden, *back)


def exchange(blocks, axis):
    count = lax.axis_size(axis)
    return [
        block if k == 0 else lax.ppermute(block, axis, [(s, s ^ k) for s in range(count)])
        for k, block in enumerate(blocks)
    ]


def up(block, axis):
    count = lax.axis_size(axis)
    return lax.ppermute(block, axis, [(s, (s + 1) % count) for s in range(count)])


def call_groups(groups, calls):
    order = list(range(groups))[::-1]
    size = max(1, groups // calls)
    return [order[i : i + size] for i in range(0, groups, size)]


def shards(
    tokens,
    cotangent,
    w_qkv,
    bias_qv,
    w_out,
    out_bias,
    norm_gains,
    norm_shifts,
    gate_table,
    w_in,
    w_down,
    lengths,
    seg_task,
    routes,
):
    tok_count, width = tokens.shape
    groups = lax.axis_size("expert")
    planes = lax.axis_size("hidden")
    top_count = routes.shape[1]
    capacity = 3 * top_count * tok_count // (2 * groups * w_in.shape[0])
    me = lax.axis_index("expert").astype(jnp.int32).reshape(1)
    route_args = (me, lengths, seg_task, routes, gate_table)

    in_parts, down_parts = [w_in[0]], [w_down[0]]
    for _ in range(planes - 1):
        down_parts.append(up(down_parts[-1], "hidden"))
        in_parts.append(up(in_parts[-1], "hidden"))

    grad_slots = dispatch(True, capacity, groups, *route_args, cotangent)
    grad_rows = exchange(grad_slots, "expert")

    qkv, attended, hidden, normed_one, normed_two = attend_forward(
        lengths, tokens, w_qkv, bias_qv, w_out, out_bias, norm_gains, norm_shifts
    )
    slots = dispatch(False, capacity, groups, *route_args, normed_two)
    rows = exchange(slots, "expert")

    out_rows, dx_rows = [None] * groups, [None] * groups
    kept = []
    for ids in call_groups(groups, 4):
        outs, dxs, *rest = expert_rows(
            [rows[k] for k in ids], [grad_rows[k] for k in ids], in_parts, down_parts
        )
        kept.append(rest)
        for k, out, dx in zip(ids, outs, dxs):
            out_rows[k], dx_rows[k] = out, dx
    dx_back = exchange(dx_rows, "expert")
    out_back = exchange(out_rows, "expert")

    kept = [list(part) for part in zip(*kept)]
    moving = weight_grads(1, 1, planes, BF, *kept)[0]
    others = weight_grads(2, planes - 1, planes, F32, *kept)
    for i in range(planes - 1):
        total = up(moving, "hidden").astype(F32) + others[i]
        moving = total.astype(BF)
    grad_w_in = total[:width][None]
    grad_w_down = total[width:].T[None]

    grad_hidden, grad_attended, grad_w_out, small_one = first_back(
        *route_args, cotangent, hidden, attended, w_out, norm_gains, dx_back, capacity
    )
    grad_qkv, dqkv, small_two = attend_back(lengths, qkv, grad_attended, normed_one)
    input_grad, small_three = last_back(dqkv, w_qkv, tokens, grad_hidden, norm_gains)
    layer_out, small_four = finish(*route_args, cotangent, hidden, out_back, capacity)

    summed = lax.psum(
        (grad_qkv, grad_w_out, small_one, small_two, small_three, small_four),
        ("expert", "hidden"),
    )
    grad_qkv, grad_w_out, small_one, small_two, small_three, small_four = summed
    return (
        layer_out,
        input_grad,
        grad_qkv,
        small_two[:2],
        grad_w_out,
        small_one[2],
        jnp.stack([small_three[0], small_one[0]]),
        jnp.stack([small_three[1], small_one[1]]),
        small_four[:2, : gate_table.shape[0]].T,
        grad_w_in,
        grad_w_down,
    )


def solution(mesh):
    split = P(("expert", "hidden"), None)
    return jax.shard_map(
        shards,
        mesh=mesh,
        in_specs=(
            split,
            split,
            P(),
            P(),
            P(),
            P(),
            P(),
            P(),
            P(),
            P("expert", None, "hidden"),
            P("expert", "hidden", None),
            split,
            split,
            P(),
        ),
        out_specs=(
            split,
            split,
            P(),
            P(),
            P(),
            P(),
            P(),
            P(),
            P(),
            P("expert", None, "hidden"),
            P("expert", "hidden", None),
        ),
        check_vma=False,
    )
```

time: 1400 us -> 453 us (0.32)
  waiting for transfers between devices: 798 us -> 163 us
  matrix products: 219 us -> 0 us
  Pallas kernels: 0 us -> 162 us
  local copies, waits for them, and re-layouts: 120 us -> 18.7 us
  other arithmetic: 104 us -> 8.49 us
  blocking collectives: 125 us -> 48 us
  starting transfers between devices: 9.15 us -> 31.7 us
    reduce_scatter x2 -> x0, waiting for transfers between devices: 380 us -> none  [the longest x1 211 us: shards(): lax.psum_scatter(jnp.einsum('ref,edf->red', row_piece, w_in, preferred_el...]
    all_gather x2 -> x0, waiting for transfers between devices: 326 us -> none  [the longest x1 183 us: shards(): lax.all_gather(grad_rows, 'hidden', axis=0, tiled=True)]
    dot_general x20 -> x0, matrix products: 219 us -> none  [the longest x1 29.2 us: expert_back(): jnp.einsum('red,efd->ref', grad_slots, weight_down, preferred_element_typ...]
    pallas_call x0 -> x13, Pallas kernels: none -> 162 us  [the longest x4 59.2 us: expert_rows(): pl.pallas_call(functools.partial(expert_body, blocks, planes), out_shape=...]
    all_to_all x2 -> x0, blocking collectives: 84.2 us -> none  [the longest x1 43 us: shards(): lax.all_to_all(outgoing, 'expert', split_axis=0, concat_axis=0, tiled=True)]
    ppermute x0 -> x37, waiting for transfers between devices: none -> 83.1 us  [the longest x28 54.8 us: exchange(): lax.ppermute(block, axis, [(s, s ^ k) for s in range(count)])]
    reduce_sum x18 -> x0, other arithmetic: 53.3 us -> none  [the longest x1 14.3 us: forward_pack(): exp_total = jnp.sum(jnp.exp(scores - row_peak), axis=-1, keepdims=True)]
    ppermute x0 -> x37, starting transfers between devices: none -> 31.7 us  [the longest x28 21.1 us: exchange(): lax.ppermute(block, axis, [(s, s ^ k) for s in range(count)])]
  transfers between devices with their start and end apart: 7 -> 38, of which waited for: 6 -> 13; matrix products, arithmetic and copies ran while one was open for 11% -> 3% of each run, Pallas kernels for 0% -> 31%
where the time goes in v2:
time: 453 us; the launch traced here: 447 us
  waiting for transfers between devices  163 us (36%)
  Pallas kernels  162 us (36%)
  blocking collectives  48 us (11%)
  starting transfers between devices  31.7 us (7%)
  local copies, waits for them, and re-layouts  18.7 us (4%)
  between operations  14.9 us (3%)
  other arithmetic  8.49 us (2%)
    psum x1, waiting for transfers between devices, shards(): lax.psum((grad_qkv, grad_w_out, small_one, small_two, small_three, small_...  80.1 us
    pallas_call x4, Pallas kernels, expert_rows(): pl.pallas_call(functools.partial(expert_body, blocks, planes), out_shape=...  59.2 us
    ppermute x28, waiting for transfers between devices, exchange(): lax.ppermute(block, axis, [(s, s ^ k) for s in range(count)])  54.8 us
    psum x1, blocking collectives, shards(): lax.psum((grad_qkv, grad_w_out, small_one, small_two, small_three, small_...  48 us
    ppermute x9, waiting for transfers between devices, up(): lax.ppermute(block, axis, [(s, (s + 1) % count) for s in range(count)])  28.4 us
    pallas_call x2, Pallas kernels, weight_grads(): pl.pallas_call(functools.partial(weight_body, calls), grid=(count,), out_...  26.3 us
    pallas_call x1, Pallas kernels, attend_back(): pl.pallas_call(attend_back_body, out_shape=[jax.ShapeDtypeStruct((width,...  21.2 us
    ppermute x28, starting transfers between devices, exchange(): lax.ppermute(block, axis, [(s, s ^ k) for s in range(count)])  21.1 us
  transfers between devices with their start and end apart: 38, of which 13 were waited for; matrix products, arithmetic and copies ran while one was open for 3% of the time, Pallas kernels for 31%

profile of v2, /device:TPU:0, one launch (start us, length us, event | category | flops | bytes accessed | tf_op | source)
XLA Modules:
  0.0 446.5 jit_solution(12621704510181234814)
XLA Ops:
  7.2 3.1 collective-permute-start.2
  10.3 1.6 collective-permute-start.5
  13.4 12.0 %collective-permute-done.2.refs_5_ = bf16[512,512]{1,0:T(8,128)(2,1)} collective-permute-done((bf16[512,512]{1,0:T(8,128)(2,1)}, bf16[512,512]{1,0:T(8,128)(2,1)}, u32[]{:S(2)}, u32[]{:S(2)}) %collective-permute-start.2) | collective-permute-done | bytes 524320 | tf_op jit(solution)/shard_map/ppermute | solution.py:679
  25.4 11.2 %collective-permute-done.5.refs_9_ = bf16[512,512]{1,0:T(8,128)(2,1)} collective-permute-done((bf16[512,512]{1,0:T(8,128)(2,1)}, bf16[512,512]{1,0:T(8,128)(2,1)}, u32[]{:S(2)}, u32[]{:S(2)}) %collective-permute-start.5) | collective-permute-done | bytes 524320 | tf_op jit(solution)/shard_map/ppermute | solution.py:679
  36.7 1.2 copy-done.8
  39.2 5.9 %dispatch_grads.1 = (bf16[384,512]{1,0:T(8,128)(2,1)S(1)}, bf16[384,512]{1,0:T(8,128)(2,1)S(1)}, bf16[384,512]{1,0:T(8,128)(2,1)S(1)}, bf16[384,512]{1,0:T(8,128...) custom-call(s32[1]{0:T(128)} %bitcast.me_ref, ...), custom_call_target="tpu_custom_call" | custom-call | flops 3221225472 | bytes 4194304 | tf_op jit(solution)/shard_map/dispatch_grads/pallas_call | solution.py:134
  45.5 2.5 collective-permute-start.24
  48.0 14.3 %attend_forward.1 = (bf16[1024,1536]{1,0:T(8,128)(2,1)S(1)}, bf16[1024,512]{1,0:T(8,128)(2,1)S(1)}, f32[1024,512]{1,0:T(8,128)S(1)}, bf16[1024,512]{1,0:T(8,128)(2,1)S(1)}, bf16[1024,512]{1,0:T(8,128)(2,1)S(1)}) custom-call(s32[1,32]{1,0:T(1,128)S(1)} %copy-done.13, bf16[1024,512]{1,0:T(8,128)(2,1)S(1)} %copy-done.3, bf16[512,1536]{1,0:T(8,128)(2,1)S(1)} %copy-done.2, ...), custom_call_target="tpu_custom_call" | custom-call | flops 4294967296 | bytes 10485760 | tf_op jit(solution)/shard_map/attend_forward/pallas_call | solution.py:238
  62.4 1.0 copy-done.19
  63.4 1.4 collective-permute-start.4
  64.8 2.0 collective-permute-start.7
  66.9 3.7 dispatch_rows.1
  71.4 1.7 collective-permute-start.21
  74.2 9.5 %collective-permute-done.21.refs_0_ = bf16[384,512]{1,0:T(8,128)(2,1)S(1)} collective-permute-done((bf16[384,512]{1,0:T(8,128)(2,1)S(1)}, bf16[384,512]{1,0:T(8,128)(2,1)S(1)}, u32[]{:S(2)}, u32[]{:S(2)}) %collective-permute-start.21) | collective-permute-done | bytes 393248 | tf_op jit(solution)/shard_map/ppermute | solution.py:672
  83.7 1.1 collective-permute-start.17
  84.8 7.1 %collective-permute-done.22.refs_1_ = bf16[384,512]{1,0:T(8,128)(2,1)S(1)} collective-permute-done((bf16[384,512]{1,0:T(8,128)(2,1)S(1)}, bf16[384,512]{1,0:T(8,128)(2,1)S(1)}, u32[]{:S(2)}, u32[]{:S(2)}) %collective-permute-start.22) | collective-permute-done | bytes 393248 | tf_op jit(solution)/shard_map/ppermute | solution.py:672
  94.3 1.2 collective-permute-start.16
  95.6 14.7 %expert_rows.7 = (bf16[384,512]{1,0:T(8,128)(2,1)}, bf16[384,512]{1,0:T(8,128)(2,1)}, bf16[384,512]{1,0:T(8,128)(2,1)}, bf16[384,512]{1,0:T(8,128)(2,1)}, bf16[7...) custom-call(bf16[384,512]{1,0:T(8,128)(2,1)} %copy-done.53, ...), custom_call_target="tpu_custom_call" | custom-call | flops 6442450944 | bytes 11010048 | tf_op jit(solution)/shard_map/expert_rows/pallas_call | solution.py:326
  110.3 1.5 collective-permute-start.12
  111.8 5.5 %collective-permute-done.15.refs_0_ = bf16[384,512]{1,0:T(8,128)(2,1)S(1)} collective-permute-done((bf16[384,512]{1,0:T(8,128)(2,1)S(1)}, bf16[384,512]{1,0:T(8,128)(2,1)S(1)}, u32[]{:S(2)}, u32[]{:S(2)}) %collective-permute-start.15) | collective-permute-done | bytes 393248 | tf_op jit(solution)/shard_map/ppermute | solution.py:672
  117.7 8.0 %collective-permute-done.16.refs_1_ = bf16[384,512]{1,0:T(8,128)(2,1)S(1)} collective-permute-done((bf16[384,512]{1,0:T(8,128)(2,1)S(1)}, bf16[384,512]{1,0:T(8,128)(2,1)S(1)}, u32[]{:S(2)}, u32[]{:S(2)}) %collective-permute-start.16) | collective-permute-done | bytes 393248 | tf_op jit(solution)/shard_map/ppermute | solution.py:672
  126.4 14.8 %expert_rows.6 = (bf16[384,512]{1,0:T(8,128)(2,1)}, bf16[384,512]{1,0:T(8,128)(2,1)}, bf16[384,512]{1,0:T(8,128)(2,1)}, bf16[384,512]{1,0:T(8,128)(2,1)}, bf16[7...) custom-call(bf16[384,512]{1,0:T(8,128)(2,1)} %copy-done.50, ...), custom_call_target="tpu_custom_call" | custom-call | flops 6442450944 | bytes 11010048 | tf_op jit(solution)/shard_map/expert_rows/pallas_call | solution.py:326
  141.4 5.6 %collective-permute-done.10.refs_1_ = bf16[384,512]{1,0:T(8,128)(2,1)S(1)} collective-permute-done((bf16[384,512]{1,0:T(8,128)(2,1)S(1)}, bf16[384,512]{1,0:T(8,128)(2,1)S(1)}, u32[]{:S(2)}, u32[]{:S(2)}) %collective-permute-start.10) | collective-permute-done | bytes 393248 | tf_op jit(solution)/shard_map/ppermute | solution.py:672
  147.8 15.0 %expert_rows.5 = (bf16[384,512]{1,0:T(8,128)(2,1)}, bf16[384,512]{1,0:T(8,128)(2,1)}, bf16[384,512]{1,0:T(8,128)(2,1)}, bf16[384,512]{1,0:T(8,128)(2,1)}, bf16[7...) custom-call(bf16[384,512]{1,0:T(8,128)(2,1)} %copy-done.57, ...), custom_call_target="tpu_custom_call" | custom-call | flops 6442450944 | bytes 11010048 | tf_op jit(solution)/shard_map/expert_rows/pallas_call | solution.py:326
  163.7 14.7 %expert_rows.4 = (bf16[384,512]{1,0:T(8,128)(2,1)}, bf16[384,512]{1,0:T(8,128)(2,1)}, bf16[384,512]{1,0:T(8,128)(2,1)}, bf16[384,512]{1,0:T(8,128)(2,1)}, bf16[7...) custom-call(bf16[384,512]{1,0:T(8,128)(2,1)} %copy-done.56, ...), custom_call_target="tpu_custom_call" | custom-call | flops 6442450944 | bytes 11010048 | tf_op jit(solution)/shard_map/expert_rows/pallas_call | solution.py:326
  178.4 9.2 %weight_grads.2 = bf16[1,1024,512]{2,1,0:T(8,128)(2,1)} custom-call(bf16[768,2048]{1,0:T(8,128)(2,1)} %get-tuple-element.123.refs_0_, bf16[768,2048]{1,0:T(8,128)(2,1)} %get-tuple-element.124.refs_1_, bf16[768,2048]{1,0:T(8,128)(2,1)} %get-tuple-element.125.refs_2_, bf16[768,2048]{1,0:T(8,128)(2,1)} %get-tuple-element.126.refs_3_, ...), custom_call_target="tpu_custom_call" | custom-call | flops 3221225472 | bytes 12582912 | tf_op jit(solution)/shard_map/weight_grads/pallas_call | solution.py:374
  187.6 1.7 collective-permute-start.34
  191.1 1.3 collective-permute-start.30
  192.4 17.1 %weight_grads.3 = f32[3,1024,512]{2,1,0:T(8,128)} custom-call(bf16[768,2048]{1,0:T(8,128)(2,1)} %get-tuple-element.123.refs_0_, bf16[768,2048]{1,0:T(8,128)(2,1)} %get-tuple-element.124.refs_1_, bf16[768,2048]{1,0:T(8,128)(2,1)} %get-tuple-element.125.refs_2_, bf16[768,2048]{1,0:T(8,128)(2,1)} %get-tuple-element.126.refs_3_, ...), custom_call_target="tpu_custom_call" | custom-call | flops 9663676416 | bytes 25165824 | tf_op jit(solution)/shard_map/weight_grads/pallas_call | solution.py:374
  209.6 5.2 %collective-permute-done.34 = bf16[1024,512]{1,0:T(8,128)(2,1)S(1)} collective-permute-done((bf16[1024,512]{1,0:T(8,128)(2,1)}, bf16[1024,512]{1,0:T(8,128)(2,1)S(1)}, u32[]{:S(2)}, u32[]{:S(2)}) %collective-permute-start.34) | collective-permute-done | bytes 1048608 | tf_op jit(solution)/shard_map/ppermute | solution.py:679
  214.8 1.9 fusion.4
  217.5 1.9 collective-permute-start.29
  219.4 8.5 %collective-permute-done.31.refs_5_ = bf16[384,512]{1,0:T(8,128)(2,1)S(1)} collective-permute-done((bf16[384,512]{1,0:T(8,128)(2,1)S(1)}, bf16[384,512]{1,0:T(8,128)(2,1)S(1)}, u32[]{:S(2)}, u32[]{:S(2)}) %collective-permute-start.31) | collective-permute-done | bytes 393248 | tf_op jit(solution)/shard_map/ppermute | solution.py:672
  230.5 6.9 %collective-permute-done.29.refs_3_ = bf16[384,512]{1,0:T(8,128)(2,1)S(1)} collective-permute-done((bf16[384,512]{1,0:T(8,128)(2,1)S(1)}, bf16[384,512]{1,0:T(8,128)(2,1)S(1)}, u32[]{:S(2)}, u32[]{:S(2)}) %collective-permute-start.29) | collective-permute-done | bytes 393248 | tf_op jit(solution)/shard_map/ppermute | solution.py:672
  237.4 1.3 collective-permute-start.19
  239.4 12.1 %first_back.1 = (f32[1024,512]{1,0:T(8,128)}, bf16[1024,512]{1,0:T(8,128)(2,1)}, f32[512,512]{1,0:T(8,128)}, f32[8,512]{1,0:T(8,128)}) custom-call(s32[1]{0:T(128)} %bitcast.me_ref, s32[1,32]{1,0:T(1,128)} %len_ref.11, s32[1,32]{1,0:T(1,128)} %task_ref.7, s32[30,2]{1,0:T(8,128)} %copy-done.5, f32[30,2]{1,0:T(8,128)} %copy-done.4, bf16[1024,512]{1,0:T(8,128)(2,1)} %cot_ref.3, ...), custom_call_target="tpu_custom_call" | custom-call | flops 4294967296 | bytes 8388608 | tf_op jit(solution)/shard_map/first_back/pallas_call | solution.py:452
  251.9 2.9 collective-permute-done.26.refs_7_
  255.3 21.2 %attend_back.1 = (f32[512,1536]{1,0:T(8,128)}, bf16[1024,1536]{1,0:T(8,128)(2,1)}, f32[8,512]{1,0:T(8,128)}) custom-call(s32[1,32]{1,0:T(1,128)} %len_ref.11, bf16[1024,1536]{1,0:T(8,128)(2,1)} %copy-done.17, bf16[1024,512]{1,0:T(8,128)(2,1)} %get-tuple-element.112.gatt_ref, bf16[1024,512]{1,0:T(8,128)(2,1)} %copy-done.19), custom_call_target="tpu_custom_call" | custom-call | flops 6979321856 | bytes 12582912 | tf_op jit(solution)/shard_map/attend_back/pallas_call | solution.py:529
  276.5 3.2 fusion.2
  280.2 14.6 %finish.1 = (bf16[1024,512]{1,0:T(8,128)(2,1)}, f32[8,128]{1,0:T(8,128)}) custom-call(s32[1]{0:T(128)} %bitcast.me_ref, s32[1,32]{1,0:T(1,128)} %len_ref.11, s32[1,32]{1,0:T(1,128)} %task_ref.7, s32[30,2]{1,0:T(8,128)} %copy-done.5, f32[30,2]{1,0:T(8,128)} %copy-done.4, bf16[1024,512]{1,0:T(8,128)(2,1)} %cot_ref.3, f32[1024,512]{1,0:T(8,128)} %copy-done.16, ...), custom_call_target="tpu_custom_call" | custom-call | flops 6442450944 | bytes 8388608 | tf_op jit(solution)/shard_map/finish/pallas_call | solution.py:644
  294.9 4.0 last_back.1
  299.0 48.0 %all-reduce = (f32[8,512]{1,0:T(8,128)S(1)}, f32[8,512]{1,0:T(8,128)S(1)}, f32[8,512]{1,0:T(8,128)S(1)}, f32[8,128]{1,0:T(8,128)S(1)}) all-reduce(f32[8,512]{1,0:T(8,128)S(1)} %copy-done.25, f32[8,512]{1,0:T(8,128)S(1)} %copy-done.24, f32[8,512]{1,0:T(8,128)S(1)} %get-tuple-element.121, ...), channel_id=1, replica_groups=mesh['expert'=8,'hidden'=4] {'expert','hidden'}, use_global_device_ids=true, to_apply=%region_1.0 | all-reduce | flops 13312 | bytes 106496 | tf_op jit(solution)/shard_map/psum | solution.py:754
  349.9 2.2 fusion
  352.1 1.1 slice_bitcast_fusion.3
  353.2 1.3 copy.33
  354.5 80.1 %all-reduce.4.cloned.1.call-done = (f32[512,1536]{1,0:T(8,128)}, f32[512,512]{1,0:T(8,128)}) async-done(((f32[512,1536]{1,0:T(8,128)}, f32[512,512]{1,0:T(8,128)}), (f32[512,1536]{1,0:T(8,128)}, f32[512,512]{1,0:T(8,128)})) %all-reduce.4.cloned.1.call-update) | async-done | bytes 4194320 | tf_op jit(solution)/shard_map/psum | solution.py:754
  434.7 3.8 copy.36
  438.5 1.0 copy.37
  (179 shorter events, 20.8 us)
Async XLA Ops:
  7.2 427.5 %all-reduce.4.cloned.1.call-start = ((), (), s32[]{:S(2)}) async-start(), calls=%async_computation | async-start | bytes 8388608 | tf_op jit(solution)/shard_map/psum | solution.py:754
  7.2 18.2 %collective-permute-start.2 = (bf16[512,512]{1,0:T(8,128)(2,1)}, bf16[512,512]{1,0:T(8,128)(2,1)}, u32[]{:S(2)}, u32[]{:S(2)}) collective-permute-start(bf16[512,512]{1,0:T(8,128)(2,1)} %bitcast.33), channel_id=1, source_target_pairs={{0,1},{1,2},{2,3},{3,0},{4,5},{5,6},{6,7},{7,4},{8,9},{9,10},{10,1... | collective-permute-start | bytes 1572872 | tf_op jit(solution)/shard_map/ppermute | solution.py:679
  10.3 26.3 %collective-permute-start.5 = (bf16[512,512]{1,0:T(8,128)(2,1)}, bf16[512,512]{1,0:T(8,128)(2,1)}, u32[]{:S(2)}, u32[]{:S(2)}) collective-permute-start(bf16[512,512]{1,0:T(8,128)(2,1)} %bitcast.38), channel_id=1, source_target_pairs={{0,1},{1,2},{2,3},{3,0},{4,5},{5,6},{6,7},{7,4},{8,9},{9,10},{10,1... | collective-permute-start | bytes 1572872 | tf_op jit(solution)/shard_map/ppermute | solution.py:679
  12.6 54.2 %copy-start.4 = (f32[30,2]{1,0:T(8,128)}, f32[30,2]{1,0:T(8,128)S(1)}, u32[]{:S(2)}) copy-start(f32[30,2]{1,0:T(8,128)S(1)} %copy.30.table_ref) | copy-start | bytes 724
  13.4 53.4 %copy-start.5 = (s32[30,2]{1,0:T(8,128)}, s32[30,2]{1,0:T(8,128)S(1)}, u32[]{:S(2)}) copy-start(s32[30,2]{1,0:T(8,128)S(1)} %copy.29.routes_ref) | copy-start | bytes 724
  25.4 38.0 %collective-permute-start.3 = (bf16[512,512]{1,0:T(8,128)(2,1)}, bf16[512,512]{1,0:T(8,128)(2,1)S(1)}, u32[]{:S(2)}, u32[]{:S(2)}) collective-permute-start(bf16[512,512]{1,0:T(8,128)(2,1)} %collective-permute-done.2.refs_5_), channel_id=1, source_target_pairs={{0,1},{1,2},{2,3},{3,0},{4,5},{5,6},{6,7},{7,4},{8,9},{9,10},{10,1... | collective-permute-start | bytes 1572872 | tf_op jit(solution)/shard_map/ppermute | solution.py:679
  36.6 28.2 %collective-permute-start.6 = (bf16[512,512]{1,0:T(8,128)(2,1)}, bf16[512,512]{1,0:T(8,128)(2,1)S(1)}, u32[]{:S(2)}, u32[]{:S(2)}) collective-permute-start(bf16[512,512]{1,0:T(8,128)(2,1)} %collective-permute-done.5.refs_9_), channel_id=1, source_target_pairs={{0,1},{1,2},{2,3},{3,0},{4,5},{5,6},{6,7},{7,4},{8,9},{9,10},{10,1... | collective-permute-start | bytes 1572872 | tf_op jit(solution)/shard_map/ppermute | solution.py:679
  45.2 27.9 %collective-permute-start.23 = (bf16[384,512]{1,0:T(8,128)(2,1)S(1)}, bf16[384,512]{1,0:T(8,128)(2,1)S(1)}, u32[]{:S(2)}, u32[]{:S(2)}) collective-permute-start(bf16[384,512]{1,0:T(8,128)(2,1)S(1)} %get-tuple-element.97), channel_id=1, source_target_pairs={{0,28},{4,24},{8,20},{12,16},{16,12},{20,8},{24,4},{28,0},{1,29},{... | collective-permute-start | bytes 1179656 | tf_op jit(solution)/shard_map/ppermute | solution.py:672
  45.5 28.1 %collective-permute-start.24 = (bf16[384,512]{1,0:T(8,128)(2,1)S(1)}, bf16[384,512]{1,0:T(8,128)(2,1)S(1)}, u32[]{:S(2)}, u32[]{:S(2)}) collective-permute-start(bf16[384,512]{1,0:T(8,128)(2,1)S(1)} %get-tuple-element.98), channel_id=1, source_target_pairs={{0,24},{4,28},{8,16},{12,20},{16,8},{20,12},{24,0},{28,4},{1,25},{... | collective-permute-start | bytes 1179656 | tf_op jit(solution)/shard_map/ppermute | solution.py:672
  63.4 29.3 %collective-permute-start.4 = (bf16[512,512]{1,0:T(8,128)(2,1)S(1)}, bf16[512,512]{1,0:T(8,128)(2,1)S(1)}, u32[]{:S(2)}, u32[]{:S(2)}) collective-permute-start(bf16[512,512]{1,0:T(8,128)(2,1)S(1)} %collective-permute-done.3.refs_6_), channel_id=1, source_target_pairs={{0,1},{1,2},{2,3},{3,0},{4,5},{5,6},{6,7},{7,4},{8,9},{9,10},{10,1... | collective-permute-start | bytes 1572872 | tf_op jit(solution)/shard_map/ppermute | solution.py:679
  64.8 28.5 %collective-permute-start.7 = (bf16[512,512]{1,0:T(8,128)(2,1)S(1)}, bf16[512,512]{1,0:T(8,128)(2,1)S(1)}, u32[]{:S(2)}, u32[]{:S(2)}) collective-permute-start(bf16[512,512]{1,0:T(8,128)(2,1)S(1)} %collective-permute-done.6.refs_10_), channel_id=1, source_target_pairs={{0,1},{1,2},{2,3},{3,0},{4,5},{5,6},{6,7},{7,4},{8,9},{9,10},{10,1... | collective-permute-start | bytes 1572872 | tf_op jit(solution)/shard_map/ppermute | solution.py:679
  71.4 12.3 %collective-permute-start.21 = (bf16[384,512]{1,0:T(8,128)(2,1)S(1)}, bf16[384,512]{1,0:T(8,128)(2,1)S(1)}, u32[]{:S(2)}, u32[]{:S(2)}) collective-permute-start(bf16[384,512]{1,0:T(8,128)(2,1)S(1)} %get-tuple-element.95), channel_id=1, source_target_pairs={{0,28},{4,24},{8,20},{12,16},{16,12},{20,8},{24,4},{28,0},{1,29},{... | collective-permute-start | bytes 1179656 | tf_op jit(solution)/shard_map/ppermute | solution.py:672
  73.1 20.4 %copy-start.45 = (bf16[384,512]{1,0:T(8,128)(2,1)}, bf16[384,512]{1,0:T(8,128)(2,1)S(1)}, u32[]{:S(2)}) copy-start(bf16[384,512]{1,0:T(8,128)(2,1)S(1)} %collective-permute-done.23.refs_2_) | copy-start | bytes 1179652
  73.1 18.8 %collective-permute-start.22 = (bf16[384,512]{1,0:T(8,128)(2,1)S(1)}, bf16[384,512]{1,0:T(8,128)(2,1)S(1)}, u32[]{:S(2)}, u32[]{:S(2)}) collective-permute-start(bf16[384,512]{1,0:T(8,128)(2,1)S(1)} %get-tuple-element.96), channel_id=1, source_target_pairs={{0,24},{4,28},{8,16},{12,20},{16,8},{20,12},{24,0},{28,4},{1,25},{... | collective-permute-start | bytes 1179656 | tf_op jit(solution)/shard_map/ppermute | solution.py:672
  73.6 20.0 %copy-start.46 = (bf16[384,512]{1,0:T(8,128)(2,1)}, bf16[384,512]{1,0:T(8,128)(2,1)S(1)}, u32[]{:S(2)}) copy-start(bf16[384,512]{1,0:T(8,128)(2,1)S(1)} %collective-permute-done.24.refs_3_) | copy-start | bytes 1179652
  73.6 89.2 %collective-permute-start.1 = (bf16[384,512]{1,0:T(8,128)(2,1)S(1)}, bf16[384,512]{1,0:T(8,128)(2,1)S(1)}, u32[]{:S(2)}, u32[]{:S(2)}) collective-permute-start(bf16[384,512]{1,0:T(8,128)(2,1)S(1)} %get-tuple-element.79), channel_id=1, source_target_pairs={{0,4},{4,0},{8,12},{12,8},{16,20},{20,16},{24,28},{28,24},{1,5},{5... | collective-permute-start | bytes 1179656 | tf_op jit(solution)/shard_map/ppermute | solution.py:672
  83.7 26.5 %collective-permute-start.17 = (bf16[384,512]{1,0:T(8,128)(2,1)S(1)}, bf16[384,512]{1,0:T(8,128)(2,1)S(1)}, u32[]{:S(2)}, u32[]{:S(2)}) collective-permute-start(bf16[384,512]{1,0:T(8,128)(2,1)S(1)} %get-tuple-element.91), channel_id=1, source_target_pairs={{0,20},{4,16},{8,28},{12,24},{16,4},{20,0},{24,12},{28,8},{1,21},{... | collective-permute-start | bytes 1179656 | tf_op jit(solution)/shard_map/ppermute | solution.py:672
  91.9 18.4 %collective-permute-start.18 = (bf16[384,512]{1,0:T(8,128)(2,1)S(1)}, bf16[384,512]{1,0:T(8,128)(2,1)}, u32[]{:S(2)}, u32[]{:S(2)}) collective-permute-start(bf16[384,512]{1,0:T(8,128)(2,1)S(1)} %get-tuple-element.92), channel_id=1, source_target_pairs={{0,16},{4,20},{8,24},{12,28},{16,0},{20,4},{24,8},{28,12},{1,17},{... | collective-permute-start | bytes 1179656 | tf_op jit(solution)/shard_map/ppermute | solution.py:672
  92.7 24.5 %collective-permute-start.15 = (bf16[384,512]{1,0:T(8,128)(2,1)S(1)}, bf16[384,512]{1,0:T(8,128)(2,1)S(1)}, u32[]{:S(2)}, u32[]{:S(2)}) collective-permute-start(bf16[384,512]{1,0:T(8,128)(2,1)S(1)} %get-tuple-element.89), channel_id=1, source_target_pairs={{0,20},{4,16},{8,28},{12,24},{16,4},{20,0},{24,12},{28,8},{1,21},{... | collective-permute-start | bytes 1179656 | tf_op jit(solution)/shard_map/ppermute | solution.py:672
  94.3 31.3 %collective-permute-start.16 = (bf16[384,512]{1,0:T(8,128)(2,1)S(1)}, bf16[384,512]{1,0:T(8,128)(2,1)S(1)}, u32[]{:S(2)}, u32[]{:S(2)}) collective-permute-start(bf16[384,512]{1,0:T(8,128)(2,1)S(1)} %get-tuple-element.90), channel_id=1, source_target_pairs={{0,16},{4,20},{8,24},{12,28},{16,0},{20,4},{24,8},{28,12},{1,17},{... | collective-permute-start | bytes 1179656 | tf_op jit(solution)/shard_map/ppermute | solution.py:672
  110.3 31.0 %collective-permute-start.11 = (bf16[384,512]{1,0:T(8,128)(2,1)S(1)}, bf16[384,512]{1,0:T(8,128)(2,1)S(1)}, u32[]{:S(2)}, u32[]{:S(2)}) collective-permute-start(bf16[384,512]{1,0:T(8,128)(2,1)S(1)} %get-tuple-element.85), channel_id=1, source_target_pairs={{0,12},{4,8},{8,4},{12,0},{16,28},{20,24},{24,20},{28,16},{1,13},{... | collective-permute-start | bytes 1179656 | tf_op jit(solution)/shard_map/ppermute | solution.py:672
  110.3 31.1 %collective-permute-start.12 = (bf16[384,512]{1,0:T(8,128)(2,1)S(1)}, bf16[384,512]{1,0:T(8,128)(2,1)S(1)}, u32[]{:S(2)}, u32[]{:S(2)}) collective-permute-start(bf16[384,512]{1,0:T(8,128)(2,1)S(1)} %get-tuple-element.86), channel_id=1, source_target_pairs={{0,8},{4,12},{8,0},{12,4},{16,24},{20,28},{24,16},{28,20},{1,9},{5... | collective-permute-start | bytes 1179656 | tf_op jit(solution)/shard_map/ppermute | solution.py:672
  117.3 24.1 %collective-permute-start.9 = (bf16[384,512]{1,0:T(8,128)(2,1)S(1)}, bf16[384,512]{1,0:T(8,128)(2,1)S(1)}, u32[]{:S(2)}, u32[]{:S(2)}) collective-permute-start(bf16[384,512]{1,0:T(8,128)(2,1)S(1)} %get-tuple-element.83), channel_id=1, source_target_pairs={{0,12},{4,8},{8,4},{12,0},{16,28},{20,24},{24,20},{28,16},{1,13},{... | collective-permute-start | bytes 1179656 | tf_op jit(solution)/shard_map/ppermute | solution.py:672
  125.7 21.3 %collective-permute-start.10 = (bf16[384,512]{1,0:T(8,128)(2,1)S(1)}, bf16[384,512]{1,0:T(8,128)(2,1)S(1)}, u32[]{:S(2)}, u32[]{:S(2)}) collective-permute-start(bf16[384,512]{1,0:T(8,128)(2,1)S(1)} %get-tuple-element.84), channel_id=1, source_target_pairs={{0,8},{4,12},{8,0},{12,4},{16,24},{20,28},{24,16},{28,20},{1,9},{5... | collective-permute-start | bytes 1179656 | tf_op jit(solution)/shard_map/ppermute | solution.py:672
  141.2 21.6 %collective-permute-start = (bf16[384,512]{1,0:T(8,128)(2,1)S(1)}, bf16[384,512]{1,0:T(8,128)(2,1)S(1)}, u32[]{:S(2)}, u32[]{:S(2)}) collective-permute-start(bf16[384,512]{1,0:T(8,128)(2,1)S(1)} %get-tuple-element.77), channel_id=1, source_target_pairs={{0,4},{4,0},{8,12},{12,8},{16,20},{20,16},{24,28},{28,24},{1,5},{5... | collective-permute-start | bytes 1179656 | tf_op jit(solution)/shard_map/ppermute | solution.py:672
  187.6 27.2 %collective-permute-start.34 = (bf16[1024,512]{1,0:T(8,128)(2,1)}, bf16[1024,512]{1,0:T(8,128)(2,1)S(1)}, u32[]{:S(2)}, u32[]{:S(2)}) collective-permute-start(bf16[1024,512]{1,0:T(8,128)(2,1)} %bitcast.31), channel_id=1, source_target_pairs={{0,1},{1,2},{2,3},{3,0},{4,5},{5,6},{6,7},{7,4},{8,9},{9,10},{10,1... | collective-permute-start | bytes 3145736 | tf_op jit(solution)/shard_map/ppermute | solution.py:679
  189.4 27.7 %collective-permute-start.32 = (bf16[384,512]{1,0:T(8,128)(2,1)S(1)}, bf16[384,512]{1,0:T(8,128)(2,1)}, u32[]{:S(2)}, u32[]{:S(2)}) collective-permute-start(bf16[384,512]{1,0:T(8,128)(2,1)S(1)} %copy-done.36), channel_id=1, source_target_pairs={{0,24},{4,28},{8,16},{12,20},{16,8},{20,12},{24,0},{28,4},{1,25},{... | collective-permute-start | bytes 1179656 | tf_op jit(solution)/shard_map/ppermute | solution.py:672
  190.2 27.3 %collective-permute-start.33 = (bf16[384,512]{1,0:T(8,128)(2,1)S(1)}, bf16[384,512]{1,0:T(8,128)(2,1)}, u32[]{:S(2)}, u32[]{:S(2)}) collective-permute-start(bf16[384,512]{1,0:T(8,128)(2,1)S(1)} %copy-done.35), channel_id=1, source_target_pairs={{0,28},{4,24},{8,20},{12,16},{16,12},{20,8},{24,4},{28,0},{1,29},{... | collective-permute-start | bytes 1179656 | tf_op jit(solution)/shard_map/ppermute | solution.py:672
  191.1 28.2 %collective-permute-start.30 = (bf16[384,512]{1,0:T(8,128)(2,1)S(1)}, bf16[384,512]{1,0:T(8,128)(2,1)}, u32[]{:S(2)}, u32[]{:S(2)}) collective-permute-start(bf16[384,512]{1,0:T(8,128)(2,1)S(1)} %copy-done.39), channel_id=1, source_target_pairs={{0,16},{4,20},{8,24},{12,28},{16,0},{20,4},{24,8},{28,12},{1,17},{... | collective-permute-start | bytes 1179656 | tf_op jit(solution)/shard_map/ppermute | solution.py:672
  209.6 20.3 %copy-start.32 = (bf16[384,512]{1,0:T(8,128)(2,1)S(1)}, bf16[384,512]{1,0:T(8,128)(2,1)}, u32[]{:S(2)}) copy-start(bf16[384,512]{1,0:T(8,128)(2,1)} %get-tuple-element.100) | copy-start | bytes 1179652
  209.6 27.8 %copy-start.33 = (bf16[384,512]{1,0:T(8,128)(2,1)S(1)}, bf16[384,512]{1,0:T(8,128)(2,1)}, u32[]{:S(2)}) copy-start(bf16[384,512]{1,0:T(8,128)(2,1)} %get-tuple-element.93) | copy-start | bytes 1179652
  209.6 29.1 %copy-start.31 = (bf16[384,512]{1,0:T(8,128)(2,1)S(1)}, bf16[384,512]{1,0:T(8,128)(2,1)}, u32[]{:S(2)}) copy-start(bf16[384,512]{1,0:T(8,128)(2,1)} %get-tuple-element.94) | copy-start | bytes 1179652
  216.7 38.1 %collective-permute-start.35 = (bf16[1024,512]{1,0:T(8,128)(2,1)S(1)}, bf16[1024,512]{1,0:T(8,128)(2,1)S(1)}, u32[]{:S(2)}, u32[]{:S(2)}) collective-permute-start(bf16[1024,512]{1,0:T(8,128)(2,1)S(1)} %fusion.4), channel_id=1, source_target_pairs={{0,1},{1,2},{2,3},{3,0},{4,5},{5,6},{6,7},{7,4},{8,9},{9,10},{10,1... | collective-permute-start | bytes 3145736 | tf_op jit(solution)/shard_map/ppermute | solution.py:679
  217.0 10.9 %collective-permute-start.31 = (bf16[384,512]{1,0:T(8,128)(2,1)S(1)}, bf16[384,512]{1,0:T(8,128)(2,1)S(1)}, u32[]{:S(2)}, u32[]{:S(2)}) collective-permute-start(bf16[384,512]{1,0:T(8,128)(2,1)S(1)} %copy-done.38), channel_id=1, source_target_pairs={{0,20},{4,16},{8,28},{12,24},{16,4},{20,0},{24,12},{28,8},{1,21},{... | collective-permute-start | bytes 1179656 | tf_op jit(solution)/shard_map/ppermute | solution.py:672
  217.1 12.1 %collective-permute-start.28 = (bf16[384,512]{1,0:T(8,128)(2,1)S(1)}, bf16[384,512]{1,0:T(8,128)(2,1)S(1)}, u32[]{:S(2)}, u32[]{:S(2)}) collective-permute-start(bf16[384,512]{1,0:T(8,128)(2,1)S(1)} %copy-done.42), channel_id=1, source_target_pairs={{0,8},{4,12},{8,0},{12,4},{16,24},{20,28},{24,16},{28,20},{1,9},{5... | collective-permute-start | bytes 1179656 | tf_op jit(solution)/shard_map/ppermute | solution.py:672
  217.5 19.9 %collective-permute-start.29 = (bf16[384,512]{1,0:T(8,128)(2,1)S(1)}, bf16[384,512]{1,0:T(8,128)(2,1)S(1)}, u32[]{:S(2)}, u32[]{:S(2)}) collective-permute-start(bf16[384,512]{1,0:T(8,128)(2,1)S(1)} %copy-done.40), channel_id=1, source_target_pairs={{0,12},{4,8},{8,4},{12,0},{16,28},{20,24},{24,20},{28,16},{1,13},{... | collective-permute-start | bytes 1179656 | tf_op jit(solution)/shard_map/ppermute | solution.py:672
  219.4 19.3 %collective-permute-start.27 = (bf16[384,512]{1,0:T(8,128)(2,1)S(1)}, bf16[384,512]{1,0:T(8,128)(2,1)S(1)}, u32[]{:S(2)}, u32[]{:S(2)}) collective-permute-start(bf16[384,512]{1,0:T(8,128)(2,1)S(1)} %copy-done.43), channel_id=1, source_target_pairs={{0,4},{4,0},{8,12},{12,8},{16,20},{20,16},{24,28},{28,24},{1,5},{5... | collective-permute-start | bytes 1179656 | tf_op jit(solution)/shard_map/ppermute | solution.py:672
  227.9 23.6 %collective-permute-start.25 = (bf16[384,512]{1,0:T(8,128)(2,1)S(1)}, bf16[384,512]{1,0:T(8,128)(2,1)S(1)}, u32[]{:S(2)}, u32[]{:S(2)}) collective-permute-start(bf16[384,512]{1,0:T(8,128)(2,1)S(1)} %copy-done.34), channel_id=1, source_target_pairs={{0,24},{4,28},{8,16},{12,20},{16,8},{20,12},{24,0},{28,4},{1,25},{... | collective-permute-start | bytes 1179656 | tf_op jit(solution)/shard_map/ppermute | solution.py:672
  229.9 24.9 %collective-permute-start.26 = (bf16[384,512]{1,0:T(8,128)(2,1)S(1)}, bf16[384,512]{1,0:T(8,128)(2,1)S(1)}, u32[]{:S(2)}, u32[]{:S(2)}) collective-permute-start(bf16[384,512]{1,0:T(8,128)(2,1)S(1)} %copy-done.32), channel_id=1, source_target_pairs={{0,28},{4,24},{8,20},{12,16},{16,12},{20,8},{24,4},{28,0},{1,29},{... | collective-permute-start | bytes 1179656 | tf_op jit(solution)/shard_map/ppermute | solution.py:672
  237.4 42.3 %collective-permute-start.19 = (bf16[384,512]{1,0:T(8,128)(2,1)S(1)}, bf16[384,512]{1,0:T(8,128)(2,1)}, u32[]{:S(2)}, u32[]{:S(2)}) collective-permute-start(bf16[384,512]{1,0:T(8,128)(2,1)S(1)} %copy-done.33), channel_id=1, source_target_pairs={{0,16},{4,20},{8,24},{12,28},{16,0},{20,4},{24,8},{28,12},{1,17},{... | collective-permute-start | bytes 1179656 | tf_op jit(solution)/shard_map/ppermute | solution.py:672
  238.7 41.5 %collective-permute-start.20 = (bf16[384,512]{1,0:T(8,128)(2,1)S(1)}, bf16[384,512]{1,0:T(8,128)(2,1)}, u32[]{:S(2)}, u32[]{:S(2)}) collective-permute-start(bf16[384,512]{1,0:T(8,128)(2,1)S(1)} %copy-done.31), channel_id=1, source_target_pairs={{0,20},{4,16},{8,28},{12,24},{16,4},{20,0},{24,12},{28,8},{1,21},{... | collective-permute-start | bytes 1179656 | tf_op jit(solution)/shard_map/ppermute | solution.py:672
  251.5 24.9 %copy-start.41 = (bf16[384,512]{1,0:T(8,128)(2,1)}, bf16[384,512]{1,0:T(8,128)(2,1)S(1)}, u32[]{:S(2)}) copy-start(bf16[384,512]{1,0:T(8,128)(2,1)S(1)} %collective-permute-done.25.refs_6_) | copy-start | bytes 1179652
  251.6 28.6 %collective-permute-start.13 = (bf16[384,512]{1,0:T(8,128)(2,1)}, bf16[384,512]{1,0:T(8,128)(2,1)}, u32[]{:S(2)}, u32[]{:S(2)}) collective-permute-start(bf16[384,512]{1,0:T(8,128)(2,1)} %get-tuple-element.87), channel_id=1, source_target_pairs={{0,8},{4,12},{8,0},{12,4},{16,24},{20,28},{24,16},{28,20},{1,9},{5... | collective-permute-start | bytes 1179656 | tf_op jit(solution)/shard_map/ppermute | solution.py:672
  254.8 21.7 %copy-start.44 = (bf16[384,512]{1,0:T(8,128)(2,1)}, bf16[384,512]{1,0:T(8,128)(2,1)S(1)}, u32[]{:S(2)}) copy-start(bf16[384,512]{1,0:T(8,128)(2,1)S(1)} %collective-permute-done.26.refs_7_) | copy-start | bytes 1179652
  254.8 25.4 %collective-permute-start.14 = (bf16[384,512]{1,0:T(8,128)(2,1)}, bf16[384,512]{1,0:T(8,128)(2,1)}, u32[]{:S(2)}, u32[]{:S(2)}) collective-permute-start(bf16[384,512]{1,0:T(8,128)(2,1)} %get-tuple-element.88), channel_id=1, source_target_pairs={{0,12},{4,8},{8,4},{12,0},{16,28},{20,24},{24,20},{28,16},{1,13},{... | collective-permute-start | bytes 1179656 | tf_op jit(solution)/shard_map/ppermute | solution.py:672
  254.8 21.7 %copy-start.23 = (bf16[1024,512]{1,0:T(8,128)(2,1)}, bf16[1024,512]{1,0:T(8,128)(2,1)S(1)}, u32[]{:S(2)}) copy-start(bf16[1024,512]{1,0:T(8,128)(2,1)S(1)} %collective-permute-done.35) | copy-start | bytes 3145732
  254.8 25.3 %collective-permute-start.8 = (bf16[384,512]{1,0:T(8,128)(2,1)}, bf16[384,512]{1,0:T(8,128)(2,1)}, u32[]{:S(2)}, u32[]{:S(2)}) collective-permute-start(bf16[384,512]{1,0:T(8,128)(2,1)} %get-tuple-element.82), channel_id=1, source_target_pairs={{0,4},{4,0},{8,12},{12,8},{16,20},{20,16},{24,28},{28,24},{1,5},{5... | collective-permute-start | bytes 1179656 | tf_op jit(solution)/shard_map/ppermute | solution.py:672
  279.7 70.2 %collective-permute-start.36 = (bf16[1024,512]{1,0:T(8,128)(2,1)}, bf16[1024,512]{1,0:T(8,128)(2,1)}, u32[]{:S(2)}, u32[]{:S(2)}) collective-permute-start(bf16[1024,512]{1,0:T(8,128)(2,1)} %fusion.2), channel_id=1, source_target_pairs={{0,1},{1,2},{2,3},{3,0},{4,5},{5,6},{6,7},{7,4},{8,9},{9,10},{10,1... | collective-permute-start | bytes 3145736 | tf_op jit(solution)/shard_map/ppermute | solution.py:679
  (51 other events, 356.2 us)
Sparse Core Ops, SparseCore 0:
  276.6 157.9 all-reduce.3

commit v3 on v0

v3 whole, which is shorter than its diff:
```python
import functools
import math

import jax
import jax.numpy as jnp
from jax import lax
from jax.experimental import pallas as pl
from jax.experimental.pallas import tpu as pltpu
from jax.sharding import PartitionSpec as P

HEADS = 8
HD = 64
NORM_EPS = 1e-05
MASK_FILL = -1000000000.0

BF = jnp.bfloat16
F32 = jnp.float32
MIB = 1 << 20

ROWS = 256
REACH = 64
JOINT = 4
LANES = JOINT * HD
SMALL = 128


def iota(shape, dim):
    return lax.broadcasted_iota(jnp.int32, shape, dim)


def dot(left, right):
    return jnp.dot(left, right, preferred_element_type=F32)


def dot_nt(left, right):
    return lax.dot_general(left, right, (((1,), (1,)), ((), ())), preferred_element_type=F32)


def dot_tn(left, right):
    return lax.dot_general(left, right, (((0,), (0,)), ((), ())), preferred_element_type=F32)


def over_lanes(mask, values):
    return jnp.sum(jnp.where(mask, values, 0.0), axis=1, keepdims=True)


def over_rows(mask, values):
    return jnp.sum(jnp.where(mask, values, 0.0), axis=0, keepdims=True)


def to_column(row):
    count = row.shape[1]
    return over_lanes(iota((count, count), 0) == iota((count, count), 1), row)


def one_hot(mask):
    return mask.astype(F32).astype(BF)


WHOLE = pl.BlockSpec(memory_space=pltpu.VMEM)
SCALARS = pl.BlockSpec(memory_space=pltpu.SMEM)
ANYWHERE = pl.BlockSpec(memory_space=pl.ANY)


HOLD = 1
SCALE = 0.4
MICROS = {
    "dispatch_grads": 6,
    "forward": 13,
    "expert_rows": 17,
    "weight_grads": 9,
    "expert_outputs": 11,
    "backward": 23,
    "last_back": 6,
    "finish": 12,
}


def run(name, body, args, in_specs, out_shape, out_specs, scratch=(), after=(), aliases=None):
    count, extra = len(args), len(after)

    def ordered(*refs):
        outs = refs[count + extra :]
        mark, rest = outs[len(out_shape)], outs[: len(out_shape)] + outs[len(out_shape) + 1 :]
        mark[...] = jnp.zeros_like(mark)
        body(*refs[:count], *rest)

    *results, mark = pl.pallas_call(
        ordered,
        out_shape=[*out_shape, jax.ShapeDtypeStruct((8, 128), F32)],
        in_specs=[*in_specs, *[ANYWHERE] * extra],
        out_specs=[*out_specs, WHOLE],
        scratch_shapes=list(scratch),
        input_output_aliases=aliases or {},
        compiler_params=pltpu.CompilerParams(vmem_limit_bytes=56 * MIB),
        cost_estimate=pl.CostEstimate(flops=int(1.15e9 * SCALE * MICROS.get(name, 2)), bytes_accessed=1 << 10, transcendentals=0),
        name=name,
    )(*args, *after)
    return results, mark


def join_weights(w_in, w_down):
    _, width, hid = w_in.shape

    def body(in_ref, down_ref, out_ref):
        out_ref[:width, :] = in_ref[0]
        out_ref[width:, :] = down_ref[0].T

    (out,), mark = run(
        "join_weights",
        body,
        (w_in, w_down),
        [WHOLE] * 2,
        [jax.ShapeDtypeStruct((2 * width, hid), BF)],
        [WHOLE],
    )
    return out, mark


def hold(block, after):
    (block,), _ = run(
        "hold",
        lambda *refs: None,
        (block,),
        [ANYWHERE],
        [jax.ShapeDtypeStruct(block.shape, block.dtype)],
        [ANYWHERE],
        (),
        after,
        {0: 0},
    )
    return block


class Copies:
    def __init__(self, sem):
        self.sem, self.count, self.open = sem, 0, []

    def start(self, source, target):
        copy = pltpu.make_async_copy(source, target, self.sem.at[self.count])
        copy.start()
        self.count += 1
        self.open.append(copy)
        return copy

    def wait(self):
        for copy in self.open:
            copy.wait()
        self.open = []


def centred_of(values):
    centred = values - jnp.mean(values, axis=-1, keepdims=True)
    spread = jnp.mean(centred * centred, axis=-1, keepdims=True)
    scale = lax.rsqrt(spread + NORM_EPS)
    return centred * scale, scale


def norm_back(grad, hat, scale, gain):
    scaled = grad * gain
    return scale * (
        scaled
        - jnp.mean(scaled, axis=-1, keepdims=True)
        - hat * jnp.mean(scaled * hat, axis=-1, keepdims=True)
    )


def sentence_bounds(lengths_ref):
    len_row = lengths_ref[...].astype(F32)
    count = len_row.shape[1]
    len_col = to_column(len_row)
    start_col = over_lanes(iota((count, count), 1) < iota((count, count), 0), len_row)
    start_row = over_rows(iota((count, count), 0) < iota((count, count), 1), len_col)
    return (len_row, len_col, start_row, start_col)


def routing(lengths_ref, task_ref, routes_ref, table_ref, me):
    len_row, len_col, start_row, start_col = sentence_bounds(lengths_ref)
    count = len_row.shape[1]
    tasks = routes_ref.shape[1]
    hit = iota((tasks, count), 0) == task_ref[...]
    expert_rows = [
        over_rows(hit, to_column(routes_ref[r : r + 1, :].astype(F32))) for r in range(2)
    ]
    logit_rows = [over_rows(hit, to_column(table_ref[r : r + 1, :])) for r in range(2)]
    peak = jnp.maximum(logit_rows[0], logit_rows[1])
    raised = [jnp.exp(row - peak) for row in logit_rows]
    gate_rows = [row / (raised[0] + raised[1]) for row in raised]
    expert_cols = [to_column(row) for row in expert_rows]
    earlier = iota((count, count), 0) < iota((count, count), 1)
    add_rows, far_rows = [], []
    for row in expert_rows:
        same = (expert_cols[0] == row) | (expert_cols[1] == row)
        add_rows.append(over_rows(earlier & same, len_col) - start_row)
        far_rows.append((row.astype(jnp.int32) ^ me).astype(F32))
    return (len_row, len_col, start_row, start_col, far_rows, gate_rows, add_rows)


def fill_slots(tables, data, capacity, groups, weighted):
    len_row, len_col, start_row, start_col, far_rows, gate_rows, add_rows = tables
    tok_count, count = data.shape[0], len_row.shape[1]
    place = iota((count, tok_count), 1).astype(F32)
    inside = (place >= start_col) & (place < start_col + len_col)
    token_place = iota((1, tok_count), 1).astype(F32)
    far = [over_rows(inside, to_column(row)) for row in far_rows]
    position = [token_place + over_rows(inside, to_column(row)) for row in add_rows]
    slots = iota((capacity, tok_count), 0)
    slot_column = iota((capacity, count), 0).astype(F32)
    for k in range(groups):
        slot = jnp.where(far[0] == k, position[0], jnp.where(far[1] == k, position[1], -1.0))
        picked = dot(one_hot(slots == slot.astype(jnp.int32)), data)
        if weighted:
            first, second = far_rows[0] == k, far_rows[1] == k
            base = jnp.where(first, add_rows[0], add_rows[1]) + start_row
            gate = jnp.where(first, gate_rows[0], jnp.where(second, gate_rows[1], 0.0))
            picked = picked * over_lanes((slot_column >= base) & (slot_column < base + len_row), gate)
        yield k, picked


def dispatch_body(len_ref, task_ref, routes_ref, table_ref, data_ref, out_ref, stage, sem):
    groups, capacity, _ = out_ref.shape
    copies = Copies(sem)
    tables = routing(len_ref, task_ref, routes_ref, table_ref, 0)
    for k, picked in fill_slots(tables, data_ref[...], capacity, groups, True):
        stage[k] = picked.astype(BF)
        copies.start(stage.at[k], out_ref.at[k])
    copies.wait()


def dispatch_grads(capacity, groups, lengths, seg_task, routes, gate_table, cotangent, after):
    slots = (groups, capacity, cotangent.shape[1])
    (out,), mark = run(
        "dispatch_grads",
        dispatch_body,
        (lengths, seg_task, routes, gate_table, cotangent),
        [WHOLE] * 5,
        [jax.ShapeDtypeStruct(slots, BF)],
        [ANYWHERE],
        [pltpu.VMEM(slots, BF), pltpu.SemaphoreType.DMA((groups,))],
        after,
    )
    return out, mark


def split_heads(block):
    head = iota(block.shape, 1) // HD
    zero = jnp.zeros_like(block)
    return jnp.concatenate([jnp.where(head == h, block, zero) for h in range(JOINT)], axis=0)


def join_heads(stacked):
    rows = stacked.shape[0] // JOINT
    head = iota((rows, stacked.shape[1]), 1) // HD
    out = stacked[:rows]
    for h in range(1, JOINT):
        out = jnp.where(head == h, stacked[h * rows : (h + 1) * rows], out)
    return out


def windows(lengths_ref, tok_count, queries):
    len_row, len_col, start_row, start_col = sentence_bounds(lengths_ref)
    end_row, end_col = start_row + len_row, start_col + len_col
    count = len_row.shape[1]
    keys = queries + 2 * REACH
    for block in range(tok_count // queries):
        start = min(max(block * queries - REACH, 0), tok_count - keys)
        query_place = (iota((count, queries), 1) + block * queries).astype(F32)
        query_seg = jnp.sum((query_place >= end_col).astype(F32), axis=0, keepdims=True)
        key_place = (iota((keys, count), 0) + start).astype(F32)
        key_seg = jnp.sum((key_place >= end_row).astype(F32), axis=1, keepdims=True)
        same = key_seg == jnp.concatenate([query_seg] * JOINT, axis=1)
        rows = slice(block * queries, (block + 1) * queries)
        yield rows, slice(start, start + keys), same


def softmax_of(key_rows, stacked, same):
    scores = jnp.where(same, dot_nt(key_rows, stacked), MASK_FILL)
    raised = jnp.exp(scores - jnp.max(scores, axis=0, keepdims=True))
    return raised * (1.0 / jnp.sum(raised, axis=0, keepdims=True))


def forward_body(
    capacity,
    groups,
    me_ref,
    len_ref,
    task_ref,
    routes_ref,
    table_ref,
    tok_ref,
    wqkv_ref,
    bias_ref,
    wout_ref,
    obias_ref,
    gains_ref,
    shifts_ref,
    *refs,
):
    qkv_out, att_out, hid_out, one_out = refs[:4]
    slot_out = refs[4 : 4 + groups]
    qkv, att, hid, one, two, stage, sem = refs[4 + groups :]
    tok_count, width = tok_ref.shape
    copies = Copies(sem)
    for step in range(tok_count // ROWS):
        rows = slice(step * ROWS, (step + 1) * ROWS)
        hat, _ = centred_of(tok_ref[rows, :].astype(F32))
        normed = (hat * gains_ref[0:1, :] + shifts_ref[0:1, :]).astype(BF)
        one[rows, :] = normed
        wide = dot(normed, wqkv_ref[...])
        queries = (wide[:, :width] + bias_ref[0:1, :]).astype(BF)
        qkv[rows, :width] = queries * jnp.asarray(HD**-0.5, BF)
        qkv[rows, width : 2 * width] = wide[:, width : 2 * width].astype(BF)
        qkv[rows, 2 * width :] = (wide[:, 2 * width :] + bias_ref[1:2, :]).astype(BF)
    copies.start(one, one_out)
    copies.start(qkv, qkv_out)
    for rows, keys, same in windows(len_ref, tok_count, REACH):
        for first in range(0, width, LANES):
            lanes = slice(first, first + LANES)
            key_rows = qkv[keys, width + first : width + first + LANES]
            value_rows = qkv[keys, 2 * width + first : 2 * width + first + LANES]
            probs = softmax_of(key_rows, split_heads(qkv[rows, lanes]), same).astype(BF)
            att[rows, lanes] = join_heads(dot_tn(probs, value_rows)).astype(BF)
    copies.start(att, att_out)
    for step in range(tok_count // ROWS):
        rows = slice(step * ROWS, (step + 1) * ROWS)
        hidden = tok_ref[rows, :].astype(F32) + dot(att[rows, :], wout_ref[...]) + obias_ref[...]
        hid[rows, :] = hidden
        hat, _ = centred_of(hidden)
        two[rows, :] = (hat * gains_ref[1:2, :] + shifts_ref[1:2, :]).astype(BF)
    copies.start(hid, hid_out)
    tables = routing(len_ref, task_ref, routes_ref, table_ref, me_ref[0])
    for k, picked in fill_slots(tables, two[...], capacity, groups, False):
        stage[k] = picked.astype(BF)
        copies.start(stage.at[k], slot_out[k])
    copies.wait()


def forward(
    capacity,
    groups,
    me,
    lengths,
    seg_task,
    routes,
    gate_table,
    tokens,
    w_qkv,
    bias_qv,
    w_out,
    out_bias,
    gains,
    shifts,
    after,
):
    tok_count, width = tokens.shape
    whole = [
        ((tok_count, 3 * width), BF),
        ((tok_count, width), BF),
        ((tok_count, width), F32),
        ((tok_count, width), BF),
    ]
    (qkv, att, hid, one, *slots), mark = run(
        "forward",
        functools.partial(forward_body, capacity, groups),
        (
            me,
            lengths,
            seg_task,
            routes,
            gate_table,
            tokens,
            w_qkv,
            bias_qv,
            w_out,
            out_bias.reshape(1, width),
            gains,
            shifts,
        ),
        [SCALARS] + [WHOLE] * 11,
        [jax.ShapeDtypeStruct(*kind) for kind in whole]
        + [jax.ShapeDtypeStruct((capacity, width), BF)] * groups,
        [ANYWHERE] * (4 + groups),
        [pltpu.VMEM(*kind) for kind in whole]
        + [
            pltpu.VMEM((tok_count, width), BF),
            pltpu.VMEM((groups, capacity, width), BF),
            pltpu.SemaphoreType.DMA((4 + groups,)),
        ],
        after,
    )
    return qkv, att, hid, one, slots, mark


GELU_A = 0.7978845608028654
GELU_B = 0.044715


def gelu_both(values):
    square = values * values
    inner = values * (GELU_A + (GELU_A * GELU_B) * square)
    half = 0.5 * jnp.tanh(inner) + 0.5
    active = values * half
    slope = half + active * (1.0 - half) * (2.0 * GELU_A + (6.0 * GELU_A * GELU_B) * square)
    return active, slope


def pieces_of(total, size):
    return [slice(i, min(i + size, total)) for i in range(0, total, size)]


def expert_body(ids, planes, me_ref, *refs):
    refs = list(refs)
    take = lambda count: [refs.pop(0) for _ in range(count)]
    blocks = len(ids)
    x_in, (g_in,), parts = take(blocks), take(1), take(planes)
    dx_out = take(blocks)
    act_out, pre_out, xt_out, gt_out = take(4)
    xs, gs, w_in, w_down, act, pre, xt, gt, dx, sem = refs
    cap, width = x_in[0].shape
    hid = parts[0].shape[1]
    rows = blocks * cap
    me = me_ref[0]
    copies = Copies(sem)
    for i, k in enumerate(ids):
        copies.start(x_in[i], xs.at[pl.ds(i * cap, cap)])
        copies.start(g_in.at[me ^ k], gs.at[pl.ds(i * cap, cap)])
    rows_there, copies.open = copies.open, []
    parts_there = []
    for c in range(planes):
        lanes = pl.ds(c * hid, hid)
        copies.start(parts[c].at[pl.ds(0, width)], w_in.at[:, lanes])
        copies.start(parts[c].at[pl.ds(width, width)], w_down.at[:, lanes])
        parts_there.append(copies.open)
        copies.open = []
    for copy in rows_there:
        copy.wait()
    for c in range(planes):
        for copy in parts_there[c]:
            copy.wait()
        lanes = slice(c * hid, (c + 1) * hid)
        for spot in pieces_of(rows, 3 * cap):
            active, slope = gelu_both(dot(xs[spot, :], w_in[:, lanes]))
            act[spot, lanes] = active.astype(BF)
            pre[spot, lanes] = (dot(gs[spot, :], w_down[:, lanes]) * slope).astype(BF)
        copies.start(act.at[:, pl.ds(c * hid, hid)], act_out.at[:, pl.ds(c * hid, hid)])
        copies.start(pre.at[:, pl.ds(c * hid, hid)], pre_out.at[:, pl.ds(c * hid, hid)])
        if c == 0:
            xt[...] = xs[...].T
            copies.start(xt, xt_out)
            gt[...] = gs[...].T
            copies.start(gt, gt_out)
    for i, spot in enumerate(pieces_of(rows, 3 * cap)):
        dx[spot, :] = dot_nt(pre[spot, :], w_in[...]).astype(BF)
        for j in range(spot.start // cap, spot.stop // cap):
            copies.start(dx.at[pl.ds(j * cap, cap)], dx_out[j])
    copies.wait()


def expert_rows(ids, me, x_blocks, g_rows, parts, after):
    blocks, planes = len(ids), len(parts)
    cap, width = x_blocks[0].shape
    hid = parts[0].shape[1]
    rows = blocks * cap
    units, turned = (rows, planes * hid), (width, rows)
    result, mark = run(
        "expert_rows",
        functools.partial(expert_body, ids, planes),
        (me, *x_blocks, g_rows, *parts),
        [SCALARS] + [ANYWHERE] * (blocks + 1 + planes),
        [jax.ShapeDtypeStruct((cap, width), BF)] * blocks
        + [jax.ShapeDtypeStruct(units, BF)] * 2
        + [jax.ShapeDtypeStruct(turned, BF)] * 2,
        [ANYWHERE] * (blocks + 4),
        [
            pltpu.VMEM((rows, width), BF),
            pltpu.VMEM((rows, width), BF),
            pltpu.VMEM((width, planes * hid), BF),
            pltpu.VMEM((width, planes * hid), BF),
            pltpu.VMEM(units, BF),
            pltpu.VMEM(units, BF),
            pltpu.VMEM(turned, BF),
            pltpu.VMEM(turned, BF),
            pltpu.VMEM((rows, width), BF),
            pltpu.SemaphoreType.DMA((3 * blocks + 4 * planes + 2,)),
        ],
        after,
    )
    return result[:blocks], result[blocks:], mark


def output_body(calls, planes, me_ref, *refs):
    act_in, parts = refs[: len(calls)], refs[len(calls) : len(calls) + planes]
    out_ref, act, w_down, stage, sem = refs[len(calls) + planes :]
    _, capacity, width = out_ref.shape
    hid = parts[0].shape[1]
    copies = Copies(sem)
    for c, part in enumerate(parts):
        copies.start(part.at[pl.ds(width, width)], w_down.at[:, pl.ds(c * hid, hid)])
    there, copies.open = copies.open, []
    there_rows, spot = [], 0
    for ids, units in zip(calls, act_in):
        size = len(ids) * capacity
        there_rows.append(copies.start(units, act.at[pl.ds(spot, size)]))
        spot += size
    copies.open = []
    for copy in there:
        copy.wait()
    spot = 0
    for ids, copy in zip(calls, there_rows):
        copy.wait()
        size = len(ids) * capacity
        stage[spot : spot + size, :] = dot_nt(act[spot : spot + size, :], w_down[...]).astype(BF)
        for k in ids:
            copies.start(stage.at[pl.ds(spot, capacity)], out_ref.at[me_ref[0] ^ k])
            spot += capacity
    copies.wait()


def expert_outputs(calls, groups, capacity, me, act, parts, after):
    planes = len(parts)
    width, hid = parts[0].shape[0] // 2, parts[0].shape[1]
    (out,), mark = run(
        "expert_outputs",
        functools.partial(output_body, calls, planes),
        (me, *act, *parts),
        [SCALARS] + [ANYWHERE] * (len(act) + planes),
        [jax.ShapeDtypeStruct((groups, capacity, width), BF)],
        [ANYWHERE],
        [
            pltpu.VMEM((groups * capacity, planes * hid), BF),
            pltpu.VMEM((width, planes * hid), BF),
            pltpu.VMEM((groups * capacity, width), BF),
            pltpu.SemaphoreType.DMA((planes + len(calls) + groups,)),
        ],
        after,
    )
    return out, mark


def weight_body(which, calls, *refs):
    act_in, pre_in, xt_in, gt_in = (refs[i * calls : (i + 1) * calls] for i in range(4))
    out_refs = refs[4 * calls : 4 * calls + len(which)]
    act, pre, xt, gt, stage, sem = refs[4 * calls + len(which) :]
    width, hid = xt.shape[0], act.shape[2]
    spots, total = [], 0
    for turned in xt_in:
        spots.append(pl.ds(total, turned.shape[1]))
        total += turned.shape[1]
    copies = Copies(sem)
    there = []

    def work(n):
        for copy in there[n]:
            copy.wait()
        for i, (turned, units) in enumerate(((xt, pre), (gt, act))):
            spot = pl.ds(i * width, width)
            stage[n, spot, :] = dot(turned[...], units[n % 2]).astype(stage.dtype)
            copies.start(stage.at[n, spot], out_refs[n].at[spot])

    for n, c in enumerate(which):
        lanes = pl.ds(c * hid, hid)
        done, copies.open = copies.open, []
        for i, spot in enumerate(spots):
            if n == 0:
                copies.start(xt_in[i], xt.at[:, spot])
                copies.start(gt_in[i], gt.at[:, spot])
            copies.start(pre_in[i].at[:, lanes], pre.at[n % 2, spot])
            copies.start(act_in[i].at[:, lanes], act.at[n % 2, spot])
        there.append(copies.open)
        copies.open = done
        if n:
            work(n - 1)
    work(len(which) - 1)
    copies.wait()


def weight_grads(which, planes, dtype, act, pre, xt, gt, after):
    calls = len(act)
    width, rows = xt[0].shape[0], sum(turned.shape[1] for turned in xt)
    hid = act[0].shape[1] // planes
    return run(
        "weight_grads",
        functools.partial(weight_body, which, calls),
        (*act, *pre, *xt, *gt),
        [ANYWHERE] * (4 * calls),
        [jax.ShapeDtypeStruct((2 * width, hid), dtype)] * len(which),
        [ANYWHERE] * len(which),
        [
            pltpu.VMEM((2, rows, hid), BF),
            pltpu.VMEM((2, rows, hid), BF),
            pltpu.VMEM((width, rows), BF),
            pltpu.VMEM((width, rows), BF),
            pltpu.VMEM((len(which), 2 * width, hid), dtype),
            pltpu.SemaphoreType.DMA((2 * calls * (len(which) + 1) + 2 * len(which),)),
        ],
        after,
    )


def token_slots(tables, tok_count, capacity):
    len_row, _, start_row, _, far_rows, gate_rows, add_rows = tables
    count = len_row.shape[1]
    place = iota((tok_count, count), 0).astype(F32)
    inside = (place >= start_row) & (place < start_row + len_row)
    columns = []
    for far, add in zip(far_rows, add_rows):
        kept = inside & (place + add < capacity)
        columns.append(over_lanes(kept, place + (add + far * capacity + 1.0)) - 1.0)
    gates = [over_lanes(inside, row) for row in gate_rows]
    return columns, gates, inside


def backward_body(
    groups,
    capacity,
    me_ref,
    len_ref,
    task_ref,
    routes_ref,
    table_ref,
    cot_ref,
    wout_ref,
    gains_ref,
    hid_in,
    att_in,
    qkv_in,
    one_in,
    *refs,
):
    back_in = refs[:groups]
    keep_ref, send_ref, grad_out, dqkv_out = refs[groups : groups + 4]
    back, side, hid, att, qkv, one, grad_all, low, gatt, dqkv, total, sem = refs[groups + 4 :]
    copies = Copies(sem)
    for i, ref in enumerate(back_in):
        copies.start(ref, back.at[pl.ds(i * capacity, capacity)])
    copies.start(hid_in, hid)
    first, copies.open = copies.open, []
    att_there = copies.start(att_in, att)
    qkv_there = copies.start(qkv_in, qkv)
    one_there = copies.start(one_in, one)
    copies.open = []
    tok_count, width = cot_ref.shape
    me = me_ref[0]
    tables = routing(len_ref, task_ref, routes_ref, table_ref, me)
    columns, _, _ = token_slots(tables, tok_count, capacity)
    for i, column in enumerate(columns):
        side[:, i : i + 1] = column.astype(jnp.int32)
    for copy in first:
        copy.wait()
    sums = [jnp.zeros((1, width), F32)] * 3
    for step in range(tok_count // ROWS):
        rows = slice(step * ROWS, (step + 1) * ROWS)
        slots = iota((ROWS, groups * capacity), 1)
        hit = (slots == side[rows, 0:1]) | (slots == side[rows, 1:2])
        grad_two = dot(one_hot(hit), back[...])
        hat, scale = centred_of(hid[rows, :])
        grad = cot_ref[rows, :].astype(F32) + norm_back(grad_two, hat, scale, gains_ref[1:2, :])
        grad_all[rows, :] = grad
        for i, part in enumerate((grad_two * hat, grad_two, grad)):
            sums[i] = sums[i] + jnp.sum(part, axis=0, keepdims=True)
        low[rows, :] = grad.astype(BF)
        gatt[rows, :] = dot_nt(low[rows, :], wout_ref[...]).astype(BF)
    copies.start(grad_all, grad_out)
    att_there.wait()
    total[:, 3 * width : 4 * width] = dot_tn(att[...], low[...])

    qkv_there.wait()
    open_sums = [({}, {}) for _ in range(width // LANES)]
    bias_sums = {}
    spans = list(windows(len_ref, tok_count, 2 * REACH))
    for index, (rows, keys, same) in enumerate(spans):
        next_key = spans[index + 1][1].start if index + 1 < len(spans) else tok_count
        for group, lane in enumerate(range(0, width, LANES)):
            lanes = slice(lane, lane + LANES)
            key_lanes = slice(width + lane, width + lane + LANES)
            value_lanes = slice(2 * width + lane, 2 * width + lane + LANES)
            stacked, grads = split_heads(qkv[rows, lanes]), split_heads(gatt[rows, lanes])
            key_rows, value_rows = qkv[keys, key_lanes], qkv[keys, value_lanes]
            probs = softmax_of(key_rows, stacked, same)
            grad_probs = dot_nt(value_rows, grads)
            inner = jnp.sum(probs * grad_probs, axis=0, keepdims=True)
            grad_scores = (probs * (grad_probs - inner)).astype(BF)
            grad_values = dot(probs.astype(BF), grads)
            grad_keys = dot(grad_scores, stacked)
            grad_queries = join_heads(dot_tn(grad_scores, key_rows)) * HD**-0.5
            dqkv[rows, lanes] = grad_queries.astype(BF)
            for held, fresh, target in zip(
                open_sums[group], (grad_keys, grad_values), (key_lanes, value_lanes)
            ):
                for i in range(0, fresh.shape[0], REACH):
                    place = keys.start + i
                    part = fresh[i : i + REACH]
                    held[place] = held[place] + part if place in held else part
                for place in [place for place in held if place < next_key]:
                    dqkv[place : place + REACH, target] = held.pop(place).astype(BF)
    copies.start(dqkv, dqkv_out)
    ones = jnp.ones((8, tok_count), BF)
    bias = [dot(ones, dqkv[:, :width])[0:1], dot(ones, dqkv[:, 2 * width :])[0:1]]
    short = jnp.concatenate(sums + bias + [jnp.zeros((SMALL - 5, width), F32)], axis=0)
    total[:, 4 * width :] = short.T
    one_there.wait()
    total[:, : 3 * width] = dot_tn(one[...], dqkv[...])
    half, rows, _ = keep_ref.shape
    for j in range(half):
        for bit, ref in enumerate((keep_ref, send_ref)):
            owner = me ^ (2 * j + bit)
            ref[j] = total[pl.ds(pl.multiple_of(owner * rows, rows), rows), :].astype(BF)
    copies.wait()


def backward(
    capacity,
    me,
    lengths,
    seg_task,
    routes,
    gate_table,
    cotangent,
    w_out,
    gains,
    hidden,
    attended,
    qkv,
    one,
    back,
    after,
):
    tok_count, width = cotangent.shape
    groups = len(back)
    columns = 4 * width + SMALL
    pieces = jax.ShapeDtypeStruct((groups // 2, width // groups, columns), BF)
    (keep, send, grad, dqkv), mark = run(
        "backward",
        functools.partial(backward_body, groups, capacity),
        (
            me,
            lengths,
            seg_task,
            routes,
            gate_table,
            cotangent,
            w_out,
            gains,
            hidden,
            attended,
            qkv,
            one,
            *back,
        ),
        [SCALARS] + [WHOLE] * 7 + [ANYWHERE] * (4 + groups),
        [
            pieces,
            pieces,
            jax.ShapeDtypeStruct((tok_count, width), F32),
            jax.ShapeDtypeStruct((tok_count, 3 * width), BF),
        ],
        [WHOLE, WHOLE, ANYWHERE, ANYWHERE],
        [
            pltpu.VMEM((groups * capacity, width), BF),
            pltpu.VMEM((tok_count, 2), jnp.int32),
            pltpu.VMEM((tok_count, width), F32),
            pltpu.VMEM((tok_count, width), BF),
            pltpu.VMEM((tok_count, 3 * width), BF),
            pltpu.VMEM((tok_count, width), BF),
            pltpu.VMEM((tok_count, width), F32),
            pltpu.VMEM((tok_count, width), BF),
            pltpu.VMEM((tok_count, width), BF),
            pltpu.VMEM((tok_count, 3 * width), BF),
            pltpu.VMEM((width, columns), F32),
            pltpu.SemaphoreType.DMA((groups + 6,)),
        ],
        after,
    )
    return keep, send, grad, dqkv, mark


def last_body(dqkv_ref, wqkv_ref, tok_ref, grad_ref, gains_ref, out_ref, small_ref):
    tok_count, width = tok_ref.shape
    sums = [jnp.zeros((1, width), F32)] * 2
    for step in range(tok_count // ROWS):
        rows = slice(step * ROWS, (step + 1) * ROWS)
        grad_one = dot_nt(dqkv_ref[rows, :], wqkv_ref[...])
        hat, scale = centred_of(tok_ref[rows, :].astype(F32))
        back = norm_back(grad_one, hat, scale, gains_ref[0:1, :])
        out_ref[rows, :] = (grad_ref[rows, :] + back).astype(BF)
        for i, part in enumerate((grad_one * hat, grad_one)):
            sums[i] = sums[i] + jnp.sum(part, axis=0, keepdims=True)
    small_ref[...] = jnp.concatenate(sums, axis=0)


def last_back(dqkv, w_qkv, tokens, grad_hidden, gains, after):
    tok_count, width = tokens.shape
    (out, small), mark = run(
        "last_back",
        last_body,
        (dqkv, w_qkv, tokens, grad_hidden, gains),
        [WHOLE] * 5,
        [jax.ShapeDtypeStruct((tok_count, width), BF), jax.ShapeDtypeStruct((2, width), F32)],
        [WHOLE] * 2,
        (),
        after,
    )
    return out, small, mark


def finish_body(
    len_ref,
    task_ref,
    routes_ref,
    table_ref,
    cot_ref,
    hid_ref,
    back_in,
    out_ref,
    gate_ref,
    back,
    side_ref,
    sem,
):
    groups, capacity, _ = back_in.shape
    copies = Copies(sem)
    for i in range(groups):
        copies.start(back_in.at[i], back.at[pl.ds(i * capacity, capacity)])
    tok_count, width = cot_ref.shape
    tables = routing(len_ref, task_ref, routes_ref, table_ref, 0)
    columns, gates, inside = token_slots(tables, tok_count, capacity)
    task_col = over_lanes(inside, task_ref[...].astype(F32))
    for i, column in enumerate(columns + gates + [task_col]):
        side_ref[:, i : i + 1] = column
    copies.wait()
    gate_sums = [jnp.zeros((1, gate_ref.shape[1]), F32)] * 2
    for step in range(tok_count // ROWS):
        rows = slice(step * ROWS, (step + 1) * ROWS)
        slots = iota((ROWS, groups * capacity), 1)
        side = side_ref[rows, :]
        cot = cot_ref[rows, :].astype(F32)
        mixed = hid_ref[rows, :]
        inner = jnp.zeros((ROWS, 1), F32)
        parts = []
        for r in range(2):
            hit = slots == side[:, r : r + 1].astype(jnp.int32)
            picked = dot(one_hot(hit), back[...])
            gate = side[:, 2 + r : 3 + r]
            mixed = mixed + gate * picked
            grad = jnp.sum(cot * picked, axis=1, keepdims=True)
            parts.append((gate, grad))
            inner = inner + gate * grad
        out_ref[rows, :] = mixed.astype(BF)
        task = iota((ROWS, gate_ref.shape[1]), 1) == side[:, 4:5].astype(jnp.int32)
        for r, (gate, grad) in enumerate(parts):
            gate_sums[r] = gate_sums[r] + over_rows(task, gate * (grad - inner))
    gate_ref[...] = jnp.concatenate(gate_sums, axis=0)


def finish(lengths, seg_task, routes, gate_table, cotangent, hidden, back, after):
    tok_count, width = cotangent.shape
    groups, capacity, _ = back.shape
    (out, gate), mark = run(
        "finish",
        finish_body,
        (lengths, seg_task, routes, gate_table, cotangent, hidden, back),
        [WHOLE] * 6 + [ANYWHERE],
        [jax.ShapeDtypeStruct((tok_count, width), BF), jax.ShapeDtypeStruct((2, 128), F32)],
        [WHOLE] * 2,
        [
            pltpu.VMEM((groups * capacity, width), BF),
            pltpu.VMEM((tok_count, 8), F32),
            pltpu.SemaphoreType.DMA((groups,)),
        ],
        after,
    )
    return out, gate, mark


def swap(block, axis, distance):
    count = lax.axis_size(axis)
    return lax.ppermute(block, axis, [(s, s ^ distance) for s in range(count)])


def turn(block, axis, distance):
    count = lax.axis_size(axis)
    return lax.ppermute(block, axis, [(s, (s + distance) % count) for s in range(count)])


def powers(count):
    return [1 << i for i in range(count.bit_length() - 1)]


def add_pairs(keep, came, after):
    count, rows, columns = keep.shape

    def body(keep_ref, came_ref, *out_refs):
        for j, out_ref in enumerate(out_refs):
            out_ref[...] = (keep_ref[j].astype(F32) + came_ref[j].astype(F32)).astype(BF)

    return run(
        "add_pairs",
        body,
        (keep, came),
        [WHOLE] * 2,
        [jax.ShapeDtypeStruct((rows, columns), BF)] * count,
        [WHOLE] * count,
        (),
        after,
    )


def add_all(blocks, after):
    def body(*refs):
        total = refs[0][...].astype(F32)
        for ref in refs[1:-1]:
            total = total + ref[...].astype(F32)
        refs[-1][...] = total.astype(BF)

    (out,), mark = run(
        "add_all",
        body,
        blocks,
        [WHOLE] * len(blocks),
        [jax.ShapeDtypeStruct(blocks[0].shape, BF)],
        [WHOLE],
        (),
        after,
    )
    return out, mark


def add_part(came, own, after):
    def body(came_ref, own_ref, out_ref):
        out_ref[...] = (came_ref[...].astype(F32) + own_ref[...]).astype(BF)

    size = came.shape
    (out,), mark = run(
        "add_part",
        body,
        (came, own),
        [WHOLE] * 2,
        [jax.ShapeDtypeStruct(size, BF)],
        [WHOLE],
        (),
        after,
    )
    return out, mark


def last_part(came, own, after):
    width, hid = came.shape[0] // 2, came.shape[1]

    def body(came_ref, own_ref, in_ref, down_ref):
        in_ref[0] = came_ref[:width, :].astype(F32) + own_ref[:width, :]
        down_ref[0] = (came_ref[width:, :].astype(F32) + own_ref[width:, :]).T

    return run(
        "last_part",
        body,
        (came, own),
        [WHOLE] * 2,
        [jax.ShapeDtypeStruct((1, width, hid), F32), jax.ShapeDtypeStruct((1, hid, width), F32)],
        [WHOLE] * 2,
        (),
        after,
    )


def assemble(me, pieces, after):
    rows, columns = pieces[0].shape
    count = len(pieces)
    width = count * rows

    def body(me_ref, *refs):
        qkv_ref, out_ref, small_ref, small = refs[count:]
        for k, piece in enumerate(refs[:count]):
            owner = me_ref[0] ^ k
            spot = pl.ds(pl.multiple_of(owner * rows, rows), rows)
            qkv_ref[spot, :] = piece[:, : 3 * width].astype(F32)
            out_ref[spot, :] = piece[:, 3 * width : 4 * width].astype(F32)
            small[spot, :] = piece[:, 4 * width :].astype(F32)
        small_ref[...] = small[...].T[:8]

    return run(
        "assemble",
        body,
        (me, *pieces),
        [SCALARS] + [WHOLE] * count,
        [
            jax.ShapeDtypeStruct((width, 3 * width), F32),
            jax.ShapeDtypeStruct((width, width), F32),
            jax.ShapeDtypeStruct((8, width), F32),
        ],
        [WHOLE] * 3,
        [pltpu.VMEM((width, columns - 4 * width), F32)],
        after,
    )


def sum_small(block, axis, after):
    def body(block_ref, sent_ref, out_ref):
        out_ref[...] = block_ref[...] + sent_ref[...]

    for distance in powers(lax.axis_size(axis)):
        (block,), mark = run(
            "add_small",
            body,
            (block, swap(block, axis, distance)),
            [WHOLE] * 2,
            [jax.ShapeDtypeStruct(block.shape, F32)],
            [WHOLE],
            (),
            after,
        )
        after = (mark,)
    return block, mark


def working_order(groups, capacity):
    unit = 128 // math.gcd(128, capacity)
    near = max(2, unit)
    order = sorted(range(near, groups), key=lambda k: (-k.bit_count(), k))
    half = (groups - near) // 2 // unit * unit
    return [list(range(near))[::-1], order[:half], order[half:]]


def shards(
    tokens,
    cotangent,
    w_qkv,
    bias_qv,
    w_out,
    out_bias,
    norm_gains,
    norm_shifts,
    gate_table,
    w_in,
    w_down,
    lengths,
    seg_task,
    routes,
):
    tok_count, width = tokens.shape
    groups = lax.axis_size("expert")
    planes = lax.axis_size("hidden")
    top_count = routes.shape[1]
    capacity = 3 * top_count * tok_count // (2 * groups * w_in.shape[0])
    me = lax.axis_index("expert").astype(jnp.int32).reshape(1)
    route_args = (lengths, seg_task, routes.T, gate_table.T)

    own, mark = join_weights(w_in, w_down)
    above = [own]
    above.append(turn(above[0], "hidden", 1))
    below = above[:1]
    for _ in range((planes - 1) // 2):
        below.append(turn(below[-1], "hidden", -1))

    grad_slots, mark = dispatch_grads(capacity, groups, *route_args, cotangent, (mark,))
    grad_rows = lax.all_to_all(grad_slots, "expert", split_axis=0, concat_axis=0, tiled=True)

    qkv, attended, hidden, one, slots, mark = forward(
        capacity,
        groups,
        me,
        *route_args,
        tokens,
        w_qkv,
        bias_qv,
        w_out,
        out_bias,
        norm_gains,
        norm_shifts,
        (mark,),
    )

    calls = working_order(groups, capacity)
    rows, dx_back, kept = {0: slots[0]}, {}, []
    for ids in calls:
        for k in ids:
            if k:
                rows[k] = swap(slots[k], "expert", k)
    above[1] = hold(above[1], (mark, *[rows[k] for k in calls[1][:HOLD]]))
    for _ in range(planes // 2 - 1):
        above.append(turn(above[-1], "hidden", 1))
    parts = above + below[:0:-1]

    for ids in calls:
        dxs, rest, mark = expert_rows(ids, me, [rows[k] for k in ids], grad_rows, parts, (mark,))
        kept.append(rest)
        for k, dx in zip(ids, dxs):
            dx_back[k] = swap(dx, "expert", k) if k else dx
    kept = [list(part) for part in zip(*kept)]

    (moving, *others), mark = weight_grads(
        [i % planes for i in range(1, 1 + planes // 2)], planes, BF, *kept, (mark,)
    )
    came = turn(moving, "hidden", 1)
    out_rows, mark = expert_outputs(calls, groups, capacity, me, kept[0], parts, (mark,))
    out_back = lax.all_to_all(out_rows, "expert", split_axis=0, concat_axis=0, tiled=True)

    keep, send, grad_hidden, dqkv, mark = backward(
        capacity,
        me,
        *route_args,
        cotangent,
        w_out,
        norm_gains,
        hidden,
        attended,
        qkv,
        one,
        [dx_back[k] for k in range(groups)],
        (mark,),
    )
    sent = swap(send, "expert", 1)
    part, mark = add_part(came, others.pop(0), (mark,))
    came = turn(part, "hidden", 1)
    input_grad, small_one, mark = last_back(dqkv, w_qkv, tokens, grad_hidden, norm_gains, (mark,))
    mine, mark = add_pairs(keep, sent, (mark,))
    sent = [swap(mine[j], "expert", 2 * j) for j in range(1, groups // 2)]
    fresh, mark = weight_grads(
        [i % planes for i in range(1 + planes // 2, planes + 1)], planes, F32, *kept, (mark,)
    )
    others += fresh
    total, mark = add_all([mine[0], *sent], (mark,))
    for step, distance in enumerate(powers(planes)):
        sent = swap(total, "hidden", distance)
        if step == 0:
            layer_out, small_two, mark = finish(
                *route_args, cotangent, hidden, out_back, (mark,)
            )
        total, mark = add_all([total, sent], (mark,))
    even = [total] + [swap(total, "expert", 2 * j) for j in range(1, groups // 2)]
    own = jnp.concatenate([small_one.reshape(-1, 128), small_two], axis=0)
    own, mark = sum_small(own, "hidden", (mark,))
    for other in others[:-1]:
        part, mark = add_part(came, other, (mark,))
        came = turn(part, "hidden", 1)
    odd = [swap(piece, "expert", 1) for piece in even]
    own, mark = sum_small(own, "expert", (mark, *even[1:]))
    (grad_qkv, grad_w_out, small), mark = assemble(
        me, [piece for pair in zip(even, odd) for piece in pair], (mark,)
    )
    (grad_w_in, grad_w_down), _ = last_part(came, others[-1], (mark,))

    first = own[:-2].reshape(2, width)
    return (
        layer_out,
        input_grad,
        grad_qkv,
        small[3:5],
        grad_w_out,
        small[2],
        jnp.stack([first[0], small[0]]),
        jnp.stack([first[1], small[1]]),
        own[-2:, : gate_table.shape[0]].T,
        grad_w_in,
        grad_w_down,
    )


def solution(mesh):
    split = P(("expert", "hidden"), None)
    return jax.shard_map(
        shards,
        mesh=mesh,
        in_specs=(
            split,
            split,
            P(),
            P(),
            P(),
            P(),
            P(),
            P(),
            P(),
            P("expert", None, "hidden"),
            P("expert", "hidden", None),
            split,
            split,
            P(),
        ),
        out_specs=(
            split,
            split,
            P(),
            P(),
            P(),
            P(),
            P(),
            P(),
            P(),
            P("expert", None, "hidden"),
            P("expert", "hidden", None),
        ),
        check_vma=False,
    )
```

time: 1400 us -> 322 us (0.23)
  waiting for transfers between devices: 798 us -> 83.4 us
  matrix products: 219 us -> 0 us
  Pallas kernels: 0 us -> 168 us
  blocking collectives: 125 us -> 0 us
  other arithmetic: 104 us -> 0.6 us
  local copies, waits for them, and re-layouts: 120 us -> 19.2 us
  starting transfers between devices: 9.15 us -> 44.7 us
    reduce_scatter x2 -> x0, waiting for transfers between devices: 380 us -> none  [the longest x1 211 us: shards(): lax.psum_scatter(jnp.einsum('ref,edf->red', row_piece, w_in, preferred_el...]
    all_gather x2 -> x0, waiting for transfers between devices: 326 us -> none  [the longest x1 183 us: shards(): lax.all_gather(grad_rows, 'hidden', axis=0, tiled=True)]
    dot_general x20 -> x0, matrix products: 219 us -> none  [the longest x1 29.2 us: expert_back(): jnp.einsum('red,efd->ref', grad_slots, weight_down, preferred_element_typ...]
    pallas_call x0 -> x26, Pallas kernels: none -> 168 us  [run(): pl.pallas_call(ordered, out_shape=[*out_shape, jax.ShapeDtypeStruct((8, 1...]
    psum x1 -> x0, waiting for transfers between devices: 90.3 us -> none  [shards(): lax.psum((grad_qkv, grad_bias_qv, grad_w_out, grad_out_bias, grad_gains,...]
    all_to_all x2 -> x0, blocking collectives: 84.2 us -> none  [the longest x1 43 us: shards(): lax.all_to_all(outgoing, 'expert', split_axis=0, concat_axis=0, tiled=True)]
    ppermute x0 -> x38, waiting for transfers between devices: none -> 83.4 us  [the longest x32 50.4 us: swap(): return lax.ppermute(block, axis, [(s, s ^ distance) for s in range(count)])]
    reduce_sum x18 -> x0, other arithmetic: 53.3 us -> none  [the longest x1 14.3 us: forward_pack(): exp_total = jnp.sum(jnp.exp(scores - row_peak), axis=-1, keepdims=True)]
  transfers between devices with their start and end apart: 7 -> 40, of which waited for: 6 -> 11; matrix products, arithmetic and copies ran while one was open for 11% -> 2% of each run, Pallas kernels for 0% -> 49%
where the time goes in v3:
time: 322 us; the launch traced here: 318 us
  Pallas kernels  168 us (52%)
  waiting for transfers between devices  83.4 us (26%)
  starting transfers between devices  44.7 us (14%)
  local copies, waits for them, and re-layouts  19.2 us (6%)
    pallas_call x26, Pallas kernels, run(): pl.pallas_call(ordered, out_shape=[*out_shape, jax.ShapeDtypeStruct((8, 1...  168 us
    ppermute x32, waiting for transfers between devices, swap(): return lax.ppermute(block, axis, [(s, s ^ distance) for s in range(count)])  50.4 us
    ppermute x6, waiting for transfers between devices, turn(): lax.ppermute(block, axis, [(s, (s + distance) % count) for s in range(cou...  32.9 us
    ppermute x32, starting transfers between devices, swap(): return lax.ppermute(block, axis, [(s, s ^ distance) for s in range(count)])  29.2 us
    unnamed x79, local copies, waits for them, and re-layouts  14.5 us
    ppermute x6, starting transfers between devices, turn(): lax.ppermute(block, axis, [(s, (s + distance) % count) for s in range(cou...  6.65 us
  transfers between devices with their start and end apart: 40, of which 11 were waited for; matrix products, arithmetic and copies ran while one was open for 2% of the time, Pallas kernels for 49%

profile of v3, /device:TPU:0, one launch (start us, length us, event | category | flops | bytes accessed | tf_op | source)
XLA Modules:
  0.0 317.5 jit_solution(9096918423645367111)
XLA Ops:
  0.6 2.4 join_weights.1
  3.0 6.5 %dispatch_grads.1 = (bf16[8,384,512]{2,1,0:T(8,128)(2,1)}, f32[8,128]{1,0:T(8,128)}) custom-call(s32[1,32]{1,0:T(1,128)} %refs_0_.5, s32[1,32]{1,0:T(1,128)} %refs_1_.11, s32[2,30]{1,0:T(2,128)} %bitcast.13, f32[2,30]{1,0:T(2,128)} %bitcast.17, bf16[1024,512]{1,0:T(8,128)(2,1)} %refs_4_.5, f32[8,128]{1,0:T(8,128)} %get-tuple-element.102.refs_5_), custom_call_target="tpu_custom_call" | custom-call | flops 2760000000 | bytes 1024 | tf_op jit(solution)/shard_map/dispatch_grads/pallas_call | solution.py:88
  9.5 5.2 %all-to-all-start = ((bf16[8,384,512]{2,1,0:T(8,128)(2,1)}), bf16[8,384,512]{2,1,0:T(8,128)(2,1)S(1)}, u32[]{:S(2)}, u32[]{:S(2)}) async-start(bf16[8,384,512]{2,1,0:T(8,128)(2,1)} %get-tuple-element.107), calls=%async_computation | async-start | bytes 6291456 | tf_op jit(solution)/shard_map/all_to_all | solution.py:1055
  14.7 1.8 collective-permute-start.1
  16.5 13.1 %forward.1 = (bf16[1024,1536]{1,0:T(8,128)(2,1)}, bf16[1024,512]{1,0:T(8,128)(2,1)}, f32[1024,512]{1,0:T(8,128)}, bf16[1024,512]{1,0:T(8,128)(2,1)}, bf16[384,51...) custom-call(s32[1]{0:T(128)} %bitcast.2.refs_0_, ...), custom_call_target="tpu_custom_call" | custom-call | flops 5980000256 | bytes 1024 | tf_op jit(solution)/shard_map/forward/pallas_call | solution.py:88
  29.6 2.4 collective-permute-start.2
  32.0 2.4 collective-permute-start.4
  34.4 26.1 %collective-permute-done.2.refs_2_.refs_1_ = bf16[384,512]{1,0:T(8,128)(2,1)S(1)} collective-permute-done((bf16[384,512]{1,0:T(8,128)(2,1)}, bf16[384,512]{1,0:T(8,128)(2,1)S(1)}, u32[]{:S(2)}, u32[]{:S(2)}) %collective-permute-start.2) | collective-permute-done | bytes 393248 | tf_op jit(solution)/shard_map/ppermute | solution.py:877
  61.8 2.0 collective-permute-start.3
  65.5 1.6 collective-permute-start.7
  67.7 22.3 %collective-permute-done.3.refs_6_.refs_7_ = bf16[1024,512]{1,0:T(8,128)(2,1)S(1)} collective-permute-done((bf16[1024,512]{1,0:T(8,128)(2,1)}, bf16[1024,512]{1,0:T(8,128)(2,1)S(1)}, u32[]{:S(2)}, u32[]{:S(2)}) %collective-permute-start.3) | collective-permute-done | bytes 1048608 | tf_op jit(solution)/shard_map/ppermute | solution.py:882
  91.5 1.7 copy-done
  93.2 10.5 %expert_rows.3 = (bf16[384,512]{1,0:T(8,128)(2,1)}, bf16[384,512]{1,0:T(8,128)(2,1)}, bf16[768,2048]{1,0:T(8,128)(2,1)}, bf16[768,2048]{1,0:T(8,128)(2,1)}, bf16...) custom-call(s32[1]{0:T(128)} %bitcast.2.refs_0_, bf16[384,512]{1,0:T(8,128)(2,1)} %copy-done.17, ...), custom_call_target="tpu_custom_call" | custom-call | flops 7820000256 | bytes 1024 | tf_op jit(solution)/shard_map/expert_rows/pallas_call | solution.py:88
  103.7 14.1 %expert_rows.4 = (bf16[384,512]{1,0:T(8,128)(2,1)}, bf16[384,512]{1,0:T(8,128)(2,1)}, bf16[384,512]{1,0:T(8,128)(2,1)}, bf16[1152,2048]{1,0:T(8,128)(2,1)}, bf16...) custom-call(s32[1]{0:T(128)} %bitcast.2.refs_0_, ...), custom_call_target="tpu_custom_call" | custom-call | flops 7820000256 | bytes 1024 | tf_op jit(solution)/shard_map/expert_rows/pallas_call | solution.py:88
  119.7 1.5 collective-permute-start.16
  121.2 13.9 %expert_rows.5 = (bf16[384,512]{1,0:T(8,128)(2,1)}, bf16[384,512]{1,0:T(8,128)(2,1)}, bf16[384,512]{1,0:T(8,128)(2,1)}, bf16[1152,2048]{1,0:T(8,128)(2,1)}, bf16...) custom-call(s32[1]{0:T(128)} %bitcast.2.refs_0_, ...), custom_call_target="tpu_custom_call" | custom-call | flops 7820000256 | bytes 1024 | tf_op jit(solution)/shard_map/expert_rows/pallas_call | solution.py:88
  135.6 13.3 %weight_grads.2 = (bf16[1024,512]{1,0:T(8,128)(2,1)}, bf16[1024,512]{1,0:T(8,128)(2,1)}, f32[8,128]{1,0:T(8,128)}) custom-call(bf16[768,2048]{1,0:T(8,128)(2,1)} %get-tuple-element.112.refs_0_.refs_1_, bf16[1152,2048]{1,0:T(8,128)(2,1)} %get-tuple-element.116.refs_1_.refs_2_, bf16[1152,2048]{1,0:T(8,128)(2,1)} %get-tuple-element.121.refs_2_.refs_3_, ...), custom_call_target="tpu_custom_call" | custom-call | flops 4140000000 | bytes 1024 | tf_op jit(solution)/shard_map/weight_grads/pallas_call | solution.py:88
  148.9 1.7 collective-permute-start.13
  150.6 1.4 collective-permute-start.15
  152.0 11.4 %expert_outputs.1 = (bf16[8,384,512]{2,1,0:T(8,128)(2,1)}, f32[8,128]{1,0:T(8,128)}) custom-call(s32[1]{0:T(128)} %bitcast.2.refs_0_, bf16[768,2048]{1,0:T(8,128)(2,1)} %get-tuple-element.112.refs_0_.refs_1_, bf16[1152,2048]{1,0:T(8,128)(2,1)} %get-tuple-element.116.refs_1_.refs_2_, bf16[1152,2048]{1,0:T(8,128)(2,1)} %get-tuple-element.121.refs_2_.refs_3_, ...), custom_call_target="tpu_custom_call" | custom-call | flops 5059999744 | bytes 1024 | tf_op jit(solution)/shard_map/expert_outputs/pallas_call | solution.py:88
  163.4 3.7 %all-to-all-start.1 = ((bf16[8,384,512]{2,1,0:T(8,128)(2,1)}), bf16[8,384,512]{2,1,0:T(8,128)(2,1)S(1)}, u32[]{:S(2)}, u32[]{:S(2)}) async-start(bf16[8,384,512]{2,1,0:T(8,128)(2,1)} %get-tuple-element.133), calls=%async_computation.1 | async-start | bytes 6291456 | tf_op jit(solution)/shard_map/all_to_all | solution.py:1095
  168.5 22.8 %backward.1 = (bf16[4,64,2176]{2,1,0:T(8,128)(2,1)}, bf16[4,64,2176]{2,1,0:T(8,128)(2,1)}, f32[1024,512]{1,0:T(8,128)}, bf16[1024,1536]{1,0:T(8,128)(2,1)}, f32[8,128]{1,0:T(8,128)}) custom-call(s32[1]{0:T(128)} %bitcast.2.refs_0_, s32[1,32]{1,0:T(1,128)} %refs_0_.5, s32[1,32]{1,0:T(1,128)} %refs_1_.11, s32[2,30]{1,0:T(2,128)} %bitcast.15, ...), custom_call_target="tpu_custom_call" | custom-call | flops 10579999744 | bytes 1024 | tf_op jit(solution)/shard_map/backward/pallas_call | solution.py:88
  191.3 3.7 %collective-permute-done.18.refs_0_ = bf16[1024,512]{1,0:T(8,128)(2,1)S(1)} collective-permute-done((bf16[1024,512]{1,0:T(8,128)(2,1)}, bf16[1024,512]{1,0:T(8,128)(2,1)S(1)}, u32[]{:S(2)}, u32[]{:S(2)}) %collective-permute-start.18) | collective-permute-done | bytes 1048608 | tf_op jit(solution)/shard_map/ppermute | solution.py:882
  196.0 2.8 add_part.2
  198.8 6.5 %last_back.1 = (bf16[1024,512]{1,0:T(8,128)(2,1)}, f32[2,512]{1,0:T(2,128)}, f32[8,128]{1,0:T(8,128)}) custom-call(bf16[1024,1536]{1,0:T(8,128)(2,1)} %get-tuple-element.148.refs_0_, bf16[512,1536]{1,0:T(8,128)(2,1)} %refs_1_.10, bf16[1024,512]{1,0:T(8,128)(2,1)} %refs_2_.5, f32[1024,512]{1,0:T(8,128)} %get-tuple-element.149.refs_3_, f32[2,512]{1,0:T(2,128)} %refs_4_.4, ...), custom_call_target="tpu_custom_call" | custom-call | flops 2760000000 | bytes 1024 | tf_op jit(solution)/shard_map/last_back/pallas_call | solution.py:88
  206.2 2.6 add_pairs.1
  208.9 1.7 collective-permute-start.19
  210.5 1.5 collective-permute-start.20
  212.3 13.2 %weight_grads.3 = (f32[1024,512]{1,0:T(8,128)}, f32[1024,512]{1,0:T(8,128)}, f32[8,128]{1,0:T(8,128)}) custom-call(bf16[768,2048]{1,0:T(8,128)(2,1)} %get-tuple-element.112.refs_0_.refs_1_, bf16[1152,2048]{1,0:T(8,128)(2,1)} %get-tuple-element.116.refs_1_.refs_2_, bf16[1152,2048]{1,0:T(8,128)(2,1)} %get-tuple-element.121.refs_2_.refs_3_, ...), custom_call_target="tpu_custom_call" | custom-call | flops 4140000000 | bytes 1024 | tf_op jit(solution)/shard_map/weight_grads/pallas_call | solution.py:88
  226.5 2.1 add_all.3
  228.6 1.7 copy-done.1
  230.2 12.1 %finish.1 = (bf16[1024,512]{1,0:T(8,128)(2,1)}, f32[2,128]{1,0:T(2,128)}, f32[8,128]{1,0:T(8,128)}) custom-call(s32[1,32]{1,0:T(1,128)} %refs_0_.5, s32[1,32]{1,0:T(1,128)} %refs_1_.11, s32[2,30]{1,0:T(2,128)} %bitcast.16, f32[2,30]{1,0:T(2,128)} %bitcast.20, bf16[1024,512]{1,0:T(8,128)(2,1)} %refs_4_.5, f32[1024,512]{1,0:T(8,128)} %get-tuple-element.104.refs_8_.refs_5_, ...), custom_call_target="tpu_custom_call" | custom-call | flops 5520000000 | bytes 1024 | tf_op jit(solution)/shard_map/finish/pallas_call | solution.py:88
  243.1 1.8 add_all.4
  244.9 4.4 %collective-permute-start.23 = (bf16[64,2176]{1,0:T(8,128)(2,1)}, bf16[64,2176]{1,0:T(8,128)(2,1)S(1)}, u32[]{:S(2)}, u32[]{:S(2)}) collective-permute-start(bf16[64,2176]{1,0:T(8,128)(2,1)} %get-tuple-element.166.refs_0_), channel_id=1, source_target_pairs={{0,2},{1,3},{2,0},{3,1},{4,6},{5,7},{6,4},{7,5},{8,10},{9,11},{10,... | collective-permute-start | bytes 835592 | tf_op jit(solution)/shard_map/ppermute | solution.py:877
  249.3 11.1 %collective-permute-done.23.refs_1_ = bf16[64,2176]{1,0:T(8,128)(2,1)S(1)} collective-permute-done((bf16[64,2176]{1,0:T(8,128)(2,1)}, bf16[64,2176]{1,0:T(8,128)(2,1)S(1)}, u32[]{:S(2)}, u32[]{:S(2)}) %collective-permute-start.23) | collective-permute-done | bytes 278560 | tf_op jit(solution)/shard_map/ppermute | solution.py:877
  261.1 1.8 add_all.5
  262.9 2.4 collective-permute-start.29
  266.5 3.6 %collective-permute-done.31.refs_1_ = f32[10,128]{1,0:T(8,128)S(1)} collective-permute-done((f32[10,128]{1,0:T(8,128)S(1)}, f32[10,128]{1,0:T(8,128)S(1)}, u32[]{:S(2)}, u32[]{:S(2)}) %collective-permute-start.31) | collective-permute-done | bytes 5152 | tf_op jit(solution)/shard_map/ppermute | solution.py:877
  273.0 3.9 %collective-permute-done.32.refs_1_ = f32[10,128]{1,0:T(8,128)S(1)} collective-permute-done((f32[10,128]{1,0:T(8,128)}, f32[10,128]{1,0:T(8,128)S(1)}, u32[]{:S(2)}, u32[]{:S(2)}) %collective-permute-start.32) | collective-permute-done | bytes 5152 | tf_op jit(solution)/shard_map/ppermute | solution.py:877
  278.7 3.1 add_part.3
  284.1 1.5 collective-permute-start.35
  285.6 2.4 collective-permute-done.35.refs_1_
  289.9 1.5 collective-permute-start.36
  292.0 1.8 collective-permute-done.36.refs_1_
  298.7 3.7 %assemble.1 = (f32[512,1536]{1,0:T(8,128)}, f32[512,512]{1,0:T(8,128)}, f32[8,512]{1,0:T(8,128)}, f32[8,128]{1,0:T(8,128)}) custom-call(s32[1]{0:T(128)} %bitcast.2.refs_0_, bf16[64,2176]{1,0:T(8,128)(2,1)} %get-tuple-element.168.refs_1_, bf16[64,2176]{1,0:T(8,128)(2,1)} %copy-done.25, bf16[64,2176]{1,0:T(8,128)(2,1)} %copy-done.23, ...), custom_call_target="tpu_custom_call" | custom-call | flops 920000000 | bytes 1024 | tf_op jit(solution)/shard_map/assemble/pallas_call | solution.py:88
  303.7 1.4 fusion
  305.7 7.0 %collective-permute-done.37.refs_0_ = bf16[1024,512]{1,0:T(8,128)(2,1)S(1)} collective-permute-done((bf16[1024,512]{1,0:T(8,128)(2,1)S(1)}, bf16[1024,512]{1,0:T(8,128)(2,1)S(1)}, u32[]{:S(2)}, u32[]{:S(2)}) %collective-permute-start.37) | collective-permute-done | bytes 1048608 | tf_op jit(solution)/shard_map/ppermute | solution.py:882
  313.7 3.6 %last_part.1 = (f32[1,512,512]{2,1,0:T(8,128)}, f32[1,512,512]{2,1,0:T(8,128)}, f32[8,128]{1,0:T(8,128)}) custom-call(bf16[1024,512]{1,0:T(8,128)(2,1)} %copy-done.10, f32[1024,512]{1,0:T(8,128)} %get-tuple-element.189.refs_1_, f32[8,128]{1,0:T(8,128)} %get-tuple-element.190.refs_2_), custom_call_target="tpu_custom_call" | custom-call | flops 920000000 | bytes 1024 | tf_op jit(solution)/shard_map/last_part/pallas_call | solution.py:88
  (144 shorter events, 32.1 us)
Async XLA Ops:
  9.5 82.0 %all-to-all-start = ((bf16[8,384,512]{2,1,0:T(8,128)(2,1)}), bf16[8,384,512]{2,1,0:T(8,128)(2,1)S(1)}, u32[]{:S(2)}, u32[]{:S(2)}) async-start(bf16[8,384,512]{2,1,0:T(8,128)(2,1)} %get-tuple-element.107), calls=%async_computation | async-start | bytes 6291456 | tf_op jit(solution)/shard_map/all_to_all | solution.py:1055
  14.7 45.8 %collective-permute-start.1 = (bf16[1024,512]{1,0:T(8,128)(2,1)}, bf16[1024,512]{1,0:T(8,128)(2,1)}, u32[]{:S(2)}, u32[]{:S(2)}) collective-permute-start(bf16[1024,512]{1,0:T(8,128)(2,1)} %get-tuple-element.108.refs_4_.refs_5_), channel_id=1, source_target_pairs={{0,1},{1,2},{2,3},{3,0},{4,5},{5,6},{6,7},{7,4},{8,9},{9,10},{10,1... | collective-permute-start | bytes 3145736 | tf_op jit(solution)/shard_map/ppermute | solution.py:882
  16.5 15.5 %copy-start.6 = (bf16[1024,512]{1,0:T(8,128)(2,1)S(1)}, bf16[1024,512]{1,0:T(8,128)(2,1)}, u32[]{:S(2)}) copy-start(bf16[1024,512]{1,0:T(8,128)(2,1)} %get-tuple-element.108.refs_4_.refs_5_) | copy-start | bytes 3145732
  29.6 34.2 %copy-start.16 = (bf16[384,512]{1,0:T(8,128)(2,1)S(1)}, bf16[384,512]{1,0:T(8,128)(2,1)}, u32[]{:S(2)}) copy-start(bf16[384,512]{1,0:T(8,128)(2,1)} %get-tuple-element.105) | copy-start | bytes 1179652
  29.6 34.2 %copy-start.15 = (bf16[384,512]{1,0:T(8,128)(2,1)S(1)}, bf16[384,512]{1,0:T(8,128)(2,1)}, u32[]{:S(2)}) copy-start(bf16[384,512]{1,0:T(8,128)(2,1)} %get-tuple-element.113) | copy-start | bytes 1179652
  29.6 30.9 %collective-permute-start.2 = (bf16[384,512]{1,0:T(8,128)(2,1)}, bf16[384,512]{1,0:T(8,128)(2,1)S(1)}, u32[]{:S(2)}, u32[]{:S(2)}) collective-permute-start(bf16[384,512]{1,0:T(8,128)(2,1)} %get-tuple-element.110), channel_id=1, source_target_pairs={{0,28},{4,24},{8,20},{12,16},{16,12},{20,8},{24,4},{28,0},{1,29},{... | collective-permute-start | bytes 1179656 | tf_op jit(solution)/shard_map/ppermute | solution.py:877
  32.0 35.1 %collective-permute-start.4 = (bf16[1024,512]{1,0:T(8,128)(2,1)S(1)}, bf16[1024,512]{1,0:T(8,128)(2,1)S(1)}, u32[]{:S(2)}, u32[]{:S(2)}) collective-permute-start(bf16[1024,512]{1,0:T(8,128)(2,1)S(1)} %copy-done.6), channel_id=1, source_target_pairs={{0,3},{1,0},{2,1},{3,2},{4,7},{5,4},{6,5},{7,6},{8,11},{9,8},{10,9... | collective-permute-start | bytes 3145736 | tf_op jit(solution)/shard_map/ppermute | solution.py:882
  61.8 28.1 %collective-permute-start.3 = (bf16[1024,512]{1,0:T(8,128)(2,1)}, bf16[1024,512]{1,0:T(8,128)(2,1)S(1)}, u32[]{:S(2)}, u32[]{:S(2)}) collective-permute-start(bf16[1024,512]{1,0:T(8,128)(2,1)} %get-tuple-element.111.refs_5_.refs_6_), channel_id=1, source_target_pairs={{0,1},{1,2},{2,3},{3,0},{4,5},{5,6},{6,7},{7,4},{8,9},{9,10},{10,1... | collective-permute-start | bytes 3145736 | tf_op jit(solution)/shard_map/ppermute | solution.py:882
  63.8 1.7 collective-permute-start
  63.8 39.8 %collective-permute-start.5 = (bf16[384,512]{1,0:T(8,128)(2,1)S(1)}, bf16[384,512]{1,0:T(8,128)(2,1)}, u32[]{:S(2)}, u32[]{:S(2)}) collective-permute-start(bf16[384,512]{1,0:T(8,128)(2,1)S(1)} %copy-done.15), channel_id=1, source_target_pairs={{0,12},{4,8},{8,4},{12,0},{16,28},{20,24},{24,20},{28,16},{1,13},{... | collective-permute-start | bytes 1179656 | tf_op jit(solution)/shard_map/ppermute | solution.py:877
  64.5 39.2 %collective-permute-start.6 = (bf16[384,512]{1,0:T(8,128)(2,1)}, bf16[384,512]{1,0:T(8,128)(2,1)}, u32[]{:S(2)}, u32[]{:S(2)}) collective-permute-start(bf16[384,512]{1,0:T(8,128)(2,1)} %get-tuple-element.114), channel_id=1, source_target_pairs={{0,20},{4,16},{8,28},{12,24},{16,4},{20,0},{24,12},{28,8},{1,21},{... | collective-permute-start | bytes 1179656 | tf_op jit(solution)/shard_map/ppermute | solution.py:877
  65.5 24.4 %copy-start.17 = (bf16[384,512]{1,0:T(8,128)(2,1)}, bf16[384,512]{1,0:T(8,128)(2,1)S(1)}, u32[]{:S(2)}) copy-start(bf16[384,512]{1,0:T(8,128)(2,1)S(1)} %collective-permute-done.refs_1_) | copy-start | bytes 1179652
  65.5 52.8 %collective-permute-start.7 = (bf16[384,512]{1,0:T(8,128)(2,1)}, bf16[384,512]{1,0:T(8,128)(2,1)}, u32[]{:S(2)}, u32[]{:S(2)}) collective-permute-start(bf16[384,512]{1,0:T(8,128)(2,1)} %get-tuple-element.117), channel_id=1, source_target_pairs={{0,24},{4,28},{8,16},{12,20},{16,8},{20,12},{24,0},{28,4},{1,25},{... | collective-permute-start | bytes 1179656 | tf_op jit(solution)/shard_map/ppermute | solution.py:877
  67.1 22.9 %copy-start.7 = (bf16[1024,512]{1,0:T(8,128)(2,1)}, bf16[1024,512]{1,0:T(8,128)(2,1)S(1)}, u32[]{:S(2)}) copy-start(bf16[1024,512]{1,0:T(8,128)(2,1)S(1)} %collective-permute-done.4.refs_7_.refs_8_) | copy-start | bytes 3145732
  67.1 52.5 %collective-permute-start.8 = (bf16[384,512]{1,0:T(8,128)(2,1)}, bf16[384,512]{1,0:T(8,128)(2,1)}, u32[]{:S(2)}, u32[]{:S(2)}) collective-permute-start(bf16[384,512]{1,0:T(8,128)(2,1)} %get-tuple-element.118), channel_id=1, source_target_pairs={{0,8},{4,12},{8,0},{12,4},{16,24},{20,28},{24,16},{28,20},{1,9},{5... | collective-permute-start | bytes 1179656 | tf_op jit(solution)/shard_map/ppermute | solution.py:877
  90.9 30.2 %collective-permute-start.9 = (bf16[384,512]{1,0:T(8,128)(2,1)}, bf16[384,512]{1,0:T(8,128)(2,1)}, u32[]{:S(2)}, u32[]{:S(2)}) collective-permute-start(bf16[384,512]{1,0:T(8,128)(2,1)} %get-tuple-element.119), channel_id=1, source_target_pairs={{0,16},{4,20},{8,24},{12,28},{16,0},{20,4},{24,8},{28,12},{1,17},{... | collective-permute-start | bytes 1179656 | tf_op jit(solution)/shard_map/ppermute | solution.py:877
  103.6 45.2 %collective-permute-start.10 = (bf16[384,512]{1,0:T(8,128)(2,1)}, bf16[384,512]{1,0:T(8,128)(2,1)S(1)}, u32[]{:S(2)}, u32[]{:S(2)}) collective-permute-start(bf16[384,512]{1,0:T(8,128)(2,1)} %get-tuple-element.138), channel_id=1, source_target_pairs={{0,4},{4,0},{8,12},{12,8},{16,20},{20,16},{24,28},{28,24},{1,5},{5... | collective-permute-start | bytes 1179656 | tf_op jit(solution)/shard_map/ppermute | solution.py:877
  117.8 32.8 %collective-permute-start.12 = (bf16[384,512]{1,0:T(8,128)(2,1)}, bf16[384,512]{1,0:T(8,128)(2,1)S(1)}, u32[]{:S(2)}, u32[]{:S(2)}) collective-permute-start(bf16[384,512]{1,0:T(8,128)(2,1)} %get-tuple-element.140), channel_id=1, source_target_pairs={{0,12},{4,8},{8,4},{12,0},{16,28},{20,24},{24,20},{28,16},{1,13},{... | collective-permute-start | bytes 1179656 | tf_op jit(solution)/shard_map/ppermute | solution.py:877
  118.3 48.8 %collective-permute-start.14 = (bf16[384,512]{1,0:T(8,128)(2,1)}, bf16[384,512]{1,0:T(8,128)(2,1)}, u32[]{:S(2)}, u32[]{:S(2)}) collective-permute-start(bf16[384,512]{1,0:T(8,128)(2,1)} %get-tuple-element.142), channel_id=1, source_target_pairs={{0,20},{4,16},{8,28},{12,24},{16,4},{20,0},{24,12},{28,8},{1,21},{... | collective-permute-start | bytes 1179656 | tf_op jit(solution)/shard_map/ppermute | solution.py:877
  119.7 48.0 %collective-permute-start.16 = (bf16[384,512]{1,0:T(8,128)(2,1)}, bf16[384,512]{1,0:T(8,128)(2,1)}, u32[]{:S(2)}, u32[]{:S(2)}) collective-permute-start(bf16[384,512]{1,0:T(8,128)(2,1)} %get-tuple-element.144), channel_id=1, source_target_pairs={{0,28},{4,24},{8,20},{12,16},{16,12},{20,8},{24,4},{28,0},{1,29},{... | collective-permute-start | bytes 1179656 | tf_op jit(solution)/shard_map/ppermute | solution.py:877
  135.1 32.6 %collective-permute-start.11 = (bf16[384,512]{1,0:T(8,128)(2,1)}, bf16[384,512]{1,0:T(8,128)(2,1)}, u32[]{:S(2)}, u32[]{:S(2)}) collective-permute-start(bf16[384,512]{1,0:T(8,128)(2,1)} %get-tuple-element.139), channel_id=1, source_target_pairs={{0,8},{4,12},{8,0},{12,4},{16,24},{20,28},{24,16},{28,20},{1,9},{5... | collective-permute-start | bytes 1179656 | tf_op jit(solution)/shard_map/ppermute | solution.py:877
  148.9 14.5 %copy-start.12 = (bf16[384,512]{1,0:T(8,128)(2,1)}, bf16[384,512]{1,0:T(8,128)(2,1)S(1)}, u32[]{:S(2)}) copy-start(bf16[384,512]{1,0:T(8,128)(2,1)S(1)} %collective-permute-done.10.refs_13_) | copy-start | bytes 1179652
  148.9 19.6 %collective-permute-start.13 = (bf16[384,512]{1,0:T(8,128)(2,1)}, bf16[384,512]{1,0:T(8,128)(2,1)}, u32[]{:S(2)}, u32[]{:S(2)}) collective-permute-start(bf16[384,512]{1,0:T(8,128)(2,1)} %get-tuple-element.141), channel_id=1, source_target_pairs={{0,16},{4,20},{8,24},{12,28},{16,0},{20,4},{24,8},{28,12},{1,17},{... | collective-permute-start | bytes 1179656 | tf_op jit(solution)/shard_map/ppermute | solution.py:877
  150.6 12.8 %copy-start.13 = (bf16[384,512]{1,0:T(8,128)(2,1)}, bf16[384,512]{1,0:T(8,128)(2,1)S(1)}, u32[]{:S(2)}) copy-start(bf16[384,512]{1,0:T(8,128)(2,1)S(1)} %collective-permute-done.12.refs_15_) | copy-start | bytes 1179652
  150.6 17.9 %collective-permute-start.15 = (bf16[384,512]{1,0:T(8,128)(2,1)}, bf16[384,512]{1,0:T(8,128)(2,1)}, u32[]{:S(2)}, u32[]{:S(2)}) collective-permute-start(bf16[384,512]{1,0:T(8,128)(2,1)} %get-tuple-element.143), channel_id=1, source_target_pairs={{0,24},{4,28},{8,16},{12,20},{16,8},{20,12},{24,0},{28,4},{1,25},{... | collective-permute-start | bytes 1179656 | tf_op jit(solution)/shard_map/ppermute | solution.py:877
  163.4 65.1 %all-to-all-start.1 = ((bf16[8,384,512]{2,1,0:T(8,128)(2,1)}), bf16[8,384,512]{2,1,0:T(8,128)(2,1)S(1)}, u32[]{:S(2)}, u32[]{:S(2)}) async-start(bf16[8,384,512]{2,1,0:T(8,128)(2,1)} %get-tuple-element.133), calls=%async_computation.1 | async-start | bytes 6291456 | tf_op jit(solution)/shard_map/all_to_all | solution.py:1095
  167.1 27.9 %collective-permute-start.18 = (bf16[1024,512]{1,0:T(8,128)(2,1)}, bf16[1024,512]{1,0:T(8,128)(2,1)S(1)}, u32[]{:S(2)}, u32[]{:S(2)}) collective-permute-start(bf16[1024,512]{1,0:T(8,128)(2,1)} %get-tuple-element.150), channel_id=1, source_target_pairs={{0,1},{1,2},{2,3},{3,0},{4,5},{5,6},{6,7},{7,4},{8,9},{9,10},{10,1... | collective-permute-start | bytes 3145736 | tf_op jit(solution)/shard_map/ppermute | solution.py:882
  191.3 14.0 %collective-permute-start.17 = (bf16[4,64,2176]{2,1,0:T(8,128)(2,1)}, bf16[4,64,2176]{2,1,0:T(8,128)(2,1)S(1)}, u32[]{:S(2)}, u32[]{:S(2)}) collective-permute-start(bf16[4,64,2176]{2,1,0:T(8,128)(2,1)} %get-tuple-element.147), channel_id=1, source_target_pairs={{0,4},{4,0},{8,12},{12,8},{16,20},{20,16},{24,28},{28,24},{1,5},{5... | collective-permute-start | bytes 3342344 | tf_op jit(solution)/shard_map/ppermute | solution.py:877
  198.8 80.0 %collective-permute-start.34 = (bf16[1024,512]{1,0:T(8,128)(2,1)}, bf16[1024,512]{1,0:T(8,128)(2,1)}, u32[]{:S(2)}, u32[]{:S(2)}) collective-permute-start(bf16[1024,512]{1,0:T(8,128)(2,1)} %get-tuple-element.175), channel_id=1, source_target_pairs={{0,1},{1,2},{2,3},{3,0},{4,5},{5,6},{6,7},{7,4},{8,9},{9,10},{10,1... | collective-permute-start | bytes 3145736 | tf_op jit(solution)/shard_map/ppermute | solution.py:882
  208.9 16.7 %collective-permute-start.19 = (bf16[64,2176]{1,0:T(8,128)(2,1)}, bf16[64,2176]{1,0:T(8,128)(2,1)S(1)}, u32[]{:S(2)}, u32[]{:S(2)}) collective-permute-start(bf16[64,2176]{1,0:T(8,128)(2,1)} %get-tuple-element.156), channel_id=1, source_target_pairs={{0,8},{4,12},{8,0},{12,4},{16,24},{20,28},{24,16},{28,20},{1,9},{5... | collective-permute-start | bytes 835592 | tf_op jit(solution)/shard_map/ppermute | solution.py:877
  210.5 15.1 %collective-permute-start.20 = (bf16[64,2176]{1,0:T(8,128)(2,1)}, bf16[64,2176]{1,0:T(8,128)(2,1)S(1)}, u32[]{:S(2)}, u32[]{:S(2)}) collective-permute-start(bf16[64,2176]{1,0:T(8,128)(2,1)} %get-tuple-element.157), channel_id=1, source_target_pairs={{0,16},{4,20},{8,24},{12,28},{16,0},{20,4},{24,8},{28,12},{1,17},{... | collective-permute-start | bytes 835592 | tf_op jit(solution)/shard_map/ppermute | solution.py:877
  212.0 13.6 %collective-permute-start.21 = (bf16[64,2176]{1,0:T(8,128)(2,1)}, bf16[64,2176]{1,0:T(8,128)(2,1)S(1)}, u32[]{:S(2)}, u32[]{:S(2)}) collective-permute-start(bf16[64,2176]{1,0:T(8,128)(2,1)} %get-tuple-element.158), channel_id=1, source_target_pairs={{0,24},{4,28},{8,16},{12,20},{16,8},{20,12},{24,0},{28,4},{1,25},{... | collective-permute-start | bytes 835592 | tf_op jit(solution)/shard_map/ppermute | solution.py:877
  228.6 13.8 %collective-permute-start.22 = (bf16[64,2176]{1,0:T(8,128)(2,1)}, bf16[64,2176]{1,0:T(8,128)(2,1)S(1)}, u32[]{:S(2)}, u32[]{:S(2)}) collective-permute-start(bf16[64,2176]{1,0:T(8,128)(2,1)} %get-tuple-element.164.refs_0_), channel_id=1, source_target_pairs={{0,1},{1,0},{2,3},{3,2},{4,5},{5,4},{6,7},{7,6},{8,9},{9,8},{10,11... | collective-permute-start | bytes 835592 | tf_op jit(solution)/shard_map/ppermute | solution.py:877
  243.1 23.3 %copy-start.4 = (f32[2,128]{1,0:T(2,128)S(1)}, f32[2,128]{1,0:T(2,128)}, u32[]{:S(2)}) copy-start(f32[2,128]{1,0:T(2,128)} %get-tuple-element.170) | copy-start | bytes 3076
  244.9 15.5 %collective-permute-start.23 = (bf16[64,2176]{1,0:T(8,128)(2,1)}, bf16[64,2176]{1,0:T(8,128)(2,1)S(1)}, u32[]{:S(2)}, u32[]{:S(2)}) collective-permute-start(bf16[64,2176]{1,0:T(8,128)(2,1)} %get-tuple-element.166.refs_0_), channel_id=1, source_target_pairs={{0,2},{1,3},{2,0},{3,1},{4,6},{5,7},{6,4},{7,5},{8,10},{9,11},{10,... | collective-permute-start | bytes 835592 | tf_op jit(solution)/shard_map/ppermute | solution.py:877
  262.9 18.9 %collective-permute-start.29 = (bf16[64,2176]{1,0:T(8,128)(2,1)}, bf16[64,2176]{1,0:T(8,128)(2,1)S(1)}, u32[]{:S(2)}, u32[]{:S(2)}) collective-permute-start(bf16[64,2176]{1,0:T(8,128)(2,1)} %get-tuple-element.168.refs_1_), channel_id=1, source_target_pairs={{0,24},{4,28},{8,16},{12,20},{16,8},{20,12},{24,0},{28,4},{1,25},{... | collective-permute-start | bytes 835592 | tf_op jit(solution)/shard_map/ppermute | solution.py:877
  265.3 16.5 %collective-permute-start.27 = (bf16[64,2176]{1,0:T(8,128)(2,1)}, bf16[64,2176]{1,0:T(8,128)(2,1)S(1)}, u32[]{:S(2)}, u32[]{:S(2)}) collective-permute-start(bf16[64,2176]{1,0:T(8,128)(2,1)} %get-tuple-element.168.refs_1_), channel_id=1, source_target_pairs={{0,16},{4,20},{8,24},{12,28},{16,0},{20,4},{24,8},{28,12},{1,17},{... | collective-permute-start | bytes 835592 | tf_op jit(solution)/shard_map/ppermute | solution.py:877
  265.9 16.0 %collective-permute-start.25 = (bf16[64,2176]{1,0:T(8,128)(2,1)}, bf16[64,2176]{1,0:T(8,128)(2,1)S(1)}, u32[]{:S(2)}, u32[]{:S(2)}) collective-permute-start(bf16[64,2176]{1,0:T(8,128)(2,1)} %get-tuple-element.168.refs_1_), channel_id=1, source_target_pairs={{0,8},{4,12},{8,0},{12,4},{16,24},{20,28},{24,16},{28,20},{1,9},{5... | collective-permute-start | bytes 835592 | tf_op jit(solution)/shard_map/ppermute | solution.py:877
  266.4 3.7 %collective-permute-start.31 = (f32[10,128]{1,0:T(8,128)S(1)}, f32[10,128]{1,0:T(8,128)S(1)}, u32[]{:S(2)}, u32[]{:S(2)}) collective-permute-start(f32[10,128]{1,0:T(8,128)S(1)} %constant_dynamic-update-slice_fusion.refs_0_), channel_id=1, source_target_pairs={{0,1},{1,0},{2,3},{3,2},{4,5},{5,4},{6,7},{7,6},{8,9},{9,8},{10,11... | collective-permute-start | bytes 15368 | tf_op jit(solution)/shard_map/ppermute | solution.py:877
  272.0 4.8 %collective-permute-start.32 = (f32[10,128]{1,0:T(8,128)}, f32[10,128]{1,0:T(8,128)S(1)}, u32[]{:S(2)}, u32[]{:S(2)}) collective-permute-start(f32[10,128]{1,0:T(8,128)} %get-tuple-element.172.refs_0_), channel_id=1, source_target_pairs={{0,2},{1,3},{2,0},{3,1},{4,6},{5,7},{6,4},{7,5},{8,10},{9,11},{10,... | collective-permute-start | bytes 15368 | tf_op jit(solution)/shard_map/ppermute | solution.py:877
  278.7 3.1 collective-permute-start.33
  284.1 3.9 %collective-permute-start.35 = (f32[10,128]{1,0:T(8,128)}, f32[10,128]{1,0:T(8,128)S(1)}, u32[]{:S(2)}, u32[]{:S(2)}) collective-permute-start(f32[10,128]{1,0:T(8,128)} %get-tuple-element.179.refs_0_), channel_id=1, source_target_pairs={{0,8},{4,12},{8,0},{12,4},{16,24},{20,28},{24,16},{28,20},{1,9},{5... | collective-permute-start | bytes 15368 | tf_op jit(solution)/shard_map/ppermute | solution.py:877
  285.6 27.1 %collective-permute-start.37 = (bf16[1024,512]{1,0:T(8,128)(2,1)S(1)}, bf16[1024,512]{1,0:T(8,128)(2,1)S(1)}, u32[]{:S(2)}, u32[]{:S(2)}) collective-permute-start(bf16[1024,512]{1,0:T(8,128)(2,1)S(1)} %copy-done.9), channel_id=1, source_target_pairs={{0,1},{1,2},{2,3},{3,0},{4,5},{5,6},{6,7},{7,4},{8,9},{9,10},{10,1... | collective-permute-start | bytes 3145736 | tf_op jit(solution)/shard_map/ppermute | solution.py:882
  289.9 3.9 %collective-permute-start.36 = (f32[10,128]{1,0:T(8,128)}, f32[10,128]{1,0:T(8,128)S(1)}, u32[]{:S(2)}, u32[]{:S(2)}) collective-permute-start(f32[10,128]{1,0:T(8,128)} %get-tuple-element.181.refs_0_), channel_id=1, source_target_pairs={{0,16},{4,20},{8,24},{12,28},{16,0},{20,4},{24,8},{28,12},{1,17},{... | collective-permute-start | bytes 15368 | tf_op jit(solution)/shard_map/ppermute | solution.py:877
  291.4 6.3 %collective-permute-start.24 = (bf16[64,2176]{1,0:T(8,128)(2,1)S(1)}, bf16[64,2176]{1,0:T(8,128)(2,1)S(1)}, u32[]{:S(2)}, u32[]{:S(2)}) collective-permute-start(bf16[64,2176]{1,0:T(8,128)(2,1)S(1)} %copy-done.18), channel_id=1, source_target_pairs={{0,4},{4,0},{8,12},{12,8},{16,20},{20,16},{24,28},{28,24},{1,5},{5... | collective-permute-start | bytes 835592 | tf_op jit(solution)/shard_map/ppermute | solution.py:877
  291.4 6.3 %collective-permute-start.30 = (bf16[64,2176]{1,0:T(8,128)(2,1)S(1)}, bf16[64,2176]{1,0:T(8,128)(2,1)S(1)}, u32[]{:S(2)}, u32[]{:S(2)}) collective-permute-start(bf16[64,2176]{1,0:T(8,128)(2,1)S(1)} %copy-done.20), channel_id=1, source_target_pairs={{0,4},{4,0},{8,12},{12,8},{16,20},{20,16},{24,28},{28,24},{1,5},{5... | collective-permute-start | bytes 835592 | tf_op jit(solution)/shard_map/ppermute | solution.py:877
  291.9 5.8 %collective-permute-start.28 = (bf16[64,2176]{1,0:T(8,128)(2,1)S(1)}, bf16[64,2176]{1,0:T(8,128)(2,1)S(1)}, u32[]{:S(2)}, u32[]{:S(2)}) collective-permute-start(bf16[64,2176]{1,0:T(8,128)(2,1)S(1)} %copy-done.22), channel_id=1, source_target_pairs={{0,4},{4,0},{8,12},{12,8},{16,20},{20,16},{24,28},{28,24},{1,5},{5... | collective-permute-start | bytes 835592 | tf_op jit(solution)/shard_map/ppermute | solution.py:877
  293.8 4.0 %collective-permute-start.26 = (bf16[64,2176]{1,0:T(8,128)(2,1)S(1)}, bf16[64,2176]{1,0:T(8,128)(2,1)S(1)}, u32[]{:S(2)}, u32[]{:S(2)}) collective-permute-start(bf16[64,2176]{1,0:T(8,128)(2,1)S(1)} %copy-done.24), channel_id=1, source_target_pairs={{0,4},{4,0},{8,12},{12,8},{16,20},{20,16},{24,28},{28,24},{1,5},{5... | collective-permute-start | bytes 835592 | tf_op jit(solution)/shard_map/ppermute | solution.py:877
  (31 other events, 68.5 us)
